TPU v7x, 128 devices: a whole 4x4x4 slice. The times are simulated.
128 devices in a mesh: ex: 8 (over y, core), ctr: 16 (over z, x).
Axes of the slice: x: 4, y: 4, z: 4, core: 2. Of those that a mesh axis runs over, the one named last changes fastest.
Arguments:
- pool: bfloat16 [64, 32768], P(None, ('ex', 'ctr')), may hold values from -4 to 4
- indices: int32 [16384], P('ex'), may hold values from 0 to 4095
- labels: int32 [16384], P('ex'), may hold values from 0 to 143
- example_weight: float32 [16384], P('ex'), may hold values from 0.5 to 18, as said below
- centers: bfloat16 [64, 32768], P(None, 'ctr'), may hold values from -4 to 4
- alpha: bfloat16 [144, 32768], P(None, 'ctr'), may hold values from -1.5 to 1.5
- precond: float32 [32768, 256], P('ctr'), may hold values from -13.5 to 13.5, as said below
Outputs:
- margins: float32 [144, 16384], P(None, ('ex', 'ctr'))
Inputs may be any that keep to these rules, and one draw needn't show every extreme that they name: `indices`: example e belongs to example row e // 2048 and names a column of that row's part of pool, columns (e // 2048) * 4096 to (e // 2048 + 1) * 4096 - 1. `example_weight`: positive. `precond`: rows k*256 to (k+1)*256 - 1 hold block k's matrix, column j being its column j; entries below the diagonal are zero and diagonal entries are positive.
All inputs are finite; a program needn't handle non-finite values.
Results may differ from a plain program's by a relative error of at most 0.0012.
Values may be sent and summed in bfloat16 or wider, within the bound.
No kernel may reach another device: no remote copies, remote signals or barrier semaphores. Data moves between devices by JAX's collectives and lax.ppermute only.
A program may use at most 64 MiB of HBM per device.

v0:
```python
import jax
import jax.numpy as jnp
from jax import lax
from jax.sharding import PartitionSpec as P

ITERS = 2


RIDGE = 0.0001


def apply_blocks(factor, vectors):
    order_size = factor.shape[1]
    blocks = factor.reshape(-1, order_size, order_size)
    pieces = vectors.reshape(vectors.shape[0], -1, order_size)
    return jnp.einsum("kij,ckj->cki", blocks, pieces, precision=lax.Precision.HIGHEST).reshape(
        vectors.shape
    )


def apply_transposed(factor, vectors):
    order_size = factor.shape[1]
    blocks = factor.reshape(-1, order_size, order_size)
    pieces = vectors.reshape(vectors.shape[0], -1, order_size)
    return jnp.einsum("kij,cki->ckj", blocks, pieces, precision=lax.Precision.HIGHEST).reshape(
        vectors.shape
    )


def kernel_tile(points, centers):
    point_float = points.astype(jnp.float32)
    center_float = centers.astype(jnp.float32)
    point_sq = jnp.sum(point_float * point_float, axis=0)
    center_sq = jnp.sum(center_float * center_float, axis=0)
    cross_dot = lax.dot_general(
        points, centers, (((0,), (0,)), ((), ())), preferred_element_type=jnp.float32
    )
    exponent_scale = 2.0 / points.shape[0]
    distance = point_sq[:, None] + center_sq[None, :] - 2.0 * cross_dot
    return jnp.exp(-exponent_scale * distance).astype(jnp.bfloat16)


def squares(residual):
    return lax.psum(jnp.sum(residual * residual, axis=1), "ctr")


def shards(pool, indices, labels, example_weight, centers, alpha, precond):
    row_pool = lax.all_gather(pool, "ctr", axis=1, tiled=True)
    points = jnp.take(row_pool, indices, axis=1)
    tile_values = kernel_tile(points, centers)
    row_count = tile_values.shape[0]
    example_total = float(row_count * lax.axis_size("ex"))
    share_size = row_count // lax.axis_size("ctr")
    offset = lax.axis_index("ctr") * share_size
    classes = alpha.shape[0]

    def partial_rows(coefficients):
        return lax.dot_general(
            coefficients, tile_values, (((1,), (1,)), ((), ())), preferred_element_type=jnp.float32
        )

    def forward(coefficients):
        return lax.psum(partial_rows(coefficients), "ctr")

    def backward(values):
        return jnp.dot(values, tile_values, preferred_element_type=jnp.float32)

    def center_sum(values):
        return lax.psum(backward(values), "ex")

    margins = forward(alpha)
    probability = jax.nn.sigmoid(margins)
    target = (labels[None, :] == jnp.arange(classes, dtype=jnp.int32)[:, None]).astype(jnp.float32)
    hessian = example_weight[None, :] * probability * (1.0 - probability)
    gradient = (example_weight[None, :] * (probability - target)).astype(jnp.bfloat16)
    right_side = -apply_transposed(precond, center_sum(gradient)) / example_total
    residual = right_side
    direction = right_side
    norm_now = squares(residual)
    for iteration in range(ITERS):
        lifted = apply_blocks(precond, direction).astype(jnp.bfloat16)
        image_rows = forward(lifted)
        weighted = (hessian * image_rows).astype(jnp.bfloat16)
        image_vec = (
            apply_transposed(precond, center_sum(weighted)) / example_total + RIDGE * direction
        )
        curvature = lax.psum(jnp.sum(direction * image_vec, axis=1), "ctr")
        step_len = norm_now / curvature
        margins = margins + step_len[:, None] * image_rows
        if iteration + 1 < ITERS:
            residual = residual - step_len[:, None] * image_vec
            norm_next = squares(residual)
            direction = residual + (norm_next / norm_now)[:, None] * direction
            norm_now = norm_next
    margins = lax.dynamic_slice_in_dim(margins, offset, share_size, 1)
    return margins


def solution(mesh):
    return jax.shard_map(
        shards,
        mesh=mesh,
        in_specs=(
            P(None, ("ex", "ctr")),
            P("ex"),
            P("ex"),
            P("ex"),
            P(None, "ctr"),
            P(None, "ctr"),
            P("ctr", None),
        ),
        out_specs=P(None, ("ex", "ctr")),
        check_vma=False,
    )
```

profile of v0, /device:TPU:0, one launch (start us, length us, event | category | flops | bytes accessed | tf_op | source)
XLA Modules:
  0.0 674.5 jit_solution(3084411178710980754)
XLA Ops:
  6.5 0.0 copy-start
  6.5 0.0 copy-start.3
  6.5 0.0 all-reduce.8.cloned.1.call-start
  6.5 0.9 fusion.23
  7.4 0.7 compare_and_fusion
  8.1 0.9 copy.12
  9.0 26.3 %all_gather.3 = bf16[64,4096]{0,1:T(8,128)(2,1)S(1)} all-gather(bf16[64,256]{0,1:T(8,128)(2,1)S(1)} %copy.12), channel_id=1, replica_groups=mesh['ex'=8,'ctr'=16] {'ctr'}, dimensions={1}, use_global_device_ids=true | all-gather | bytes 557056 | tf_op jit(solution)/shard_map/all_gather | solution.py:48
  35.2 0.0 copy-done.3
  35.2 0.1 multiply_reduce_fusion.2
  35.3 8.0 %gather_fusion = bf16[2048,64]{1,0:T(8,128)(2,1)} fusion(bf16[64,4096]{0,1:T(8,128)(2,1)S(1)} %all_gather.3, s32[2048]{0:T(1024)S(1)} %fusion.23), kind=kCustom, calls=%fused_computation | custom fusion | bytes 532480 | tf_op jit(solution)/shard_map/jit(_take)/gather | solution.py:49
  43.3 1.7 multiply_reduce_fusion.1
  45.0 0.0 copy-start.4
  45.0 5.2 exponential_convert_fusion
  50.2 0.0 copy-start.1
  50.2 3.2 copy-done.1
  53.4 0.0 copy-done.4
  53.4 3.9 convolution_bitcast_fusion
  57.3 0.0 copy-start.5
  57.3 0.0 copy-start.6
  57.3 0.0 all-reduce.8.cloned.1.call-update
  57.4 0.0 all-reduce.10.cloned.1.call-start
  57.4 86.5 %all-reduce.8.cloned.1.call-done = f32[144,2048]{1,0:T(8,128)} async-done(((f32[144,2048]{1,0:T(8,128)}), f32[144,2048]{1,0:T(8,128)}) %all-reduce.8.cloned.1.call-update) | async-done | bytes 1179664 | tf_op jit(solution)/shard_map/psum | solution.py:63
  143.9 0.0 copy-done.5
  143.9 0.0 copy-done.6
  144.0 5.3 fusion.12
  149.3 1.1 copy.28
  150.4 0.0 all-reduce.10.cloned.1.call-update
  150.5 0.2 all-reduce.12.cloned.1.call-start
  150.7 62.0 %all-reduce.10.cloned.1.call-done = f32[144,8,256]{2,0,1:T(8,128)} async-done(((f32[144,8,256]{2,0,1:T(8,128)}), f32[144,8,256]{2,0,1:T(8,128)}) %all-reduce.10.cloned.1.call-update) | async-done | bytes 1179664 | tf_op jit(solution)/shard_map/psum | solution.py:69
  212.7 0.0 copy-done
  212.7 0.0 copy-start.2
  212.7 2.9 convolution_negate_fusion
  215.6 2.3 fusion.6
  217.9 0.1 copy.21
  217.9 0.0 copy-done.2
  218.0 3.9 fusion.28
  221.9 0.0 all-reduce.12.cloned.1.call-update
  221.9 0.0 all-reduce.14.cloned.1.call-start
  222.0 86.4 %all-reduce.12.cloned.1.call-done = f32[144,2048]{1,0:T(8,128)} async-done(((f32[144,2048]{1,0:T(8,128)}), f32[144,2048]{1,0:T(8,128)}) %all-reduce.12.cloned.1.call-update) | async-done | bytes 1179664 | tf_op jit(solution)/shard_map/psum | solution.py:63
  308.4 5.6 fusion.13
  314.0 1.1 copy.27
  315.2 0.0 all-reduce.14.cloned.1.call-update
  315.2 0.0 all-reduce.16.cloned.1.call-start
  315.3 62.2 %all-reduce.14.cloned.1.call-done = f32[144,8,256]{2,0,1:T(8,128)} async-done(((f32[144,8,256]{2,0,1:T(8,128)}), f32[144,8,256]{2,0,1:T(8,128)}) %all-reduce.14.cloned.1.call-update) | async-done | bytes 1179664 | tf_op jit(solution)/shard_map/psum | solution.py:69
  377.5 4.0 fusion.10
  381.4 40.5 %all-reduce = (f32[144]{0:T(256)S(1)}, f32[144]{0:T(256)S(1)}) all-reduce(f32[144]{0:T(256)S(1)} %get-tuple-element.6, f32[144]{0:T(256)S(1)} %get-tuple-element.5), channel_id=1, replica_groups=mesh['ex'=8,'ctr'=16] {'ctr'}, use_global_device_ids=true, to_apply=%region_5.6 | all-reduce | flops 288 | bytes 2304 | tf_op jit(solution)/shard_map/psum | solution.py:44
  422.0 1.6 multiply_reduce_fusion
  423.6 35.7 %psum.76 = f32[144]{0:T(256)S(1)} all-reduce(f32[144]{0:T(256)S(1)} %multiply_reduce_fusion), channel_id=1, replica_groups=mesh['ex'=8,'ctr'=16] {'ctr'}, use_global_device_ids=true, to_apply=%region_11.12 | all-reduce | flops 144 | bytes 1152 | tf_op jit(solution)/shard_map/psum | solution.py:44
  459.3 3.7 fusion.7
  463.0 0.1 copy.22
  463.1 7.4 %fusion.29 = f32[144,2048]{1,0:T(8,128)} fusion(bf16[144,2048]{1,0:T(8,128)(2,1)S(1)} %bitcast.82, bf16[2048,2048]{1,0:T(8,128)(2,1)} %copy-done.1), kind=kOutput, calls=%fused_computation.60 | convolution fusion | flops 1207959552 | bytes 10158080 | tf_op jit(solution)/shard_map/dot_general | solution.py:58
  470.5 0.0 all-reduce.16.cloned.1.call-update
  470.5 0.0 all-reduce.18.cloned.1.call-start
  470.5 82.4 %all-reduce.16.cloned.1.call-done = f32[144,2048]{1,0:T(8,128)} async-done(((f32[144,2048]{1,0:T(8,128)}), f32[144,2048]{1,0:T(8,128)}) %all-reduce.16.cloned.1.call-update) | async-done | bytes 1179664 | tf_op jit(solution)/shard_map/psum | solution.py:63
  552.9 5.6 fusion.14
  558.5 1.2 copy.26
  559.7 0.0 all-reduce.18.cloned.1.call-update
  559.7 62.2 %all-reduce.18.cloned.1.call-done = f32[144,8,256]{2,0,1:T(8,128)} async-done(((f32[144,8,256]{2,0,1:T(8,128)}), f32[144,8,256]{2,0,1:T(8,128)}) %all-reduce.18.cloned.1.call-update) | async-done | bytes 1179664 | tf_op jit(solution)/shard_map/psum | solution.py:69
  621.9 3.5 fusion.5
  625.4 40.5 %psum.79 = f32[144]{0:T(256)S(1)} all-reduce(f32[144]{0:T(256)S(1)} %fusion.5), channel_id=1, replica_groups=mesh['ex'=8,'ctr'=16] {'ctr'}, use_global_device_ids=true, to_apply=%region_15.16 | all-reduce | flops 144 | bytes 1152 | tf_op jit(solution)/shard_map/psum | solution.py:87
  666.0 1.7 fusion.22
  (3 shorter events, 0.0 us)
Async XLA Ops:
  6.5 206.2 %copy-start = (f32[2048,256]{1,0:T(8,128)S(1)}, f32[2048,256]{1,0:T(8,128)}, u32[]{:S(2)}) copy-start(f32[2048,256]{1,0:T(8,128)} %param.13) | copy-start | bytes 6291460
  6.5 28.7 %copy-start.3 = (bf16[64,2048]{1,0:T(8,128)(2,1)S(1)}, bf16[64,2048]{1,0:T(8,128)(2,1)}, u32[]{:S(2)}) copy-start(bf16[64,2048]{1,0:T(8,128)(2,1)} %param.11) | copy-start | bytes 786436
  6.5 137.4 %all-reduce.8.cloned.1.call-start = ((), (), s32[]{:S(2)}) async-start(), calls=%async_computation | async-start | bytes 2359296 | tf_op jit(solution)/shard_map/psum | solution.py:63
  45.0 8.5 %copy-start.4 = (bf16[144,2048]{1,0:T(8,128)(2,1)S(1)}, bf16[144,2048]{1,0:T(8,128)(2,1)}, u32[]{:S(2)}) copy-start(bf16[144,2048]{1,0:T(8,128)(2,1)} %param.12) | copy-start | bytes 1769476
  50.2 3.2 copy-start.1
  57.3 86.6 %copy-start.5 = (s32[2048]{0:T(1024)S(1)}, s32[2048]{0:T(1024)}, u32[]{:S(2)}) copy-start(s32[2048]{0:T(1024)} %param.9) | copy-start | bytes 24580
  57.3 86.6 %copy-start.6 = (f32[2048]{0:T(1024)S(1)}, f32[2048]{0:T(1024)}, u32[]{:S(2)}) copy-start(f32[2048]{0:T(1024)} %param.10) | copy-start | bytes 24580
  57.4 155.3 %all-reduce.10.cloned.1.call-start = ((), (), s32[]{:S(2)}) async-start(), calls=%async_computation.1 | async-start | bytes 2359296 | tf_op jit(solution)/shard_map/psum | solution.py:69
  150.5 158.0 %all-reduce.12.cloned.1.call-start = ((), (), s32[]{:S(2)}) async-start(), calls=%async_computation.2 | async-start | bytes 2359296 | tf_op jit(solution)/shard_map/psum | solution.py:63
  212.7 5.3 copy-start.2
  221.9 155.6 %all-reduce.14.cloned.1.call-start = ((), (), s32[]{:S(2)}) async-start(), calls=%async_computation.3 | async-start | bytes 2359296 | tf_op jit(solution)/shard_map/psum | solution.py:69
  315.2 237.7 %all-reduce.16.cloned.1.call-start = ((), (), s32[]{:S(2)}) async-start(), calls=%async_computation.4 | async-start | bytes 2359296 | tf_op jit(solution)/shard_map/psum | solution.py:63
  470.5 151.4 %all-reduce.18.cloned.1.call-start = ((), (), s32[]{:S(2)}) async-start(), calls=%async_computation.5 | async-start | bytes 2359296 | tf_op jit(solution)/shard_map/psum | solution.py:69
Sparse Core Ops, SparseCore 0:
  57.5 86.4 all-reduce.7
  150.6 62.0 all-reduce.9
  222.0 86.3 all-reduce.11
  315.3 62.0 all-reduce.13
  470.6 82.2 all-reduce.15
  559.8 62.0 all-reduce.17
where the time goes:
time: 675 us
  waiting for transfers between devices  442 us (65%)
  blocking collectives  143 us (21%)
  matrix products  53.4 us (8%)
  local copies, waits for them, and re-layouts  15.6 us (2%)
  between operations  13.6 us (2%)
    psum x3, waiting for transfers between devices, forward(): return lax.psum(partial_rows(coefficients), 'ctr')  255 us
    psum x3, waiting for transfers between devices, center_sum(): return lax.psum(backward(values), 'ex')  186 us
    psum x2, blocking collectives, squares(): return lax.psum(jnp.sum(residual * residual, axis=1), 'ctr')  76.2 us
    psum x1, blocking collectives, shards(): curvature = lax.psum(jnp.sum(direction * image_vec, axis=1), 'ctr')  40.5 us
    all_gather x1, blocking collectives, shards(): row_pool = lax.all_gather(pool, 'ctr', axis=1, tiled=True)  26.3 us
    dot_general x3, matrix products, backward(): return jnp.dot(values, tile_values, preferred_element_type=jnp.float32)  16.6 us
    dot_general x3, matrix products, partial_rows(): lax.dot_general(coefficients, tile_values, (((1,), (1,)), ((), ())), pref...  15.2 us
  transfers between devices with their start and end apart: 6, of which 6 were waited for; matrix products, arithmetic and copies ran while one was open for 0% of the time, Pallas kernels for 0%

commit v1 on v0

v1 whole, which is shorter than its diff:
```python
import functools

import jax
import jax.numpy as jnp
from jax import lax
from jax.experimental import pallas as pl
from jax.experimental.pallas import tpu as pltpu
from jax.sharding import PartitionSpec as P

RIDGE = 0.0001
F32 = jnp.float32
BF16 = jnp.bfloat16
VMEM_BYTES = 48 * 1024 * 1024


def split3(values):
    high = values.astype(BF16)
    rest = values - high.astype(F32)
    middle = rest.astype(BF16)
    low = (rest - middle.astype(F32)).astype(BF16)
    return high, middle, low


def tile_kernel(index_ref, pool_ref, centers_ref, alpha_ref, tile_ref, rows_ref, aug_ref):
    features, lanes = pool_ref.shape[1], pool_ref.shape[2]
    chunks = pool_ref.shape[0]
    pad = aug_ref.shape[0] - features

    def tail(squares, first):
        pieces = [p.astype(F32) for p in split3(-0.5 * squares)]
        row = lax.broadcasted_iota(jnp.int32, (pad, squares.shape[1]), 0)
        out = jnp.where((row >= 3 - first) & (row < 6 - first), 1.0, 0.0)
        for k in range(3):
            out = jnp.where(row == k + first, pieces[k], out)
        return out.astype(BF16)

    @pl.when(pl.program_id(0) == 0)
    def _():
        center_float = centers_ref[...].astype(F32)
        center_sq = jnp.sum(center_float * center_float, axis=0, keepdims=True)
        aug_ref[:features, :] = centers_ref[...]
        aug_ref[features:, :] = tail(center_sq, 3)

    index = index_ref[0]
    chunk = index // lanes
    within = index % lanes
    count = index.shape[1]
    one_hot = (lax.broadcasted_iota(jnp.int32, (lanes, count), 0) == within).astype(BF16)
    picked = jnp.dot(
        pool_ref[...].reshape(chunks * features, lanes), one_hot, preferred_element_type=F32
    ).reshape(chunks, features, count)
    points = jnp.where(chunk == 0, picked[0], 0.0)
    for k in range(1, chunks):
        points = jnp.where(chunk == k, picked[k], points)
    point_sq = jnp.sum(points * points, axis=0, keepdims=True)
    lhs = jnp.concatenate([points.astype(BF16), tail(point_sq, 0)], axis=0)
    half_distance = lax.dot_general(
        lhs, aug_ref[...], (((0,), (0,)), ((), ())), preferred_element_type=F32
    )
    values = jnp.exp(half_distance * (4.0 / features)).astype(BF16)
    tile_ref[...] = values
    rows = lax.dot_general(
        alpha_ref[...], values, (((1,), (1,)), ((), ())), preferred_element_type=F32
    )
    share = rows_ref.shape[2]
    for k in range(rows_ref.shape[0]):
        rows_ref[k] = rows[:, k * share : (k + 1) * share]


def make_tile(row_pool, indices, centers, alpha, share):
    block = 256
    chunks, features, lanes = row_pool.shape
    examples, count = indices.shape[0], centers.shape[1]
    classes = alpha.shape[0]
    steps = examples // block
    return pl.pallas_call(
        tile_kernel,
        grid=(steps,),
        in_specs=[
            pl.BlockSpec((1, 1, block), lambda i: (i, 0, 0)),
            pl.BlockSpec((chunks, features, lanes), lambda i: (0, 0, 0)),
            pl.BlockSpec((features, count), lambda i: (0, 0)),
            pl.BlockSpec((classes, count), lambda i: (0, 0)),
        ],
        out_specs=[
            pl.BlockSpec((block, count), lambda i: (i, 0)),
            pl.BlockSpec((block // share, classes, share), lambda i: (i, 0, 0)),
        ],
        out_shape=[
            jax.ShapeDtypeStruct((examples, count), BF16),
            jax.ShapeDtypeStruct((examples // share, classes, share), F32),
        ],
        scratch_shapes=[pltpu.VMEM((features + 16, count), BF16)],
        compiler_params=pltpu.CompilerParams(vmem_limit_bytes=VMEM_BYTES),
        cost_estimate=pl.CostEstimate(flops=4 << 30, bytes_accessed=10 << 20, transcendentals=4 << 20),
        name="tile",
    )(indices.reshape(steps, 1, block), row_pool, centers, alpha)


def forward_kernel(lifted_ref, tile_ref, rows_ref):
    half = lifted_ref.shape[2]
    share = rows_ref.shape[2]
    rows = sum(
        lax.dot_general(
            lifted_ref[k],
            tile_ref[:, k * half : (k + 1) * half],
            (((1,), (1,)), ((), ())),
            preferred_element_type=F32,
        )
        for k in range(lifted_ref.shape[0])
    )
    for k in range(rows_ref.shape[0]):
        rows_ref[k] = rows[:, k * share : (k + 1) * share]


def forward(lifted, tile, share):
    block = 256
    halves, classes, half = lifted.shape
    examples, count = tile.shape
    return pl.pallas_call(
        forward_kernel,
        grid=(examples // block,),
        in_specs=[
            pl.BlockSpec((halves, classes, half), lambda i: (0, 0, 0)),
            pl.BlockSpec((block, count), lambda i: (i, 0)),
        ],
        out_specs=pl.BlockSpec((block // share, classes, share), lambda i: (i, 0, 0)),
        out_shape=jax.ShapeDtypeStruct((examples // share, classes, share), F32),
        compiler_params=pltpu.CompilerParams(vmem_limit_bytes=VMEM_BYTES),
        cost_estimate=pl.CostEstimate(flops=1208 << 20, bytes_accessed=10 << 20, transcendentals=0),
        name="forward",
    )(lifted, tile)


def backward_kernel(values_ref, tile_ref, sums_ref, flat_ref):
    share = values_ref.shape[2]

    @pl.when(pl.program_id(0) == 0)
    def _():
        for k in range(values_ref.shape[0]):
            flat_ref[:, k * share : (k + 1) * share] = values_ref[k]

    sums_ref[0] = jnp.dot(flat_ref[...], tile_ref[...], preferred_element_type=F32)


def backward(values, tile):
    block = 512
    shares, classes, share = values.shape
    examples, count = tile.shape
    half = count // 2
    per_half = half // block
    return pl.pallas_call(
        backward_kernel,
        grid=(count // block,),
        in_specs=[
            pl.BlockSpec((shares, classes, share), lambda i: (0, 0, 0)),
            pl.BlockSpec((examples, block), lambda i: (0, i)),
        ],
        out_specs=pl.BlockSpec((1, classes, block), lambda i: (i // per_half, 0, i % per_half)),
        out_shape=jax.ShapeDtypeStruct((2, classes, half), F32),
        scratch_shapes=[pltpu.VMEM((classes, examples), BF16)],
        compiler_params=pltpu.CompilerParams(vmem_limit_bytes=VMEM_BYTES),
        cost_estimate=pl.CostEstimate(flops=1208 << 20, bytes_accessed=10 << 20, transcendentals=0),
        name="backward",
    )(values, tile)


def blocks_of(factor, vectors):
    order = factor.shape[1]
    return factor.reshape(-1, order, order), vectors.reshape(vectors.shape[0], -1, order)


def apply_blocks(factor, vectors):
    blocks, pieces = blocks_of(factor, vectors)
    return jnp.einsum("kij,ckj->cki", blocks, pieces, precision=lax.Precision.HIGHEST).reshape(
        vectors.shape
    )


def apply_transposed(factor, vectors):
    blocks, pieces = blocks_of(factor, vectors)
    return jnp.einsum("kij,cki->ckj", blocks, pieces, precision=lax.Precision.HIGHEST).reshape(
        vectors.shape
    )


def exchange(array, axis, pairs):
    return lax.ppermute(array, axis, pairs)


def shards(pool, indices, labels, example_weight, centers, alpha, precond):
    n_ex, n_ctr = lax.axis_size("ex"), lax.axis_size("ctr")
    classes = alpha.shape[0]
    examples = indices.shape[0]
    share = examples // n_ctr
    total = float(examples * n_ex)
    core = lax.axis_index("ex") % 2
    rows_y = n_ex // 2

    def pairs_y(flip):
        return [(2 * y + c, 2 * (y ^ flip) + c) for y in range(rows_y) for c in range(2)]

    core_pairs = [(i, i ^ 1) for i in range(n_ex)]

    def to_all(block):
        return lax.all_to_all(jnp.broadcast_to(block, (n_ctr,) + block.shape), "ctr", 0, 0)

    def sum_shares(parts):
        return jnp.sum(lax.all_to_all(parts, "ctr", 0, 0), axis=0)

    def with_rows(parts, vectors):
        flat = jnp.stack(vectors)
        flat = jnp.pad(flat, ((0, 0), (0, 2 * share - classes))).reshape(-1, share)
        flat = jnp.pad(flat, ((0, 8 - flat.shape[0]), (0, 0)))
        return jnp.concatenate(
            [parts, jnp.broadcast_to(flat, (parts.shape[0],) + flat.shape)], axis=1
        )

    def from_rows(summed, number):
        return [
            summed[classes + 2 * k : classes + 2 * k + 2].reshape(-1)[:classes]
            for k in range(number)
        ]

    def sum_examples(halves, vector=None):
        mine = lax.dynamic_index_in_dim(halves, core, 0, False)
        other = lax.dynamic_index_in_dim(halves, 1 - core, 0, False)
        if vector is not None:
            row = jnp.pad(vector, (0, mine.shape[1] - classes))[None, :]
            rows = jnp.pad(row, ((0, 7), (0, 0)))
            mine = jnp.concatenate([mine, rows], axis=0)
            other = jnp.concatenate([other, rows], axis=0)
        mine = mine + lax.ppermute(other, "ex", core_pairs)
        wide = mine.shape[1] // 2
        one, two = mine[:, :wide], mine[:, wide:]
        one = one + lax.ppermute(one, "ex", pairs_y(1))
        two = two + lax.ppermute(two, "ex", pairs_y(3))
        one = one + lax.ppermute(one, "ex", pairs_y(3))
        two = two + lax.ppermute(two, "ex", pairs_y(1))
        sums = jnp.concatenate([one[:classes], two[:classes]], axis=1)
        return sums if vector is None else (sums, one[classes, :classes])

    def both_halves(half):
        other = lax.ppermute(half, "ex", core_pairs)
        first = jnp.where(core == 0, half, other)
        second = jnp.where(core == 0, other, half)
        return jnp.stack([first, second])

    def over_cores(vector):
        return vector + lax.ppermute(vector, "ex", core_pairs)

    half = centers.shape[1] // 2
    factor = lax.dynamic_slice_in_dim(precond, core * half, half, 0)
    offset = lax.axis_index("ctr") * share
    label = lax.dynamic_slice_in_dim(labels, offset, share, 0)
    weight = lax.dynamic_slice_in_dim(example_weight, offset, share, 0)

    row_pool = to_all(pool)
    tile, base_parts = make_tile(row_pool, indices, centers, alpha, share)
    base = sum_shares(base_parts)
    probability = jax.nn.sigmoid(base)
    target = (label[None, :] == jnp.arange(classes, dtype=jnp.int32)[:, None]).astype(F32)
    hessian = weight[None, :] * probability * (1.0 - probability)
    gradient = (weight[None, :] * (probability - target)).astype(BF16)

    pulled = sum_examples(backward(to_all(gradient), tile))
    residual0 = -apply_transposed(factor, pulled) / total
    lifted0 = both_halves(apply_blocks(factor, residual0).astype(BF16))
    norm0_part = over_cores(jnp.sum(residual0 * residual0, axis=1))
    summed = sum_shares(with_rows(forward(lifted0, tile, share), [norm0_part]))
    image0 = summed[:classes]
    (norm0,) = from_rows(summed, 1)

    weighted = (hessian * image0).astype(BF16)
    curve_part = jnp.sum(weighted.astype(F32) * image0, axis=1)
    curve_rows = jnp.pad(
        jnp.pad(jnp.stack(split3(curve_part)), ((0, 0), (0, 2 * share - classes))).reshape(-1, share),
        ((0, 10), (0, 0)),
    )
    spread = to_all(jnp.concatenate([weighted, curve_rows.astype(BF16)], axis=0))
    curve_row = jnp.sum(
        spread[:, classes : classes + 6].astype(F32).reshape(-1, 3, 2 * share), axis=(0, 1)
    )[:classes]
    sums, curve = sum_examples(backward(spread[:, :classes], tile), curve_row)
    image = apply_transposed(factor, sums) / total + RIDGE * residual0
    rough = norm0 / (curve / total + RIDGE * norm0)
    residual1 = residual0 - rough[:, None] * image
    lifted1 = both_halves(apply_blocks(factor, residual1).astype(BF16))
    cross_part = over_cores(jnp.sum(residual0 * residual1, axis=1))
    norm1_part = over_cores(jnp.sum(residual1 * residual1, axis=1))
    summed = sum_shares(with_rows(forward(lifted1, tile, share), [cross_part, norm1_part]))
    image1 = summed[:classes]
    cross, norm1 = from_rows(summed, 2)

    excess = cross / (norm0 - cross)
    step0 = rough * (1.0 + excess)
    norm_next = (1.0 + excess) * ((1.0 + excess) * norm1 - 2.0 * excess * cross) + excess * excess * norm0
    ratio = norm_next / norm0
    rows = (1.0 + excess)[:, None] * image1 + (ratio - excess)[:, None] * image0
    curve1 = jnp.sum((hessian * rows).astype(BF16).astype(F32) * rows, axis=1)
    curve1 = jnp.sum(lax.all_to_all(jnp.broadcast_to(curve1, (n_ex, classes)), "ex", 0, 0), axis=0)
    curve1 = jnp.sum(lax.all_to_all(jnp.broadcast_to(curve1, (n_ctr, classes)), "ctr", 0, 0), axis=0)
    step1 = norm_next / (curve1 / total + RIDGE * (norm_next + ratio * ratio * norm0))
    return base + step0[:, None] * image0 + step1[:, None] * rows


def solution(mesh):
    return jax.shard_map(
        shards,
        mesh=mesh,
        in_specs=(
            P(None, ("ex", "ctr")),
            P("ex"),
            P("ex"),
            P("ex"),
            P(None, "ctr"),
            P(None, "ctr"),
            P("ctr", None),
        ),
        out_specs=P(None, ("ex", "ctr")),
        check_vma=False,
    )
```

time: 675 us -> 251 us (0.37)
  waiting for transfers between devices: 442 us -> 66.8 us
  matrix products: 53.4 us -> 4.5 us
  blocking collectives: 143 us -> 99.5 us
  Pallas kernels: 0 us -> 37.4 us
  starting transfers between devices: 0.39 us -> 18.4 us
  between operations: 13.6 us -> 0.39 us
    psum x6 -> x0, waiting for transfers between devices: 442 us -> none  [the longest x3 255 us: forward(): return lax.psum(partial_rows(coefficients), 'ctr')]
    psum x3 -> x0, blocking collectives: 117 us -> none  [the longest x2 76.2 us: squares(): return lax.psum(jnp.sum(residual * residual, axis=1), 'ctr')]
    all_to_all x0 -> x6, blocking collectives: none -> 99.5 us  [the longest x2 45.9 us: sum_shares(): return jnp.sum(lax.all_to_all(parts, 'ctr', 0, 0), axis=0)]
    ppermute x0 -> x15, waiting for transfers between devices: none -> 39.1 us  [the longest x2 15.1 us: sum_examples(): one = one + lax.ppermute(one, 'ex', pairs_y(3))]
    pallas_call x0 -> x5, Pallas kernels: none -> 37.4 us  [the longest x2 15.4 us: forward(): pl.pallas_call(forward_kernel, grid=(examples // block,), in_specs=[pl.Bl...]
    dot_general x7 -> x0, matrix products: 37 us -> none  [the longest x3 16.6 us: backward(): return jnp.dot(values, tile_values, preferred_element_type=jnp.float32)]
    all_to_all x0 -> x2, waiting for transfers between devices: none -> 27.7 us  [the longest x1 16.3 us: sum_shares(): return jnp.sum(lax.all_to_all(parts, 'ctr', 0, 0), axis=0)]
    all_gather x1 -> x0, blocking collectives: 26.3 us -> none  [shards(): row_pool = lax.all_gather(pool, 'ctr', axis=1, tiled=True)]
  transfers between devices with their start and end apart: 6 -> 17, of which waited for: 6 -> 15; matrix products, arithmetic and copies ran while one was open for 0% -> 1% of each run, Pallas kernels for 0% -> 0%
where the time goes in v1:
time: 251 us; the launch traced here: 249 us
  blocking collectives  99.5 us (40%)
  waiting for transfers between devices  66.8 us (27%)
  Pallas kernels  37.4 us (15%)
  starting transfers between devices  18.4 us (7%)
  other arithmetic  11.4 us (5%)
  local copies, waits for them, and re-layouts  10.9 us (4%)
  matrix products  4.5 us (2%)
    all_to_all x2, blocking collectives, sum_shares(): return jnp.sum(lax.all_to_all(parts, 'ctr', 0, 0), axis=0)  45.9 us
    all_to_all x2, blocking collectives, to_all(): lax.all_to_all(jnp.broadcast_to(block, (n_ctr,) + block.shape), 'ctr', 0, 0)  34.9 us
    all_to_all x1, waiting for transfers between devices, sum_shares(): return jnp.sum(lax.all_to_all(parts, 'ctr', 0, 0), axis=0)  16.3 us
    pallas_call x2, Pallas kernels, forward(): pl.pallas_call(forward_kernel, grid=(examples // block,), in_specs=[pl.Bl...  15.4 us
    ppermute x2, waiting for transfers between devices, sum_examples(): one = one + lax.ppermute(one, 'ex', pairs_y(3))  15.1 us
    pallas_call x1, Pallas kernels, make_tile(): pl.pallas_call(tile_kernel, grid=(steps,), in_specs=[pl.BlockSpec((1, 1,...  11.5 us
    all_to_all x1, waiting for transfers between devices, to_all(): lax.all_to_all(jnp.broadcast_to(block, (n_ctr,) + block.shape), 'ctr', 0, 0)  11.4 us
    ppermute x2, waiting for transfers between devices, sum_examples(): two = two + lax.ppermute(two, 'ex', pairs_y(3))  10.9 us
  transfers between devices with their start and end apart: 17, of which 15 were waited for; matrix products, arithmetic and copies ran while one was open for 1% of the time, Pallas kernels for 0%

profile of v1, /device:TPU:0, one launch (start us, length us, event | category | flops | bytes accessed | tf_op | source)
XLA Modules:
  0.0 249.3 jit_solution(17460138385190676233)
XLA Ops:
  0.0 1.0 broadcast_in_dim.16
  1.0 19.3 %all_to_all.42.pool_ref = bf16[16,64,256]{2,1,0:T(8,128)(2,1)S(1)} all-to-all(bf16[16,64,256]{2,1,0:T(8,128)(2,1)S(1)} %broadcast_in_dim.16), channel_id=1, replica_groups=mesh['ex'=8,'ctr'=16] {'ctr'}, dimensions={0} | all-to-all | bytes 1048576 | tf_op jit(solution)/shard_map/all_to_all | solution.py:206
  20.3 11.5 %tile.1 = (bf16[2048,2048]{1,0:T(8,128)(2,1)}, f32[16,144,128]{2,1,0:T(8,128)}) custom-call(s32[8,1,256]{2,1,0:T(1,128)S(1)} %bitcast.71, bf16[16,64,256]{2,1,0:T(8,128)(2,1)S(1)} %all_to_all.42.pool_ref, bf16[64,2048]{1,0:T(8,128)(2,1)S(1)} %copy-done.4, bf16[144,2048]{1,0:T(8,128)(2,1)S(1)} %copy-done.3), custom_call_target="tpu_custom_call" | custom-call | flops 4294967296 | bytes 10485760 | tf_op jit(solution)/shard_map/tile/pallas_call | solution.py:76
  31.8 3.7 %all-to-all-start.1 = ((f32[16,144,128]{2,1,0:T(8,128)}), f32[16,144,128]{2,1,0:T(8,128)S(1)}, u32[]{:S(2)}, u32[]{:S(2)}) async-start(f32[16,144,128]{2,1,0:T(8,128)} %get-tuple-element.7), calls=%async_computation.1 | async-start | bytes 2359296 | tf_op jit(solution)/shard_map/all_to_all | solution.py:209
  35.5 0.8 dynamic_slice.22
  36.3 0.8 dynamic_slice.23
  37.1 16.3 %all-to-all-done.1 = f32[16,144,128]{2,1,0:T(8,128)S(1)} async-done(((f32[16,144,128]{2,1,0:T(8,128)}), f32[16,144,128]{2,1,0:T(8,128)S(1)}, u32[]{:S(2)}, u32[]{:S(2)}) %all-to-all-start.1) | async-done | bytes 1179680 | tf_op jit(solution)/shard_map/all_to_all | solution.py:209
  53.5 0.9 broadcast_in_dim.34
  54.4 3.6 %all-to-all-start.2 = ((bf16[16,144,128]{2,1,0:T(8,128)(2,1)}), bf16[16,144,128]{2,1,0:T(8,128)(2,1)S(1)}, u32[]{:S(2)}, u32[]{:S(2)}) async-start(bf16[16,144,128]{2,1,0:T(8,128)(2,1)} %broadcast_in_dim.34), calls=%async_computation.2 | async-start | bytes 1179648 | tf_op jit(solution)/shard_map/all_to_all | solution.py:206
  58.0 11.4 %all-to-all-done.2.values_ref = bf16[16,144,128]{2,1,0:T(8,128)(2,1)S(1)} async-done(((bf16[16,144,128]{2,1,0:T(8,128)(2,1)}), bf16[16,144,128]{2,1,0:T(8,128)(2,1)S(1)}, u32[]{:S(2)}, u32[]{:S(2)}) %all-to-all-start.2) | async-done | bytes 589856 | tf_op jit(solution)/shard_map/all_to_all | solution.py:206
  69.4 0.9 copy-done.1
  70.3 1.1 copy-done.2
  71.3 5.2 %backward.2 = f32[2,144,1024]{2,1,0:T(8,128)S(1)} custom-call(bf16[16,144,128]{2,1,0:T(8,128)(2,1)S(1)} %copy-done.2, bf16[2048,2048]{1,0:T(8,128)(2,1)} %get-tuple-element.8.tile_ref), custom_call_target="tpu_custom_call" | custom-call | flops 1266679808 | bytes 10485760 | tf_op jit(solution)/shard_map/backward/pallas_call | solution.py:152
  76.5 0.9 dynamic-slice_bitcast_fusion.2
  77.4 2.3 collective-permute-done
  79.8 1.2 bitcast_add_fusion
  81.0 1.7 collective-permute-start.1
  82.7 2.2 collective-permute-start.3
  84.9 5.3 %collective-permute-done.1 = f32[144,512]{1,0:T(8,128)S(1)} collective-permute-done((f32[144,512]{1,0:T(8,128)S(1)}, f32[144,512]{1,0:T(8,128)S(1)}, u32[]{:S(2)}, u32[]{:S(2)}) %collective-permute-start.1) | collective-permute-done | bytes 294944 | tf_op jit(solution)/shard_map/ppermute | solution.py:236
  90.1 2.5 %collective-permute-done.3 = f32[144,512]{1,0:T(8,128)S(1)} collective-permute-done((f32[144,512]{1,0:T(8,128)S(1)}, f32[144,512]{1,0:T(8,128)S(1)}, u32[]{:S(2)}, u32[]{:S(2)}) %collective-permute-start.3) | collective-permute-done | bytes 294944 | tf_op jit(solution)/shard_map/ppermute | solution.py:237
  92.6 0.9 slice_add_fusion.2
  93.6 2.2 collective-permute-start.2
  95.9 7.2 %collective-permute-done.2 = f32[144,512]{1,0:T(8,128)} collective-permute-done((f32[144,512]{1,0:T(8,128)}, f32[144,512]{1,0:T(8,128)}, u32[]{:S(2)}, u32[]{:S(2)}) %collective-permute-start.2) | collective-permute-done | bytes 294944 | tf_op jit(solution)/shard_map/ppermute | solution.py:238
  103.0 1.1 add.120
  104.1 1.1 add.122
  105.3 0.9 fusion.14
  106.2 1.2 fusion.4
  107.4 0.8 copy.28
  108.2 0.5 collective-permute-start.6
  108.7 0.8 collective-permute-done.6
  109.6 0.6 collective-permute-done.5
  110.2 1.1 select_bitcast_fusion.3
  111.3 7.7 %forward.2 = f32[16,144,128]{2,1,0:T(8,128)S(1)} custom-call(bf16[2,144,1024]{2,1,0:T(8,128)(2,1)S(1)} %pad_maximum_fusion.3.lifted_ref, bf16[2048,2048]{1,0:T(8,128)(2,1)} %get-tuple-element.8.tile_ref), custom_call_target="tpu_custom_call" | custom-call | flops 1266679808 | bytes 10485760 | tf_op jit(solution)/shard_map/forward/pallas_call | solution.py:120
  119.1 23.2 %all_to_all.43 = f32[16,152,128]{2,1,0:T(8,128)} all-to-all(f32[16,152,128]{2,1,0:T(8,128)S(1)} %pad_maximum_fusion), channel_id=1, replica_groups=mesh['ex'=8,'ctr'=16] {'ctr'}, dimensions={0} | all-to-all | bytes 2490368 | tf_op jit(solution)/shard_map/all_to_all | solution.py:209
  142.3 1.4 reduce_sum.110
  143.7 0.1 multiply_reduce_fusion.2
  143.9 0.1 broadcast_in_dim.36
  144.0 15.5 %all_to_all.44 = bf16[16,160,128]{2,1,0:T(8,128)(2,1)S(1)} all-to-all(bf16[16,160,128]{2,1,0:T(8,128)(2,1)S(1)} %broadcast_in_dim.36), channel_id=1, replica_groups=mesh['ex'=8,'ctr'=16] {'ctr'}, dimensions={0} | all-to-all | bytes 1310720 | tf_op jit(solution)/shard_map/all_to_all | solution.py:206
  159.5 0.9 copy-done.8
  160.5 1.1 slice.76.values_ref
  161.6 5.2 %backward.3 = f32[2,144,1024]{2,1,0:T(8,128)S(1)} custom-call(bf16[16,144,128]{2,1,0:T(8,128)(2,1)S(1)} %slice.76.values_ref, bf16[2048,2048]{1,0:T(8,128)(2,1)} %get-tuple-element.8.tile_ref), custom_call_target="tpu_custom_call" | custom-call | flops 1266679808 | bytes 10485760 | tf_op jit(solution)/shard_map/backward/pallas_call | solution.py:152
  166.8 0.1 dynamic-slice_bitcast_fusion.1
  167.1 2.0 collective-permute-done.7
  169.2 2.2 collective-permute-start.10
  171.5 8.4 %collective-permute-done.10 = f32[152,512]{1,0:T(8,128)S(1)} collective-permute-done((f32[152,512]{1,0:T(8,128)S(1)}, f32[152,512]{1,0:T(8,128)S(1)}, u32[]{:S(2)}, u32[]{:S(2)}) %collective-permute-start.10) | collective-permute-done | bytes 311328 | tf_op jit(solution)/shard_map/ppermute | solution.py:237
  179.9 0.7 collective-permute-done.8
  180.6 0.1 slice_add_fusion.3
  180.7 1.6 collective-permute-start.9
  182.3 8.0 %collective-permute-done.9 = f32[152,512]{1,0:T(8,128)S(1)} collective-permute-done((f32[152,512]{1,0:T(8,128)S(1)}, f32[152,512]{1,0:T(8,128)S(1)}, u32[]{:S(2)}, u32[]{:S(2)}) %collective-permute-start.9) | collective-permute-done | bytes 311328 | tf_op jit(solution)/shard_map/ppermute | solution.py:238
  190.3 0.2 collective-permute-done.11
  190.7 0.7 copy-done.7
  191.4 1.1 fusion.15
  192.5 1.2 fusion.5
  193.8 0.5 collective-permute-start.13
  194.3 0.1 collective-permute-start.14
  194.4 1.0 collective-permute-done.13
  195.6 7.7 %forward.3 = f32[16,144,128]{2,1,0:T(8,128)S(1)} custom-call(bf16[2,144,1024]{2,1,0:T(8,128)(2,1)S(1)} %pad_maximum_fusion.5.lifted_ref, bf16[2048,2048]{1,0:T(8,128)(2,1)} %get-tuple-element.8.tile_ref), custom_call_target="tpu_custom_call" | custom-call | flops 1266679808 | bytes 10485760 | tf_op jit(solution)/shard_map/forward/pallas_call | solution.py:120
  203.4 22.7 %all_to_all.45 = f32[16,152,128]{2,1,0:T(8,128)S(1)} all-to-all(f32[16,152,128]{2,1,0:T(8,128)S(1)} %pad_maximum_fusion.1), channel_id=1, replica_groups=mesh['ex'=8,'ctr'=16] {'ctr'}, dimensions={0} | all-to-all | bytes 2490368 | tf_op jit(solution)/shard_map/all_to_all | solution.py:209
  226.1 0.7 reduce_sum.118
  226.8 0.8 slice_bitcast_fusion
  227.6 1.1 multiply_reduce_fusion.1
  228.7 8.2 %all_to_all.46 = f32[8,1,144]{2,1,0:T(1,128)S(1)} all-to-all(f32[8,1,144]{2,1,0:T(1,128)S(1)} %broadcast_in_dim.39), channel_id=1, replica_groups=mesh['ex'=8,'ctr'=16] {'ex'}, dimensions={0} | all-to-all | bytes 9216 | tf_op jit(solution)/shard_map/all_to_all | solution.py:301
  237.0 10.6 %all_to_all.47 = f32[16,1,144]{2,1,0:T(1,128)S(1)} all-to-all(f32[16,1,144]{2,1,0:T(1,128)S(1)} %broadcast_in_dim.40), channel_id=1, replica_groups=mesh['ex'=8,'ctr'=16] {'ctr'}, dimensions={0} | all-to-all | bytes 18432 | tf_op jit(solution)/shard_map/all_to_all | solution.py:302
  247.6 1.7 multiply_add_fusion
  (71 shorter events, 1.5 us)
Async XLA Ops:
  0.0 95.8 %copy-start = (f32[2048,256]{1,0:T(8,128)S(1)}, f32[2048,256]{1,0:T(8,128)}, u32[]{:S(2)}) copy-start(f32[2048,256]{1,0:T(8,128)} %param.13) | copy-start | bytes 6291460
  0.0 20.3 %copy-start.3 = (bf16[144,2048]{1,0:T(8,128)(2,1)S(1)}, bf16[144,2048]{1,0:T(8,128)(2,1)}, u32[]{:S(2)}) copy-start(bf16[144,2048]{1,0:T(8,128)(2,1)} %alpha_ref.1) | copy-start | bytes 1769476
  0.0 20.3 %copy-start.4 = (bf16[64,2048]{1,0:T(8,128)(2,1)S(1)}, bf16[64,2048]{1,0:T(8,128)(2,1)}, u32[]{:S(2)}) copy-start(bf16[64,2048]{1,0:T(8,128)(2,1)} %centers_ref.1) | copy-start | bytes 786436
  0.0 20.3 %copy-start.5 = (s32[2048]{0:T(1024)S(1)}, s32[2048]{0:T(1024)}, u32[]{:S(2)}) copy-start(s32[2048]{0:T(1024)} %param.8) | copy-start | bytes 24580
  31.8 21.6 %all-to-all-start.1 = ((f32[16,144,128]{2,1,0:T(8,128)}), f32[16,144,128]{2,1,0:T(8,128)S(1)}, u32[]{:S(2)}, u32[]{:S(2)}) async-start(f32[16,144,128]{2,1,0:T(8,128)} %get-tuple-element.7), calls=%async_computation.1 | async-start | bytes 2359296 | tf_op jit(solution)/shard_map/all_to_all | solution.py:209
  54.4 15.0 %all-to-all-start.2 = ((bf16[16,144,128]{2,1,0:T(8,128)(2,1)}), bf16[16,144,128]{2,1,0:T(8,128)(2,1)S(1)}, u32[]{:S(2)}, u32[]{:S(2)}) async-start(bf16[16,144,128]{2,1,0:T(8,128)(2,1)} %broadcast_in_dim.34), calls=%async_computation.2 | async-start | bytes 1179648 | tf_op jit(solution)/shard_map/all_to_all | solution.py:206
  69.4 0.9 copy-start.1
  70.3 1.1 copy-start.2
  77.4 2.3 collective-permute-start
  81.0 9.1 %collective-permute-start.1 = (f32[144,512]{1,0:T(8,128)S(1)}, f32[144,512]{1,0:T(8,128)S(1)}, u32[]{:S(2)}, u32[]{:S(2)}) collective-permute-start(f32[144,512]{1,0:T(8,128)S(1)} %get-tuple-element.29), channel_id=1, source_target_pairs={{0,32},{16,48},{32,0},{48,16},{64,96},{80,112},{96,64},{112,80},{1... | collective-permute-start | bytes 884744 | tf_op jit(solution)/shard_map/ppermute | solution.py:236
  82.7 10.0 %collective-permute-start.3 = (f32[144,512]{1,0:T(8,128)S(1)}, f32[144,512]{1,0:T(8,128)S(1)}, u32[]{:S(2)}, u32[]{:S(2)}) collective-permute-start(f32[144,512]{1,0:T(8,128)S(1)} %get-tuple-element.30), channel_id=1, source_target_pairs={{0,96},{16,112},{32,64},{48,80},{64,32},{80,48},{96,0},{112,16},{1... | collective-permute-start | bytes 884744 | tf_op jit(solution)/shard_map/ppermute | solution.py:237
  93.6 9.4 %collective-permute-start.2 = (f32[144,512]{1,0:T(8,128)}, f32[144,512]{1,0:T(8,128)}, u32[]{:S(2)}, u32[]{:S(2)}) collective-permute-start(f32[144,512]{1,0:T(8,128)} %get-tuple-element.27), channel_id=1, source_target_pairs={{0,96},{16,112},{32,64},{48,80},{64,32},{80,48},{96,0},{112,16},{1... | collective-permute-start | bytes 884744 | tf_op jit(solution)/shard_map/ppermute | solution.py:238
  95.8 8.3 %collective-permute-start.4 = (f32[144,512]{1,0:T(8,128)}, f32[144,512]{1,0:T(8,128)}, u32[]{:S(2)}, u32[]{:S(2)}) collective-permute-start(f32[144,512]{1,0:T(8,128)} %get-tuple-element.28), channel_id=1, source_target_pairs={{0,32},{16,48},{32,0},{48,16},{64,96},{80,112},{96,64},{112,80},{1... | collective-permute-start | bytes 884744 | tf_op jit(solution)/shard_map/ppermute | solution.py:239
  106.2 2.0 copy-start.6
  108.2 1.9 collective-permute-start.5
  108.2 1.3 collective-permute-start.6
  159.5 0.9 copy-start.8
  167.0 2.1 collective-permute-start.7
  169.2 10.7 %collective-permute-start.10 = (f32[152,512]{1,0:T(8,128)S(1)}, f32[152,512]{1,0:T(8,128)S(1)}, u32[]{:S(2)}, u32[]{:S(2)}) collective-permute-start(f32[152,512]{1,0:T(8,128)S(1)} %get-tuple-element.21), channel_id=1, source_target_pairs={{0,96},{16,112},{32,64},{48,80},{64,32},{80,48},{96,0},{112,16},{1... | collective-permute-start | bytes 933896 | tf_op jit(solution)/shard_map/ppermute | solution.py:237
  171.5 9.1 %collective-permute-start.8 = (f32[152,512]{1,0:T(8,128)S(1)}, f32[152,512]{1,0:T(8,128)S(1)}, u32[]{:S(2)}, u32[]{:S(2)}) collective-permute-start(f32[152,512]{1,0:T(8,128)S(1)} %get-tuple-element.22), channel_id=1, source_target_pairs={{0,32},{16,48},{32,0},{48,16},{64,96},{80,112},{96,64},{112,80},{1... | collective-permute-start | bytes 933896 | tf_op jit(solution)/shard_map/ppermute | solution.py:236
  180.7 9.5 %collective-permute-start.9 = (f32[152,512]{1,0:T(8,128)S(1)}, f32[152,512]{1,0:T(8,128)S(1)}, u32[]{:S(2)}, u32[]{:S(2)}) collective-permute-start(f32[152,512]{1,0:T(8,128)S(1)} %get-tuple-element.20), channel_id=1, source_target_pairs={{0,96},{16,112},{32,64},{48,80},{64,32},{80,48},{96,0},{112,16},{1... | collective-permute-start | bytes 933896 | tf_op jit(solution)/shard_map/ppermute | solution.py:238
  182.3 8.3 %collective-permute-start.11 = (f32[152,512]{1,0:T(8,128)S(1)}, f32[152,512]{1,0:T(8,128)S(1)}, u32[]{:S(2)}, u32[]{:S(2)}) collective-permute-start(f32[152,512]{1,0:T(8,128)S(1)} %get-tuple-element.19), channel_id=1, source_target_pairs={{0,32},{16,48},{32,0},{48,16},{64,96},{80,112},{96,64},{112,80},{1... | collective-permute-start | bytes 933896 | tf_op jit(solution)/shard_map/ppermute | solution.py:239
  190.3 1.1 copy-start.7
  193.7 1.8 collective-permute-start.12
  193.8 1.6 collective-permute-start.13
  194.3 1.1 collective-permute-start.14

commit v2 on v0

v2 whole, which is shorter than its diff:
```python
import functools
import math

import jax
import jax.numpy as jnp
from jax import lax
from jax.experimental import pallas as pl
from jax.experimental.pallas import tpu as pltpu
from jax.sharding import PartitionSpec as P

RIDGE = 0.0001
F32 = jnp.float32
BF16 = jnp.bfloat16
VMEM_BYTES = 24 * 1024 * 1024
DEPTH = 128
BAND = 256
EXTRA = 16
LANES = 128
NT = (((1,), (1,)), ((), ()))
TN = (((0,), (0,)), ((), ()))


def split3(values):
    high = values.astype(BF16)
    rest = values - high.astype(F32)
    middle = rest.astype(BF16)
    low = (rest - middle.astype(F32)).astype(BF16)
    return high, middle, low


SCALAR = pl.BlockSpec(memory_space=pltpu.SMEM)
WHOLE = pl.BlockSpec(memory_space=pltpu.VMEM)


def call(kernel, name, out_shape, flops, scratch=(), scalars=0, arrays=0):
    shapes = out_shape if isinstance(out_shape, list) else [out_shape]
    size = sum(math.prod(s.shape) * s.dtype.itemsize for s in shapes)
    return pl.pallas_call(
        kernel,
        out_shape=out_shape,
        scratch_shapes=list(scratch),
        in_specs=[SCALAR] * scalars + [WHOLE] * arrays,
        compiler_params=pltpu.CompilerParams(vmem_limit_bytes=VMEM_BYTES),
        cost_estimate=pl.CostEstimate(flops=flops, bytes_accessed=size, transcendentals=0),
        name=name,
    )


def rows_of(vectors):
    row = lax.broadcasted_iota(jnp.int32, (EXTRA, LANES), 0)
    out = jnp.zeros((EXTRA, LANES), F32)
    for k, vector in enumerate(vectors):
        for p, piece in enumerate(split3(vector)):
            for q in range(2):
                value = piece.astype(F32)[:, q * LANES : (q + 1) * LANES]
                out = jnp.where(row == 6 * k + 2 * p + q, value, out)
    return out.astype(BF16)


def read_rows(summed, k):
    halves = [
        sum(summed[6 * k + 2 * p + q : 6 * k + 2 * p + q + 1] for p in range(3)) for q in range(2)
    ]
    return jnp.concatenate(halves, axis=1)


def column(vector, classes):
    return jnp.broadcast_to(vector, (8, vector.shape[1])).T[:classes, :1]


def lane_sums(values):
    folded = sum(values[:, k : k + LANES] for k in range(0, values.shape[1], LANES))
    empty = jnp.zeros((2 * LANES - values.shape[0], LANES), F32)
    return jnp.sum(jnp.concatenate([folded, empty], axis=0).T, axis=0, keepdims=True)


def stack_rows(vectors):
    row = lax.broadcasted_iota(jnp.int32, (8, 2 * LANES), 0)
    out = jnp.zeros((8, 2 * LANES), F32)
    for k, vector in enumerate(vectors):
        out = jnp.where(row == k, vector, out)
    return out


def sum_parts(ref):
    total = ref[0].astype(F32)
    for k in range(1, ref.shape[0]):
        total = total + ref[k].astype(F32)
    return total


def shape(dims, dtype):
    return jax.ShapeDtypeStruct(dims, dtype)


def tail(squares, first, pad):
    pieces = [p.astype(F32) for p in split3(-0.5 * squares)]
    row = lax.broadcasted_iota(jnp.int32, (pad, squares.shape[1]), 0)
    out = jnp.where((row >= 3 - first) & (row < 6 - first), 1.0, 0.0)
    for k in range(3):
        out = jnp.where(row == k + first, pieces[k], out)
    return out


def prepare_kernel(index_ref, centers_ref, sides_ref, one_hot_ref):
    features, count = centers_ref.shape
    lanes = one_hot_ref.shape[0]
    center_float = centers_ref[...].astype(F32)
    center_sq = jnp.sum(center_float * center_float, axis=0, keepdims=True)
    side = jnp.concatenate([center_float, tail(center_sq, 3, DEPTH - features)], axis=0)
    sides_ref[...] = side.T.astype(BF16)
    within = index_ref[...] % lanes
    row = lax.broadcasted_iota(jnp.int32, (lanes, index_ref.shape[1]), 0)
    one_hot_ref[...] = (row == within).astype(F32).astype(BF16)


def prepare(indices, centers, lanes):
    features, count = centers.shape
    examples = indices.shape[0]
    return call(
        prepare_kernel,
        "prepare",
        [shape((count, DEPTH), BF16), shape((lanes, examples), BF16)],
        1 << 20,
        arrays=2,
    )(indices.reshape(1, examples), centers)


def tile_kernel(index_ref, pool_ref, one_hot_ref, sides_ref, alpha_ref, tile_ref, high_ref, low_ref, side_ref):
    chunks, features, lanes = pool_ref.shape
    count, examples = tile_ref.shape
    share = high_ref.shape[2]
    scale = 4.0 / features * math.log2(math.e)
    pool = pool_ref[...].reshape(chunks * features, lanes)

    def gather(b, carry):
        here = pl.ds(pl.multiple_of(b * BAND, BAND), BAND)
        chunk = index_ref[:, here] // lanes
        picked = jnp.dot(pool, one_hot_ref[:, here], preferred_element_type=F32)
        points = jnp.where(chunk == 0, picked[:features], 0.0)
        for k in range(1, chunks):
            points = jnp.where(chunk == k, picked[k * features : (k + 1) * features], points)
        point_sq = jnp.sum(points * points, axis=0, keepdims=True)
        side = jnp.concatenate([points, tail(point_sq, 0, DEPTH - features)], axis=0)
        side_ref[:, here] = side.astype(BF16)
        return carry

    lax.fori_loop(0, examples // BAND, gather, 0, unroll=True)

    def fill(b, carry):
        rows = pl.ds(pl.multiple_of(b * BAND, BAND), BAND)
        near = jnp.dot(sides_ref[rows, :], side_ref[...], preferred_element_type=F32)
        tile_ref[rows, :] = jnp.exp2(near * scale).astype(BF16)
        return carry

    lax.fori_loop(0, count // BAND, fill, 0, unroll=2)

    def product(b, carry):
        here = pl.ds(pl.multiple_of(b * BAND, BAND), BAND)
        rows = jnp.dot(alpha_ref[...], tile_ref[:, here], preferred_element_type=F32)
        for k in range(BAND // share):
            piece = rows[:, k * share : (k + 1) * share]
            high = piece.astype(BF16)
            high_ref[b * (BAND // share) + k] = high
            low_ref[b * (BAND // share) + k] = (piece - high.astype(F32)).astype(BF16)
        return carry

    lax.fori_loop(0, examples // BAND, product, 0, unroll=True)


def make_tile(indices, row_pool, one_hot, sides, alpha, share):
    examples, count = indices.shape[0], sides.shape[0]
    classes = alpha.shape[0]
    parts = shape((examples // share, classes, share), BF16)
    return call(
        tile_kernel,
        "tile",
        [shape((count, examples), BF16), parts, parts],
        4 << 30,
        [pltpu.VMEM((DEPTH, examples), BF16)],
        arrays=5,
    )(indices.reshape(1, examples), row_pool, one_hot, sides, alpha)


def turn_kernel(tile_ref, turned_ref):
    count, examples = tile_ref.shape

    def band(b, carry):
        start = pl.multiple_of(b * BAND, BAND)
        turned_ref[:, pl.ds(start, BAND)] = tile_ref[pl.ds(start, BAND), :].T
        return carry

    lax.fori_loop(0, count // BAND, band, 0)


def turn(tile):
    return call(turn_kernel, "turn", shape(tile.shape[::-1], BF16), 8 << 20, arrays=1)(tile)


def factors_kernel(core_ref, precond_ref, high_ref, low_ref, high_turned_ref, low_turned_ref):
    order = precond_ref.shape[1]
    half = high_ref.shape[0]
    first = core_ref[0] * half
    for k in range(half // order):
        here = slice(k * order, (k + 1) * order)
        block = precond_ref[pl.ds(pl.multiple_of(first + k * order, order), order), :]
        high = block.astype(BF16)
        high_ref[here] = high
        low_ref[here] = (block - high.astype(F32)).astype(BF16)
        turned = block.T
        high = turned.astype(BF16)
        high_turned_ref[here] = high
        low_turned_ref[here] = (turned - high.astype(F32)).astype(BF16)


def factors(core, precond):
    out = shape((precond.shape[0] // 2, precond.shape[1]), BF16)
    return call(factors_kernel, "factors", [out] * 4, 1 << 20, scalars=1, arrays=1)(core, precond)


def block_products(values, high_ref, low_ref):
    order = high_ref.shape[1]
    out = []
    for k in range(high_ref.shape[0] // order):
        here = slice(k * order, (k + 1) * order)
        block = values[:, here]
        high = block.astype(BF16)
        low = (block - high.astype(F32)).astype(BF16)
        product = jnp.dot(high, high_ref[here], preferred_element_type=F32)
        product += jnp.dot(high, low_ref[here], preferred_element_type=F32)
        product += jnp.dot(low, high_ref[here], preferred_element_type=F32)
        out.append(product)
    return jnp.concatenate(out, axis=1)


def forward_kernel(
    core_ref, own_ref, other_ref, own_part_ref, other_part_ref, tile_ref, high_ref, low_ref
):
    classes, half = own_ref.shape
    share = high_ref.shape[2]
    examples = tile_ref.shape[1]
    mine = pl.ds(pl.multiple_of(core_ref[0] * half, half), half)
    theirs = pl.ds(pl.multiple_of((1 - core_ref[0]) * half, half), half)
    part = own_part_ref[...] + other_part_ref[...]
    extra = rows_of([part[:1], part[1:2]])
    for b in range(examples // BAND):
        here = slice(b * BAND, (b + 1) * BAND)
        rows = jnp.dot(own_ref[...], tile_ref[mine, here], preferred_element_type=F32)
        rows += jnp.dot(other_ref[...], tile_ref[theirs, here], preferred_element_type=F32)
        for k in range(BAND // share):
            piece = rows[:, k * share : (k + 1) * share]
            high = piece.astype(BF16)
            at = b * (BAND // share) + k
            high_ref[at, :classes] = high
            high_ref[at, classes:] = extra
            low_ref[at] = (piece - high.astype(F32)).astype(BF16)


def forward(core, own, other, own_part, other_part, tile, share):
    classes = own.shape[0]
    shares = tile.shape[1] // share
    return call(
        forward_kernel,
        "forward",
        [shape((shares, classes + EXTRA, share), BF16), shape((shares, classes, share), BF16)],
        1208 << 20,
        scalars=1,
        arrays=5,
    )(core, own, other, own_part, other_part, tile)


def backward_kernel(core_ref, values_ref, turned_ref, other_ref, one_ref, two_ref, flat_ref):
    shares, height, share = values_ref.shape
    classes, examples = flat_ref.shape
    half = other_ref.shape[1]
    wide = half // 2
    for k in range(shares):
        flat_ref[:, k * share : (k + 1) * share] = values_ref[k, :classes]
    if height > classes:
        total = values_ref[0, classes:].astype(F32)
        for k in range(1, shares):
            total = total + values_ref[k, classes:].astype(F32)
        row = read_rows(total, 0)
        other_ref[classes:, : 2 * LANES] = jnp.broadcast_to(row, (8, 2 * LANES))
        other_ref[classes:, 2 * LANES :] = jnp.zeros((8, half - 2 * LANES), F32)
        one_ref[classes:, : 2 * LANES] = jnp.broadcast_to(row, (8, 2 * LANES))
        one_ref[classes:, 2 * LANES :] = jnp.zeros((8, wide - 2 * LANES), F32)
    for h, first in enumerate(((1 - core_ref[0]) * half, core_ref[0] * half)):
        for b in range(half // BAND):
            there = pl.ds(pl.multiple_of(first + b * BAND, BAND), BAND)
            sums = jnp.dot(flat_ref[...], turned_ref[:, there], preferred_element_type=F32)
            if h == 0:
                other_ref[:classes, b * BAND : (b + 1) * BAND] = sums
            elif b * BAND < wide:
                one_ref[:classes, b * BAND : (b + 1) * BAND] = sums
            else:
                two_ref[:, b * BAND - wide : (b + 1) * BAND - wide] = sums


def backward(core, values, turned, classes):
    examples, count = turned.shape
    height = classes + (8 if values.shape[1] > classes else 0)
    half = count // 2
    return call(
        backward_kernel,
        "backward",
        [shape((height, half), F32), shape((height, half // 2), F32), shape((classes, half // 2), F32)],
        1208 << 20,
        [pltpu.VMEM((classes, examples), BF16)],
        scalars=1,
        arrays=2,
    )(core, values, turned)


def gradient_kernel(parts_ref, label_ref, weight_ref, base_ref, hessian_ref, send_ref):
    classes, share = base_ref.shape
    base = sum_parts(parts_ref)
    base_ref[...] = base
    probability = jax.nn.sigmoid(base)
    row = lax.broadcasted_iota(jnp.int32, (classes, share), 0)
    target = jnp.where(row == label_ref[...], 1.0, 0.0)
    hessian_ref[...] = weight_ref[...] * probability * (1.0 - probability)
    gradient = (weight_ref[...] * (probability - target)).astype(BF16)
    for k in range(send_ref.shape[0]):
        send_ref[k] = gradient


def gradient(parts, label, weight):
    block = shape(parts.shape[1:], F32)
    return call(
        gradient_kernel, "gradient", [block, block, shape(parts.shape, BF16)], 1 << 20, arrays=3
    )(parts, label, weight)


def residual_kernel(
    total, one_ref, one_in_ref, two_ref, two_in_ref, high_ref, low_ref, high_turned_ref,
    low_turned_ref, residual_ref, lifted_ref, part_ref,
):
    sums = jnp.concatenate([one_ref[...] + one_in_ref[...], two_ref[...] + two_in_ref[...]], axis=1)
    residual = block_products(sums, high_ref, low_ref) * (-1.0 / total)
    residual_ref[...] = residual
    lifted_ref[...] = block_products(residual, high_turned_ref, low_turned_ref).astype(BF16)
    part_ref[...] = stack_rows([lane_sums(residual * residual)])


def first_residual(total, sums, blocks):
    classes, wide = sums[2].shape
    return call(
        functools.partial(residual_kernel, total),
        "residual",
        [
            shape((classes, 2 * wide), F32),
            shape((classes, 2 * wide), BF16),
            shape((8, 2 * LANES), F32),
        ],
        450 << 20,
        arrays=8,
    )(*sums, *blocks)


def weigh_kernel(parts_ref, hessian_ref, image_ref, norm_ref, send_ref):
    classes = hessian_ref.shape[0]
    total = sum_parts(parts_ref)
    image = total[:classes]
    image_ref[...] = image
    norm_ref[...] = stack_rows([read_rows(total[classes:], 0)])
    weighted = (hessian_ref[...] * image).astype(BF16)
    extra = rows_of([lane_sums(weighted.astype(F32) * image)])
    for k in range(send_ref.shape[0]):
        send_ref[k, :classes] = weighted
        send_ref[k, classes:] = extra


def weigh(parts, hessian):
    return call(
        weigh_kernel,
        "weigh",
        [shape(hessian.shape, F32), shape((8, 2 * LANES), F32), shape(parts.shape, BF16)],
        1 << 20,
        arrays=2,
    )(parts, hessian)


def step_kernel(
    total, one_ref, one_in_ref, two_ref, two_in_ref, high_ref, low_ref, high_turned_ref,
    low_turned_ref, residual_ref, norm_ref, lifted_ref, part_ref, rough_ref,
):
    classes = residual_ref.shape[0]
    one = one_ref[...] + one_in_ref[...]
    curve = one[classes : classes + 1, : 2 * LANES] / total
    norm = norm_ref[:1]
    lane = lax.broadcasted_iota(jnp.int32, (1, 2 * LANES), 1)
    rough = jnp.where(lane < classes, norm / (curve + RIDGE * norm), 0.0)
    rough_ref[...] = stack_rows([rough])
    sums = jnp.concatenate([one[:classes], two_ref[...] + two_in_ref[...]], axis=1)
    old = residual_ref[...]
    image = block_products(sums, high_ref, low_ref) / total + RIDGE * old
    new = old - column(rough, classes) * image
    lifted_ref[...] = block_products(new, high_turned_ref, low_turned_ref).astype(BF16)
    part_ref[...] = stack_rows([lane_sums(old * new), lane_sums(new * new)])


def step(total, sums, blocks, residual, norm):
    row = shape((8, 2 * LANES), F32)
    return call(
        functools.partial(step_kernel, total),
        "step",
        [shape(residual.shape, BF16), row, row],
        450 << 20,
        arrays=10,
    )(*sums, *blocks, residual, norm)


def curve_kernel(
    parts_ref, hessian_ref, image_ref, norm_ref, rough_ref, last_ref, scales_ref, curve_ref
):
    classes = hessian_ref.shape[0]
    total = sum_parts(parts_ref)
    last = total[:classes]
    last_ref[...] = last
    cross = read_rows(total[classes:], 0)
    norm_rough = read_rows(total[classes:], 1)
    norm = norm_ref[:1]
    lane = lax.broadcasted_iota(jnp.int32, (1, 2 * LANES), 1)
    excess = jnp.where(lane < classes, cross / (norm - cross), 0.0)
    grown = 1.0 + excess
    norm_next = grown * (grown * norm_rough - 2.0 * excess * cross) + excess * excess * norm
    ratio = jnp.where(lane < classes, norm_next / norm, 0.0)
    ridge = RIDGE * (norm_next + ratio * ratio * norm)
    scales_ref[...] = stack_rows(
        [rough_ref[:1] * grown, grown, ratio - excess, norm_next, ridge]
    )
    rows = column(grown, classes) * last + column(ratio - excess, classes) * image_ref[...]
    weighted = (hessian_ref[...] * rows).astype(BF16).astype(F32)
    curve_ref[...] = stack_rows([lane_sums(weighted * rows)])


def last_curve(parts, hessian, image, norm, rough):
    row = shape((8, 2 * LANES), F32)
    return call(
        curve_kernel,
        "curve",
        [shape(hessian.shape, F32), row, row],
        1 << 20,
        arrays=5,
    )(parts, hessian, image, norm, rough)


def margins_kernel(
    total, curve_ref, scales_ref, base_ref, base_low_ref, image_ref, image_low_ref, last_ref,
    last_low_ref, margins_ref,
):
    classes = base_ref.shape[0]
    curve = jnp.sum(curve_ref[:, 0], axis=0, keepdims=True)
    first, grown, other = scales_ref[0:1], scales_ref[1:2], scales_ref[2:3]
    lane = lax.broadcasted_iota(jnp.int32, (1, 2 * LANES), 1)
    second = jnp.where(
        lane < classes, scales_ref[3:4] / (curve / total + scales_ref[4:5]), 0.0
    )
    base = base_ref[...] + sum_parts(base_low_ref)
    image = image_ref[...] + sum_parts(image_low_ref)
    last = last_ref[...] + sum_parts(last_low_ref)
    margins_ref[...] = (
        base
        + column(first + second * other, classes) * image
        + column(second * grown, classes) * last
    )


def margins(total, curve, scales, base, base_low, image, image_low, last, last_low):
    return call(
        functools.partial(margins_kernel, total),
        "margins",
        shape(base.shape, F32),
        1 << 20,
        arrays=8,
    )(curve, scales, base, base_low, image, image_low, last, last_low)


def shards(pool, indices, labels, example_weight, centers, alpha, precond):
    n_ex, n_ctr = lax.axis_size("ex"), lax.axis_size("ctr")
    classes, count = alpha.shape
    examples = indices.shape[0]
    share = examples // n_ctr
    total = float(examples * n_ex)
    core = (lax.axis_index("ex") % 2).reshape(1)
    core_pairs = [(i, i ^ 1) for i in range(n_ex)]

    def over_y(array, flip):
        pairs = [(2 * y + c, 2 * (y ^ flip) + c) for y in range(n_ex // 2) for c in range(2)]
        return lax.ppermute(array, "ex", pairs)

    def over_cores(array):
        return lax.ppermute(array, "ex", core_pairs)

    def trade(parts):
        return lax.all_to_all(parts, "ctr", 0, 0)

    def tie(first, second):
        return lax.optimization_barrier((first, second))

    def sum_examples(products, low):
        other, one, two = products
        got = over_cores(other)
        wide = one.shape[1]
        one = one + got[:, :wide]
        two = two + got[:classes, wide:]
        one, low = tie(one, low)
        low = trade(low)
        one = one + over_y(one, 1)
        two = two + over_y(two, 3)
        one_in, two_in = over_y(one, 3), over_y(two, 1)
        one_in, low = tie(one_in, low)
        return (one, one_in, two, two_in), low

    offset = lax.axis_index("ctr") * share
    label = lax.dynamic_slice_in_dim(labels, offset, share, 0).reshape(1, share)
    weight = lax.dynamic_slice_in_dim(example_weight, offset, share, 0).reshape(1, share)

    row_pool = trade(jnp.broadcast_to(pool, (n_ctr,) + pool.shape))
    sides, one_hot = prepare(indices, centers, pool.shape[1])
    tile, base_high, base_low = make_tile(indices, row_pool, one_hot, sides, alpha, share)
    base_parts = trade(base_high)
    turned = turn(tile)
    blocks = factors(core, precond)
    base, hessian, send = gradient(base_parts, label, weight)

    sums, base_low = sum_examples(backward(core, trade(send), turned, classes), base_low)
    residual, lifted, part = first_residual(total, sums, blocks)
    high, image_low = forward(
        core, lifted, over_cores(lifted), part, over_cores(part), tile, share
    )
    image, norm, send = weigh(trade(high), hessian)

    sums, image_low = sum_examples(backward(core, trade(send), turned, classes), image_low)
    lifted, part, rough = step(total, sums, blocks, residual, norm)
    high, last_low = forward(core, lifted, over_cores(lifted), part, over_cores(part), tile, share)
    last, scales, curve = last_curve(trade(high), hessian, image, norm, rough)

    curve, last_low = tie(curve, last_low)
    last_low = trade(last_low)
    curve = curve + over_cores(curve)
    curve = curve + over_y(curve, 1)
    curve = curve + over_y(curve, 3)
    curve, last_low = tie(curve, last_low)
    curve = trade(jnp.broadcast_to(curve, (n_ctr,) + curve.shape))
    return margins(total, curve, scales, base, base_low, image, image_low, last, last_low)


def solution(mesh):
    return jax.shard_map(
        shards,
        mesh=mesh,
        in_specs=(
            P(None, ("ex", "ctr")),
            P("ex"),
            P("ex"),
            P("ex"),
            P(None, "ctr"),
            P(None, "ctr"),
            P("ctr", None),
        ),
        out_specs=P(None, ("ex", "ctr")),
        check_vma=False,
    )
```

time: 675 us -> 228 us (0.34)
  waiting for transfers between devices: 442 us -> 52.5 us
  blocking collectives: 143 us -> 64.7 us
  matrix products: 53.4 us -> 0 us
  starting transfers between devices: 0.39 us -> 42.6 us
  Pallas kernels: 0 us -> 24.2 us
  local copies, waits for them, and re-layouts: 15.6 us -> 35.8 us
  between operations: 13.6 us -> 0.33 us
    psum x6 -> x0, waiting for transfers between devices: 442 us -> none  [the longest x3 255 us: forward(): return lax.psum(partial_rows(coefficients), 'ctr')]
    psum x3 -> x0, blocking collectives: 117 us -> none  [the longest x2 76.2 us: squares(): return lax.psum(jnp.sum(residual * residual, axis=1), 'ctr')]
    all_to_all x0 -> x4, blocking collectives: none -> 64.7 us  [trade(): return lax.all_to_all(parts, 'ctr', 0, 0)]
    dot_general x12 -> x0, matrix products: 53.4 us -> none  [the longest x3 16.6 us: backward(): return jnp.dot(values, tile_values, preferred_element_type=jnp.float32)]
    all_to_all x0 -> x6, waiting for transfers between devices: none -> 31.3 us  [trade(): return lax.all_to_all(parts, 'ctr', 0, 0)]
    unnamed x15 -> x62, local copies, waits for them, and re-layouts: 4.11 us -> 33.3 us
    all_to_all x0 -> x6, starting transfers between devices: none -> 28.5 us  [trade(): return lax.all_to_all(parts, 'ctr', 0, 0)]
    all_gather x1 -> x0, blocking collectives: 26.3 us -> none  [shards(): row_pool = lax.all_gather(pool, 'ctr', axis=1, tiled=True)]
  transfers between devices with their start and end apart: 6 -> 23, of which waited for: 6 -> 17; matrix products, arithmetic and copies ran while one was open for 0% -> 3% of each run, Pallas kernels for 0% -> 2%
where the time goes in v2:
time: 228 us; the launch traced here: 226 us
  blocking collectives  64.7 us (28%)
  waiting for transfers between devices  52.5 us (23%)
  starting transfers between devices  42.6 us (19%)
  local copies, waits for them, and re-layouts  35.8 us (16%)
  Pallas kernels  24.2 us (11%)
  other arithmetic  5.96 us (3%)
    all_to_all x4, blocking collectives, trade(): return lax.all_to_all(parts, 'ctr', 0, 0)  64.7 us
    unnamed x62, local copies, waits for them, and re-layouts  33.3 us
    all_to_all x6, waiting for transfers between devices, trade(): return lax.all_to_all(parts, 'ctr', 0, 0)  31.3 us
    all_to_all x6, starting transfers between devices, trade(): return lax.all_to_all(parts, 'ctr', 0, 0)  28.5 us
    ppermute x10, waiting for transfers between devices, over_y(): return lax.ppermute(array, 'ex', pairs)  13.8 us
    ppermute x10, starting transfers between devices, over_y(): return lax.ppermute(array, 'ex', pairs)  12.6 us
    ppermute x7, waiting for transfers between devices, over_cores(): return lax.ppermute(array, 'ex', core_pairs)  7.36 us
    pallas_call x1, Pallas kernels, make_tile(): call(tile_kernel, 'tile', [shape((count, examples), BF16), parts, parts],...  6.57 us
  transfers between devices with their start and end apart: 23, of which 17 were waited for; matrix products, arithmetic and copies ran while one was open for 3% of the time, Pallas kernels for 2%

profile of v2, /device:TPU:0, one launch (start us, length us, event | category | flops | bytes accessed | tf_op | source)
XLA Modules:
  0.0 226.0 jit_solution(12259910597438009088)
XLA Ops:
  0.0 1.6 broadcast_in_dim.6
  1.6 8.0 %all-to-all-start = ((bf16[16,64,256]{2,1,0:T(8,128)(2,1)}), bf16[16,64,256]{2,1,0:T(8,128)(2,1)S(1)}, u32[]{:S(2)}, u32[]{:S(2)}) async-start(bf16[16,64,256]{2,1,0:T(8,128)(2,1)} %broadcast_in_dim.6), calls=%async_computation | async-start | bytes 1048576 | tf_op jit(solution)/shard_map/all_to_all | solution.py:497
  9.6 0.9 copy-done.23
  11.9 9.2 %all-to-all-done.pool_ref = bf16[16,64,256]{2,1,0:T(8,128)(2,1)S(1)} async-done(((bf16[16,64,256]{2,1,0:T(8,128)(2,1)}), bf16[16,64,256]{2,1,0:T(8,128)(2,1)S(1)}, u32[]{:S(2)}, u32[]{:S(2)}) %all-to-all-start) | async-done | bytes 524320 | tf_op jit(solution)/shard_map/all_to_all | solution.py:497
  21.8 1.1 copy-done.28
  22.9 6.6 %tile.1 = (bf16[2048,2048]{1,0:T(8,128)(2,1)S(1)}, bf16[16,144,128]{2,1,0:T(8,128)(2,1)}, bf16[16,144,128]{2,1,0:T(8,128)(2,1)}) custom-call(s32[1,2048]{1,0:T(1,128)S(1)} %bitcast.7, bf16[16,64,256]{2,1,0:T(8,128)(2,1)S(1)} %all-to-all-done.pool_ref, bf16[256,2048]{1,0:T(8,128)(2,1)S(1)} %get-tuple-element.51.one_hot_ref, ...), custom_call_target="tpu_custom_call" | custom-call | flops 4294967296 | bytes 9568256 | tf_op jit(solution)/shard_map/tile/pallas_call | solution.py:175
  29.5 3.3 %copy-done.1 = bf16[2048,2048]{1,0:T(8,128)(2,1)} copy-done((bf16[2048,2048]{1,0:T(8,128)(2,1)}, bf16[2048,2048]{1,0:T(8,128)(2,1)S(1)}, u32[]{:S(2)}) %copy-start.1) | copy-done | bytes 8388632
  32.8 3.6 %all-to-all-start.1 = ((bf16[16,144,128]{2,1,0:T(8,128)(2,1)}), bf16[16,144,128]{2,1,0:T(8,128)(2,1)S(1)}, u32[]{:S(2)}, u32[]{:S(2)}) async-start(bf16[16,144,128]{2,1,0:T(8,128)(2,1)} %get-tuple-element.53), calls=%async_computation.1 | async-start | bytes 1179648 | tf_op jit(solution)/shard_map/all_to_all | solution.py:497
  37.2 10.4 %all-to-all-done.1.parts_ref = bf16[16,144,128]{2,1,0:T(8,128)(2,1)S(1)} async-done(((bf16[16,144,128]{2,1,0:T(8,128)(2,1)}), bf16[16,144,128]{2,1,0:T(8,128)(2,1)S(1)}, u32[]{:S(2)}, u32[]{:S(2)}) %all-to-all-start.1) | async-done | bytes 589856 | tf_op jit(solution)/shard_map/all_to_all | solution.py:497
  47.6 0.9 gradient.1
  49.8 3.6 %all-to-all-start.2 = ((bf16[16,144,128]{2,1,0:T(8,128)(2,1)}), bf16[16,144,128]{2,1,0:T(8,128)(2,1)S(1)}, u32[]{:S(2)}, u32[]{:S(2)}) async-start(bf16[16,144,128]{2,1,0:T(8,128)(2,1)} %get-tuple-element.54), calls=%async_computation.2 | async-start | bytes 1179648 | tf_op jit(solution)/shard_map/all_to_all | solution.py:497
  53.4 3.4 %copy-done.2 = bf16[2048,2048]{1,0:T(8,128)(2,1)S(1)} copy-done((bf16[2048,2048]{1,0:T(8,128)(2,1)S(1)}, bf16[2048,2048]{1,0:T(8,128)(2,1)}, u32[]{:S(2)}) %copy-start.2) | copy-done | bytes 8388632
  56.8 2.8 %turn.1.turned_ref = bf16[2048,2048]{1,0:T(8,128)(2,1)S(1)} custom-call(bf16[2048,2048]{1,0:T(8,128)(2,1)S(1)} %copy-done.2), custom_call_target="tpu_custom_call" | custom-call | flops 8388608 | bytes 8388608 | tf_op jit(solution)/shard_map/turn/pallas_call | solution.py:197
  59.6 3.3 %copy-done.5 = bf16[2048,2048]{1,0:T(8,128)(2,1)} copy-done((bf16[2048,2048]{1,0:T(8,128)(2,1)}, bf16[2048,2048]{1,0:T(8,128)(2,1)S(1)}, u32[]{:S(2)}) %copy-start.5) | copy-done | bytes 8388632
  62.9 1.0 all-to-all-done.2.values_ref
  63.8 3.4 %copy-done.6 = bf16[2048,2048]{1,0:T(8,128)(2,1)S(1)} copy-done((bf16[2048,2048]{1,0:T(8,128)(2,1)S(1)}, bf16[2048,2048]{1,0:T(8,128)(2,1)}, u32[]{:S(2)}) %copy-start.6) | copy-done | bytes 8388632
  67.2 1.5 backward.2
  68.8 2.0 collective-permute-done
  70.9 1.7 collective-permute-start.1
  72.6 2.2 collective-permute-start.3
  74.7 6.2 %all-to-all-start.3 = ((bf16[16,144,128]{2,1,0:T(8,128)(2,1)}), bf16[16,144,128]{2,1,0:T(8,128)(2,1)S(1)}, u32[]{:S(2)}, u32[]{:S(2)}) async-start(bf16[16,144,128]{2,1,0:T(8,128)(2,1)} %get-tuple-element.60), calls=%async_computation.3 | async-start | bytes 1179648 | tf_op jit(solution)/shard_map/all_to_all | solution.py:497
  80.9 1.1 add.44.one_ref
  82.0 2.3 %collective-permute-start.2 = (f32[144,512]{1,0:T(8,128)S(1)}, f32[144,512]{1,0:T(8,128)}, u32[]{:S(2)}, u32[]{:S(2)}) collective-permute-start(f32[144,512]{1,0:T(8,128)S(1)} %add.44.one_ref), channel_id=1, source_target_pairs={{0,96},{16,112},{32,64},{48,80},{64,32},{80,48},{96,0},{112,16},{1... | collective-permute-start | bytes 884744 | tf_op jit(solution)/shard_map/ppermute | solution.py:491
  84.3 1.8 add.46.two_ref
  86.6 0.8 copy-done.9
  87.4 0.8 copy-done.12
  89.0 3.9 %all-to-all-done.3.base_low_ref = bf16[16,144,128]{2,1,0:T(8,128)(2,1)S(1)} async-done(((bf16[16,144,128]{2,1,0:T(8,128)(2,1)}), bf16[16,144,128]{2,1,0:T(8,128)(2,1)S(1)}, u32[]{:S(2)}, u32[]{:S(2)}) %all-to-all-start.3) | async-done | bytes 589856 | tf_op jit(solution)/shard_map/all_to_all | solution.py:497
  92.9 1.4 collective-permute-done.4.two_in_ref
  94.3 1.0 copy-done.10
  95.4 1.0 copy-done.13
  96.4 1.0 copy-done.16
  97.5 1.9 residual.1
  100.0 1.1 collective-permute-done.6.other_part_ref
  101.1 3.4 %copy-done.3 = bf16[2048,2048]{1,0:T(8,128)(2,1)S(1)} copy-done((bf16[2048,2048]{1,0:T(8,128)(2,1)S(1)}, bf16[2048,2048]{1,0:T(8,128)(2,1)}, u32[]{:S(2)}) %copy-start.3) | copy-done | bytes 8388632
  104.5 2.2 forward.2
  106.7 19.3 %all_to_all.50.parts_ref = bf16[16,160,128]{2,1,0:T(8,128)(2,1)S(1)} all-to-all(bf16[16,160,128]{2,1,0:T(8,128)(2,1)S(1)} %get-tuple-element.69), channel_id=1, replica_groups=mesh['ex'=8,'ctr'=16] {'ctr'}, dimensions={0} | all-to-all | bytes 1310720 | tf_op jit(solution)/shard_map/all_to_all | solution.py:497
  126.1 0.9 copy-done.21
  127.1 15.6 %all_to_all.51.values_ref = bf16[16,160,128]{2,1,0:T(8,128)(2,1)S(1)} all-to-all(bf16[16,160,128]{2,1,0:T(8,128)(2,1)S(1)} %get-tuple-element.71), channel_id=1, replica_groups=mesh['ex'=8,'ctr'=16] {'ctr'}, dimensions={0} | all-to-all | bytes 1310720 | tf_op jit(solution)/shard_map/all_to_all | solution.py:497
  142.7 1.5 backward.3
  144.3 2.0 collective-permute-done.7
  147.5 1.8 collective-permute-start.10
  149.3 3.6 %all-to-all-start.6 = ((bf16[16,144,128]{2,1,0:T(8,128)(2,1)}), bf16[16,144,128]{2,1,0:T(8,128)(2,1)S(1)}, u32[]{:S(2)}, u32[]{:S(2)}) async-start(bf16[16,144,128]{2,1,0:T(8,128)(2,1)} %get-tuple-element.76), calls=%async_computation.6 | async-start | bytes 1179648 | tf_op jit(solution)/shard_map/all_to_all | solution.py:497
  152.9 3.1 %collective-permute-done.8 = f32[152,512]{1,0:T(8,128)} collective-permute-done((f32[152,512]{1,0:T(8,128)S(1)}, f32[152,512]{1,0:T(8,128)}, u32[]{:S(2)}, u32[]{:S(2)}) %collective-permute-start.8) | collective-permute-done | bytes 311328 | tf_op jit(solution)/shard_map/ppermute | solution.py:491
  156.0 1.1 add.48.one_ref
  157.1 1.9 collective-permute-start.9
  159.0 1.1 add.50.two_ref
  160.1 5.0 %all-to-all-done.6.image_low_ref = bf16[16,144,128]{2,1,0:T(8,128)(2,1)S(1)} async-done(((bf16[16,144,128]{2,1,0:T(8,128)(2,1)}), bf16[16,144,128]{2,1,0:T(8,128)(2,1)S(1)}, u32[]{:S(2)}, u32[]{:S(2)}) %all-to-all-start.6) | async-done | bytes 589856 | tf_op jit(solution)/shard_map/all_to_all | solution.py:497
  165.1 1.9 collective-permute-done.9.one_in_ref
  167.1 1.1 collective-permute-done.11.two_in_ref
  168.2 1.0 copy-done.17
  169.2 1.1 copy-done.19
  170.3 2.0 step.1
  172.9 1.1 collective-permute-done.13.other_part_ref
  174.0 3.4 %copy-done.4 = bf16[2048,2048]{1,0:T(8,128)(2,1)S(1)} copy-done((bf16[2048,2048]{1,0:T(8,128)(2,1)S(1)}, bf16[2048,2048]{1,0:T(8,128)(2,1)}, u32[]{:S(2)}) %copy-start.4) | copy-done | bytes 8388632
  177.4 2.3 forward.3
  179.6 16.8 %all_to_all.52.parts_ref = bf16[16,160,128]{2,1,0:T(8,128)(2,1)S(1)} all-to-all(bf16[16,160,128]{2,1,0:T(8,128)(2,1)S(1)} %get-tuple-element.83), channel_id=1, replica_groups=mesh['ex'=8,'ctr'=16] {'ctr'}, dimensions={0} | all-to-all | bytes 1310720 | tf_op jit(solution)/shard_map/all_to_all | solution.py:497
  196.8 3.6 %all-to-all-start.8 = ((bf16[16,144,128]{2,1,0:T(8,128)(2,1)}), bf16[16,144,128]{2,1,0:T(8,128)(2,1)S(1)}, u32[]{:S(2)}, u32[]{:S(2)}) async-start(bf16[16,144,128]{2,1,0:T(8,128)(2,1)} %get-tuple-element.89), calls=%async_computation.8 | async-start | bytes 1179648 | tf_op jit(solution)/shard_map/all_to_all | solution.py:497
  200.5 1.2 collective-permute-done.14
  202.1 3.1 %collective-permute-done.15 = f32[8,256]{1,0:T(8,128)S(1)} collective-permute-done((f32[8,256]{1,0:T(8,128)S(1)}, f32[8,256]{1,0:T(8,128)S(1)}, u32[]{:S(2)}, u32[]{:S(2)}) %collective-permute-start.15) | collective-permute-done | bytes 8224 | tf_op jit(solution)/shard_map/ppermute | solution.py:491
  205.3 1.8 collective-permute-start.16
  207.1 3.1 %collective-permute-done.16 = f32[8,256]{1,0:T(8,128)S(1)} collective-permute-done((f32[8,256]{1,0:T(8,128)S(1)}, f32[8,256]{1,0:T(8,128)S(1)}, u32[]{:S(2)}, u32[]{:S(2)}) %collective-permute-start.16) | collective-permute-done | bytes 8224 | tf_op jit(solution)/shard_map/ppermute | solution.py:491
  210.1 1.9 all-to-all-done.8.last_low_ref
  212.0 13.0 %all_to_all.53.curve_ref = f32[16,8,256]{2,1,0:T(8,128)S(1)} all-to-all(f32[16,8,256]{2,1,0:T(8,128)S(1)} %broadcast_in_dim.7), channel_id=1, replica_groups=mesh['ex'=8,'ctr'=16] {'ctr'}, dimensions={0} | all-to-all | bytes 262144 | tf_op jit(solution)/shard_map/all_to_all | solution.py:497
  225.0 1.0 margins.1
  (76 shorter events, 9.3 us)
Async XLA Ops:
  0.0 36.4 %copy-start = (s32[2048]{0:T(1024)S(1)}, s32[2048]{0:T(1024)}, u32[]{:S(2)}) copy-start(s32[2048]{0:T(1024)} %param.9) | copy-start | bytes 24580
  1.6 19.5 %all-to-all-start = ((bf16[16,64,256]{2,1,0:T(8,128)(2,1)}), bf16[16,64,256]{2,1,0:T(8,128)(2,1)S(1)}, u32[]{:S(2)}, u32[]{:S(2)}) async-start(bf16[16,64,256]{2,1,0:T(8,128)(2,1)} %broadcast_in_dim.6), calls=%async_computation | async-start | bytes 1048576 | tf_op jit(solution)/shard_map/all_to_all | solution.py:497
  9.6 1.0 copy-start.23
  10.6 0.7 copy-start.26
  21.1 0.7 copy-start.27
  21.8 1.1 copy-start.28
  29.5 3.3 %copy-start.1 = (bf16[2048,2048]{1,0:T(8,128)(2,1)}, bf16[2048,2048]{1,0:T(8,128)(2,1)S(1)}, u32[]{:S(2)}) copy-start(bf16[2048,2048]{1,0:T(8,128)(2,1)S(1)} %get-tuple-element.55.tile_ref) | copy-start | bytes 25165828
  32.8 14.8 %all-to-all-start.1 = ((bf16[16,144,128]{2,1,0:T(8,128)(2,1)}), bf16[16,144,128]{2,1,0:T(8,128)(2,1)S(1)}, u32[]{:S(2)}, u32[]{:S(2)}) async-start(bf16[16,144,128]{2,1,0:T(8,128)(2,1)} %get-tuple-element.53), calls=%async_computation.1 | async-start | bytes 1179648 | tf_op jit(solution)/shard_map/all_to_all | solution.py:497
  48.5 0.6 copy-start.20
  49.2 0.6 copy-start.24
  49.8 14.0 %all-to-all-start.2 = ((bf16[16,144,128]{2,1,0:T(8,128)(2,1)}), bf16[16,144,128]{2,1,0:T(8,128)(2,1)S(1)}, u32[]{:S(2)}, u32[]{:S(2)}) async-start(bf16[16,144,128]{2,1,0:T(8,128)(2,1)} %get-tuple-element.54), calls=%async_computation.2 | async-start | bytes 1179648 | tf_op jit(solution)/shard_map/all_to_all | solution.py:497
  53.4 3.4 %copy-start.2 = (bf16[2048,2048]{1,0:T(8,128)(2,1)S(1)}, bf16[2048,2048]{1,0:T(8,128)(2,1)}, u32[]{:S(2)}) copy-start(bf16[2048,2048]{1,0:T(8,128)(2,1)} %copy-done.1) | copy-start | bytes 25165828
  56.8 29.4 %copy-start.8 = (f32[2048,256]{1,0:T(8,128)S(1)}, f32[2048,256]{1,0:T(8,128)}, u32[]{:S(2)}) copy-start(f32[2048,256]{1,0:T(8,128)} %precond_ref.1) | copy-start | bytes 6291460
  59.6 3.3 %copy-start.5 = (bf16[2048,2048]{1,0:T(8,128)(2,1)}, bf16[2048,2048]{1,0:T(8,128)(2,1)S(1)}, u32[]{:S(2)}) copy-start(bf16[2048,2048]{1,0:T(8,128)(2,1)S(1)} %turn.1.turned_ref) | copy-start | bytes 25165828
  63.8 3.4 %copy-start.6 = (bf16[2048,2048]{1,0:T(8,128)(2,1)S(1)}, bf16[2048,2048]{1,0:T(8,128)(2,1)}, u32[]{:S(2)}) copy-start(bf16[2048,2048]{1,0:T(8,128)(2,1)} %copy-done.5) | copy-start | bytes 25165828
  68.7 2.1 collective-permute-start
  70.9 10.0 %copy-start.30 = (f32[144,512]{1,0:T(8,128)}, f32[144,512]{1,0:T(8,128)S(1)}, u32[]{:S(2)}) copy-start(f32[144,512]{1,0:T(8,128)S(1)} %get-tuple-element.59) | copy-start | bytes 884740
  70.9 10.0 %collective-permute-start.1 = (f32[144,512]{1,0:T(8,128)S(1)}, f32[144,512]{1,0:T(8,128)}, u32[]{:S(2)}, u32[]{:S(2)}) collective-permute-start(f32[144,512]{1,0:T(8,128)S(1)} %get-tuple-element.59), channel_id=1, source_target_pairs={{0,32},{16,48},{32,0},{48,16},{64,96},{80,112},{96,64},{112,80},{1... | collective-permute-start | bytes 884744 | tf_op jit(solution)/shard_map/ppermute | solution.py:491
  72.6 11.8 %collective-permute-start.3 = (f32[144,512]{1,0:T(8,128)S(1)}, f32[144,512]{1,0:T(8,128)}, u32[]{:S(2)}, u32[]{:S(2)}) collective-permute-start(f32[144,512]{1,0:T(8,128)S(1)} %get-tuple-element.97), channel_id=1, source_target_pairs={{0,96},{16,112},{32,64},{48,80},{64,32},{80,48},{96,0},{112,16},{1... | collective-permute-start | bytes 884744 | tf_op jit(solution)/shard_map/ppermute | solution.py:491
  74.7 18.2 %all-to-all-start.3 = ((bf16[16,144,128]{2,1,0:T(8,128)(2,1)}), bf16[16,144,128]{2,1,0:T(8,128)(2,1)S(1)}, u32[]{:S(2)}, u32[]{:S(2)}) async-start(bf16[16,144,128]{2,1,0:T(8,128)(2,1)} %get-tuple-element.60), calls=%async_computation.3 | async-start | bytes 1179648 | tf_op jit(solution)/shard_map/all_to_all | solution.py:497
  82.0 10.9 %collective-permute-start.2 = (f32[144,512]{1,0:T(8,128)S(1)}, f32[144,512]{1,0:T(8,128)}, u32[]{:S(2)}, u32[]{:S(2)}) collective-permute-start(f32[144,512]{1,0:T(8,128)S(1)} %add.44.one_ref), channel_id=1, source_target_pairs={{0,96},{16,112},{32,64},{48,80},{64,32},{80,48},{96,0},{112,16},{1... | collective-permute-start | bytes 884744 | tf_op jit(solution)/shard_map/ppermute | solution.py:491
  86.1 8.3 %collective-permute-start.4 = (f32[144,512]{1,0:T(8,128)}, f32[144,512]{1,0:T(8,128)}, u32[]{:S(2)}, u32[]{:S(2)}) collective-permute-start(f32[144,512]{1,0:T(8,128)} %add.46.two_ref), channel_id=1, source_target_pairs={{0,32},{16,48},{32,0},{48,16},{64,96},{80,112},{96,64},{112,80},{1... | collective-permute-start | bytes 884744 | tf_op jit(solution)/shard_map/ppermute | solution.py:491
  86.6 0.8 copy-start.9
  87.4 0.8 copy-start.12
  88.2 0.8 copy-start.15
  94.3 1.0 copy-start.10
  95.4 1.0 copy-start.13
  96.4 1.0 copy-start.16
  99.4 26.7 %copy-start.18 = (f32[144,1024]{1,0:T(8,128)}, f32[144,1024]{1,0:T(8,128)S(1)}, u32[]{:S(2)}) copy-start(f32[144,1024]{1,0:T(8,128)S(1)} %get-tuple-element.79.residual_ref) | copy-start | bytes 1769476
  99.4 1.7 collective-permute-start.5
  99.5 1.6 collective-permute-start.6
  101.1 3.4 %copy-start.3 = (bf16[2048,2048]{1,0:T(8,128)(2,1)S(1)}, bf16[2048,2048]{1,0:T(8,128)(2,1)}, u32[]{:S(2)}) copy-start(bf16[2048,2048]{1,0:T(8,128)(2,1)} %copy-done.1) | copy-start | bytes 25165828
  104.5 38.3 %copy-start.7 = (bf16[2048,2048]{1,0:T(8,128)(2,1)S(1)}, bf16[2048,2048]{1,0:T(8,128)(2,1)}, u32[]{:S(2)}) copy-start(bf16[2048,2048]{1,0:T(8,128)(2,1)} %copy-done.5) | copy-start | bytes 25165828
  106.7 61.5 %copy-start.11 = (bf16[1024,256]{1,0:T(8,128)(2,1)S(1)}, bf16[1024,256]{1,0:T(8,128)(2,1)}, u32[]{:S(2)}) copy-start(bf16[1024,256]{1,0:T(8,128)(2,1)} %copy-done.9) | copy-start | bytes 1572868
  106.7 61.5 %copy-start.14 = (bf16[1024,256]{1,0:T(8,128)(2,1)S(1)}, bf16[1024,256]{1,0:T(8,128)(2,1)}, u32[]{:S(2)}) copy-start(bf16[1024,256]{1,0:T(8,128)(2,1)} %copy-done.12) | copy-start | bytes 1572868
  126.1 0.9 copy-start.21
  144.2 2.1 collective-permute-start.7
  146.4 6.5 %copy-start.29 = (f32[152,512]{1,0:T(8,128)}, f32[152,512]{1,0:T(8,128)S(1)}, u32[]{:S(2)}) copy-start(f32[152,512]{1,0:T(8,128)S(1)} %slice_add_fusion) | copy-start | bytes 933892
  146.4 9.6 %collective-permute-start.8 = (f32[152,512]{1,0:T(8,128)S(1)}, f32[152,512]{1,0:T(8,128)}, u32[]{:S(2)}, u32[]{:S(2)}) collective-permute-start(f32[152,512]{1,0:T(8,128)S(1)} %slice_add_fusion), channel_id=1, source_target_pairs={{0,32},{16,48},{32,0},{48,16},{64,96},{80,112},{96,64},{112,80},{1... | collective-permute-start | bytes 933896 | tf_op jit(solution)/shard_map/ppermute | solution.py:491
  147.5 48.9 %copy-start.22 = (f32[144,128]{1,0:T(8,128)S(1)}, f32[144,128]{1,0:T(8,128)}, u32[]{:S(2)}) copy-start(f32[144,128]{1,0:T(8,128)} %copy-done.20) | copy-start | bytes 221188
  147.5 11.4 %collective-permute-start.10 = (f32[144,512]{1,0:T(8,128)}, f32[144,512]{1,0:T(8,128)}, u32[]{:S(2)}, u32[]{:S(2)}) collective-permute-start(f32[144,512]{1,0:T(8,128)} %slice_add_fusion.1), channel_id=1, source_target_pairs={{0,96},{16,112},{32,64},{48,80},{64,32},{80,48},{96,0},{112,16},{1... | collective-permute-start | bytes 884744 | tf_op jit(solution)/shard_map/ppermute | solution.py:491
  149.3 15.8 %all-to-all-start.6 = ((bf16[16,144,128]{2,1,0:T(8,128)(2,1)}), bf16[16,144,128]{2,1,0:T(8,128)(2,1)S(1)}, u32[]{:S(2)}, u32[]{:S(2)}) async-start(bf16[16,144,128]{2,1,0:T(8,128)(2,1)} %get-tuple-element.76), calls=%async_computation.6 | async-start | bytes 1179648 | tf_op jit(solution)/shard_map/all_to_all | solution.py:497
  157.1 10.0 %collective-permute-start.9 = (f32[152,512]{1,0:T(8,128)S(1)}, f32[152,512]{1,0:T(8,128)}, u32[]{:S(2)}, u32[]{:S(2)}) collective-permute-start(f32[152,512]{1,0:T(8,128)S(1)} %add.48.one_ref), channel_id=1, source_target_pairs={{0,96},{16,112},{32,64},{48,80},{64,32},{80,48},{96,0},{112,16},{1... | collective-permute-start | bytes 933896 | tf_op jit(solution)/shard_map/ppermute | solution.py:491
  160.1 8.1 %collective-permute-start.11 = (f32[144,512]{1,0:T(8,128)S(1)}, f32[144,512]{1,0:T(8,128)}, u32[]{:S(2)}, u32[]{:S(2)}) collective-permute-start(f32[144,512]{1,0:T(8,128)S(1)} %add.50.two_ref), channel_id=1, source_target_pairs={{0,32},{16,48},{32,0},{48,16},{64,96},{80,112},{96,64},{112,80},{1... | collective-permute-start | bytes 884744 | tf_op jit(solution)/shard_map/ppermute | solution.py:491
  168.2 1.0 copy-start.17
  169.2 1.1 copy-start.19
  172.3 1.7 collective-permute-start.12
  172.4 1.6 collective-permute-start.13
  174.0 3.4 %copy-start.4 = (bf16[2048,2048]{1,0:T(8,128)(2,1)S(1)}, bf16[2048,2048]{1,0:T(8,128)(2,1)}, u32[]{:S(2)}) copy-start(bf16[2048,2048]{1,0:T(8,128)(2,1)} %copy-done.1) | copy-start | bytes 25165828
  177.4 47.7 %copy-start.25 = (f32[144,128]{1,0:T(8,128)S(1)}, f32[144,128]{1,0:T(8,128)}, u32[]{:S(2)}) copy-start(f32[144,128]{1,0:T(8,128)} %copy-done.24) | copy-start | bytes 221188
  196.8 15.3 %all-to-all-start.8 = ((bf16[16,144,128]{2,1,0:T(8,128)(2,1)}), bf16[16,144,128]{2,1,0:T(8,128)(2,1)S(1)}, u32[]{:S(2)}, u32[]{:S(2)}) async-start(bf16[16,144,128]{2,1,0:T(8,128)(2,1)} %get-tuple-element.89), calls=%async_computation.8 | async-start | bytes 1179648 | tf_op jit(solution)/shard_map/all_to_all | solution.py:497
  200.4 1.3 collective-permute-start.14
  201.6 3.7 %collective-permute-start.15 = (f32[8,256]{1,0:T(8,128)S(1)}, f32[8,256]{1,0:T(8,128)S(1)}, u32[]{:S(2)}, u32[]{:S(2)}) collective-permute-start(f32[8,256]{1,0:T(8,128)S(1)} %add.51), channel_id=1, source_target_pairs={{0,32},{16,48},{32,0},{48,16},{64,96},{80,112},{96,64},{112,80},{1... | collective-permute-start | bytes 24584 | tf_op jit(solution)/shard_map/ppermute | solution.py:491
  205.3 4.9 %collective-permute-start.16 = (f32[8,256]{1,0:T(8,128)S(1)}, f32[8,256]{1,0:T(8,128)S(1)}, u32[]{:S(2)}, u32[]{:S(2)}) collective-permute-start(f32[8,256]{1,0:T(8,128)S(1)} %add.52), channel_id=1, source_target_pairs={{0,96},{16,112},{32,64},{48,80},{64,32},{80,48},{96,0},{112,16},{1... | collective-permute-start | bytes 24584 | tf_op jit(solution)/shard_map/ppermute | solution.py:491

commit v3 on v2

--- a/solution.py
+++ b/solution.py
@@ -10,6 +10,7 @@
 
 RIDGE = 0.0001
 F32 = jnp.float32
+F16 = jnp.float16
 BF16 = jnp.bfloat16
 VMEM_BYTES = 24 * 1024 * 1024
 DEPTH = 128
@@ -64,6 +65,43 @@
     return jnp.concatenate(halves, axis=1)
 
 
+def exponents(bounds):
+    return jnp.ceil(jnp.log2(jnp.maximum(bounds, 1e-30)))
+
+
+def half_rows(powers, vectors):
+    row = lax.broadcasted_iota(jnp.int32, (EXTRA, LANES), 0)
+    pieces = [powers]
+    for vector in vectors:
+        power = exponents(jnp.abs(vector)) + 1.0
+        scaled = vector * jnp.exp2(-power) * 2048.0
+        high = jnp.floor(scaled + 0.5)
+        pieces += [power, high / 2048.0, jnp.floor((scaled - high) * 2048.0 + 0.5) / 2048.0]
+    out = jnp.zeros((EXTRA, LANES), F32)
+    for p, piece in enumerate(pieces):
+        for q in range(2):
+            out = jnp.where(row == 2 * p + q, piece[:, q * LANES : (q + 1) * LANES], out)
+    return out
+
+
+def half_row(parts_ref, first, p):
+    rows = [parts_ref[:, first + 2 * p + q, :] for q in range(2)]
+    return jnp.concatenate(rows, axis=1)
+
+
+def half_vector(parts_ref, first, k):
+    power, high, low = (half_row(parts_ref, first, 1 + 3 * k + p) for p in range(3))
+    return jnp.sum(jnp.exp2(power) * (high + low / 2048.0), axis=0, keepdims=True)
+
+
+def sum_scaled(parts_ref, classes):
+    scales = jnp.exp2(half_row(parts_ref, classes, 0)).T
+    total = parts_ref[0, :classes] * scales[:classes, :1]
+    for k in range(1, parts_ref.shape[0]):
+        total = total + parts_ref[k, :classes] * scales[:classes, k : k + 1]
+    return total
+
+
 def column(vector, classes):
     return jnp.broadcast_to(vector, (8, vector.shape[1])).T[:classes, :1]
 
@@ -114,27 +152,28 @@
     one_hot_ref[...] = (row == within).astype(F32).astype(BF16)
 
 
-def prepare(indices, centers, lanes):
+def prepare(index, centers, lanes):
     features, count = centers.shape
-    examples = indices.shape[0]
+    examples = index.shape[1]
     return call(
         prepare_kernel,
         "prepare",
         [shape((count, DEPTH), BF16), shape((lanes, examples), BF16)],
         1 << 20,
         arrays=2,
-    )(indices.reshape(1, examples), centers)
-
-
-def tile_kernel(index_ref, pool_ref, one_hot_ref, sides_ref, alpha_ref, tile_ref, high_ref, low_ref, side_ref):
+    )(index, centers)
+
+
+def tile_kernel(
+    index_ref, pool_ref, one_hot_ref, sides_ref, alpha_ref, tile_ref, turned_ref, rows_ref, side_ref
+):
     chunks, features, lanes = pool_ref.shape
     count, examples = tile_ref.shape
-    share = high_ref.shape[2]
+    share = rows_ref.shape[2]
     scale = 4.0 / features * math.log2(math.e)
     pool = pool_ref[...].reshape(chunks * features, lanes)
-
-    def gather(b, carry):
-        here = pl.ds(pl.multiple_of(b * BAND, BAND), BAND)
+    for b in range(examples // BAND):
+        here = slice(b * BAND, (b + 1) * BAND)
         chunk = index_ref[:, here] // lanes
         picked = jnp.dot(pool, one_hot_ref[:, here], preferred_element_type=F32)
         points = jnp.where(chunk == 0, picked[:features], 0.0)
@@ -143,58 +182,34 @@
         point_sq = jnp.sum(points * points, axis=0, keepdims=True)
         side = jnp.concatenate([points, tail(point_sq, 0, DEPTH - features)], axis=0)
         side_ref[:, here] = side.astype(BF16)
-        return carry
-
-    lax.fori_loop(0, examples // BAND, gather, 0, unroll=True)
-
-    def fill(b, carry):
-        rows = pl.ds(pl.multiple_of(b * BAND, BAND), BAND)
-        near = jnp.dot(sides_ref[rows, :], side_ref[...], preferred_element_type=F32)
-        tile_ref[rows, :] = jnp.exp2(near * scale).astype(BF16)
-        return carry
-
-    lax.fori_loop(0, count // BAND, fill, 0, unroll=2)
-
-    def product(b, carry):
-        here = pl.ds(pl.multiple_of(b * BAND, BAND), BAND)
+    for b in range(count // BAND):
+        here = slice(b * BAND, (b + 1) * BAND)
+        near = jnp.dot(sides_ref[here, :], side_ref[...], preferred_element_type=F32)
+        values = jnp.exp2(near * scale).astype(BF16)
+        tile_ref[here, :] = values
+        turned_ref[:, here] = values.T
+    for b in range(examples // BAND):
+        here = slice(b * BAND, (b + 1) * BAND)
         rows = jnp.dot(alpha_ref[...], tile_ref[:, here], preferred_element_type=F32)
         for k in range(BAND // share):
-            piece = rows[:, k * share : (k + 1) * share]
-            high = piece.astype(BF16)
-            high_ref[b * (BAND // share) + k] = high
-            low_ref[b * (BAND // share) + k] = (piece - high.astype(F32)).astype(BF16)
-        return carry
-
-    lax.fori_loop(0, examples // BAND, product, 0, unroll=True)
-
-
-def make_tile(indices, row_pool, one_hot, sides, alpha, share):
-    examples, count = indices.shape[0], sides.shape[0]
+            rows_ref[b * (BAND // share) + k] = rows[:, k * share : (k + 1) * share]
+
+
+def make_tile(index, row_pool, one_hot, sides, alpha, share):
+    examples, count = index.shape[1], sides.shape[0]
     classes = alpha.shape[0]
-    parts = shape((examples // share, classes, share), BF16)
     return call(
         tile_kernel,
         "tile",
-        [shape((count, examples), BF16), parts, parts],
+        [
+            shape((count, examples), BF16),
+            shape((examples, count), BF16),
+            shape((examples // share, classes, share), F32),
+        ],
         4 << 30,
         [pltpu.VMEM((DEPTH, examples), BF16)],
         arrays=5,
-    )(indices.reshape(1, examples), row_pool, one_hot, sides, alpha)
-
-
-def turn_kernel(tile_ref, turned_ref):
-    count, examples = tile_ref.shape
-
-    def band(b, carry):
-        start = pl.multiple_of(b * BAND, BAND)
-        turned_ref[:, pl.ds(start, BAND)] = tile_ref[pl.ds(start, BAND), :].T
-        return carry
-
-    lax.fori_loop(0, count // BAND, band, 0)
-
-
-def turn(tile):
-    return call(turn_kernel, "turn", shape(tile.shape[::-1], BF16), 8 << 20, arrays=1)(tile)
+    )(index, row_pool, one_hot, sides, alpha)
 
 
 def factors_kernel(core_ref, precond_ref, high_ref, low_ref, high_turned_ref, low_turned_ref):
@@ -234,26 +249,26 @@
 
 
 def forward_kernel(
-    core_ref, own_ref, other_ref, own_part_ref, other_part_ref, tile_ref, high_ref, low_ref
+    core_ref, own_ref, other_ref, own_part_ref, other_part_ref, tile_ref, rows_ref
 ):
     classes, half = own_ref.shape
-    share = high_ref.shape[2]
+    share = rows_ref.shape[2]
     examples = tile_ref.shape[1]
     mine = pl.ds(pl.multiple_of(core_ref[0] * half, half), half)
     theirs = pl.ds(pl.multiple_of((1 - core_ref[0]) * half, half), half)
     part = own_part_ref[...] + other_part_ref[...]
-    extra = rows_of([part[:1], part[1:2]])
+    powers = exponents(part[2:3]) - 14.0
+    extra = half_rows(powers, [part[:1], part[1:2]])
+    scales = column(jnp.exp2(-powers), classes)
     for b in range(examples // BAND):
         here = slice(b * BAND, (b + 1) * BAND)
         rows = jnp.dot(own_ref[...], tile_ref[mine, here], preferred_element_type=F32)
         rows += jnp.dot(other_ref[...], tile_ref[theirs, here], preferred_element_type=F32)
+        rows *= scales
         for k in range(BAND // share):
-            piece = rows[:, k * share : (k + 1) * share]
-            high = piece.astype(BF16)
             at = b * (BAND // share) + k
-            high_ref[at, :classes] = high
-            high_ref[at, classes:] = extra
-            low_ref[at] = (piece - high.astype(F32)).astype(BF16)
+            rows_ref[at, :classes] = rows[:, k * share : (k + 1) * share]
+            rows_ref[at, classes:] = extra
 
 
 def forward(core, own, other, own_part, other_part, tile, share):
@@ -262,7 +277,7 @@
     return call(
         forward_kernel,
         "forward",
-        [shape((shares, classes + EXTRA, share), BF16), shape((shares, classes, share), BF16)],
+        shape((shares, classes + EXTRA, share), F32),
         1208 << 20,
         scalars=1,
         arrays=5,
@@ -312,10 +327,9 @@
     )(core, values, turned)
 
 
-def gradient_kernel(parts_ref, label_ref, weight_ref, base_ref, hessian_ref, send_ref):
+def gradient_kernel(base_ref, label_ref, weight_ref, hessian_ref, send_ref):
     classes, share = base_ref.shape
-    base = sum_parts(parts_ref)
-    base_ref[...] = base
+    base = base_ref[...]
     probability = jax.nn.sigmoid(base)
     row = lax.broadcasted_iota(jnp.int32, (classes, share), 0)
     target = jnp.where(row == label_ref[...], 1.0, 0.0)
@@ -325,11 +339,14 @@
         send_ref[k] = gradient
 
 
-def gradient(parts, label, weight):
-    block = shape(parts.shape[1:], F32)
-    return call(
-        gradient_kernel, "gradient", [block, block, shape(parts.shape, BF16)], 1 << 20, arrays=3
-    )(parts, label, weight)
+def gradient(base, label, weight, shares):
+    return call(
+        gradient_kernel,
+        "gradient",
+        [shape(base.shape, F32), shape((shares,) + base.shape, BF16)],
+        1 << 20,
+        arrays=3,
+    )(base, label, weight)
 
 
 def residual_kernel(
@@ -339,8 +356,12 @@
     sums = jnp.concatenate([one_ref[...] + one_in_ref[...], two_ref[...] + two_in_ref[...]], axis=1)
     residual = block_products(sums, high_ref, low_ref) * (-1.0 / total)
     residual_ref[...] = residual
-    lifted_ref[...] = block_products(residual, high_turned_ref, low_turned_ref).astype(BF16)
-    part_ref[...] = stack_rows([lane_sums(residual * residual)])
+    lifted = block_products(residual, high_turned_ref, low_turned_ref).astype(BF16)
+    lifted_ref[...] = lifted
+    zero = jnp.zeros((1, 2 * LANES), F32)
+    part_ref[...] = stack_rows(
+        [lane_sums(residual * residual), zero, lane_sums(jnp.abs(lifted.astype(F32)))]
+    )
 
 
 def first_residual(total, sums, blocks):
@@ -360,10 +381,9 @@
 
 def weigh_kernel(parts_ref, hessian_ref, image_ref, norm_ref, send_ref):
     classes = hessian_ref.shape[0]
-    total = sum_parts(parts_ref)
-    image = total[:classes]
+    image = sum_scaled(parts_ref, classes)
     image_ref[...] = image
-    norm_ref[...] = stack_rows([read_rows(total[classes:], 0)])
+    norm_ref[...] = stack_rows([half_vector(parts_ref, classes, 0)])
     weighted = (hessian_ref[...] * image).astype(BF16)
     extra = rows_of([lane_sums(weighted.astype(F32) * image)])
     for k in range(send_ref.shape[0]):
@@ -396,8 +416,11 @@
     old = residual_ref[...]
     image = block_products(sums, high_ref, low_ref) / total + RIDGE * old
     new = old - column(rough, classes) * image
-    lifted_ref[...] = block_products(new, high_turned_ref, low_turned_ref).astype(BF16)
-    part_ref[...] = stack_rows([lane_sums(old * new), lane_sums(new * new)])
+    lifted = block_products(new, high_turned_ref, low_turned_ref).astype(BF16)
+    lifted_ref[...] = lifted
+    part_ref[...] = stack_rows(
+        [lane_sums(old * new), lane_sums(new * new), lane_sums(jnp.abs(lifted.astype(F32)))]
+    )
 
 
 def step(total, sums, blocks, residual, norm):
@@ -415,11 +438,10 @@
     parts_ref, hessian_ref, image_ref, norm_ref, rough_ref, last_ref, scales_ref, curve_ref
 ):
     classes = hessian_ref.shape[0]
-    total = sum_parts(parts_ref)
-    last = total[:classes]
+    last = sum_scaled(parts_ref, classes)
     last_ref[...] = last
-    cross = read_rows(total[classes:], 0)
-    norm_rough = read_rows(total[classes:], 1)
+    cross = half_vector(parts_ref, classes, 0)
+    norm_rough = half_vector(parts_ref, classes, 1)
     norm = norm_ref[:1]
     lane = lax.broadcasted_iota(jnp.int32, (1, 2 * LANES), 1)
     excess = jnp.where(lane < classes, cross / (norm - cross), 0.0)
@@ -446,10 +468,7 @@
     )(parts, hessian, image, norm, rough)
 
 
-def margins_kernel(
-    total, curve_ref, scales_ref, base_ref, base_low_ref, image_ref, image_low_ref, last_ref,
-    last_low_ref, margins_ref,
-):
+def margins_kernel(total, curve_ref, scales_ref, base_ref, image_ref, last_ref, margins_ref):
     classes = base_ref.shape[0]
     curve = jnp.sum(curve_ref[:, 0], axis=0, keepdims=True)
     first, grown, other = scales_ref[0:1], scales_ref[1:2], scales_ref[2:3]
@@ -457,24 +476,17 @@
     second = jnp.where(
         lane < classes, scales_ref[3:4] / (curve / total + scales_ref[4:5]), 0.0
     )
-    base = base_ref[...] + sum_parts(base_low_ref)
-    image = image_ref[...] + sum_parts(image_low_ref)
-    last = last_ref[...] + sum_parts(last_low_ref)
     margins_ref[...] = (
-        base
-        + column(first + second * other, classes) * image
-        + column(second * grown, classes) * last
-    )
-
-
-def margins(total, curve, scales, base, base_low, image, image_low, last, last_low):
-    return call(
-        functools.partial(margins_kernel, total),
-        "margins",
-        shape(base.shape, F32),
-        1 << 20,
-        arrays=8,
-    )(curve, scales, base, base_low, image, image_low, last, last_low)
+        base_ref[...]
+        + column(first + second * other, classes) * image_ref[...]
+        + column(second * grown, classes) * last_ref[...]
+    )
+
+
+def margins(total, curve, scales, base, image, last):
+    return call(
+        functools.partial(margins_kernel, total), "margins", shape(base.shape, F32), 1 << 20, arrays=5
+    )(curve, scales, base, image, last)
 
 
 def shards(pool, indices, labels, example_weight, centers, alpha, precond):
@@ -496,55 +508,48 @@
     def trade(parts):
         return lax.all_to_all(parts, "ctr", 0, 0)
 
-    def tie(first, second):
-        return lax.optimization_barrier((first, second))
-
-    def sum_examples(products, low):
+    def trade_halves(parts):
+        return trade(parts.astype(F16)).astype(F32)
+
+    def sum_examples(products):
         other, one, two = products
         got = over_cores(other)
         wide = one.shape[1]
         one = one + got[:, :wide]
         two = two + got[:classes, wide:]
-        one, low = tie(one, low)
-        low = trade(low)
         one = one + over_y(one, 1)
         two = two + over_y(two, 3)
-        one_in, two_in = over_y(one, 3), over_y(two, 1)
-        one_in, low = tie(one_in, low)
-        return (one, one_in, two, two_in), low
+        return one, over_y(one, 3), two, over_y(two, 1)
 
     offset = lax.axis_index("ctr") * share
     label = lax.dynamic_slice_in_dim(labels, offset, share, 0).reshape(1, share)
     weight = lax.dynamic_slice_in_dim(example_weight, offset, share, 0).reshape(1, share)
-
+    index = indices.reshape(1, examples)
+    sides, one_hot = prepare(index, centers, pool.shape[1])
+    blocks = factors(core, precond)
     row_pool = trade(jnp.broadcast_to(pool, (n_ctr,) + pool.shape))
-    sides, one_hot = prepare(indices, centers, pool.shape[1])
-    tile, base_high, base_low = make_tile(indices, row_pool, one_hot, sides, alpha, share)
-    base_parts = trade(base_high)
-    turned = turn(tile)
-    blocks = factors(core, precond)
-    base, hessian, send = gradient(base_parts, label, weight)
-
-    sums, base_low = sum_examples(backward(core, trade(send), turned, classes), base_low)
+    row_pool, sides, one_hot, index, label, weight, core, *blocks = lax.optimization_barrier(
+        (row_pool, sides, one_hot, index, label, weight, core, *blocks)
+    )
+    tile, turned, rows = make_tile(index, row_pool, one_hot, sides, alpha, share)
+    base = jnp.sum(trade_halves(rows), axis=0)
+    hessian, send = gradient(base, label, weight, n_ctr)
+
+    sums = sum_examples(backward(core, trade(send), turned, classes))
     residual, lifted, part = first_residual(total, sums, blocks)
-    high, image_low = forward(
-        core, lifted, over_cores(lifted), part, over_cores(part), tile, share
-    )
-    image, norm, send = weigh(trade(high), hessian)
-
-    sums, image_low = sum_examples(backward(core, trade(send), turned, classes), image_low)
+    rows = forward(core, lifted, over_cores(lifted), part, over_cores(part), tile, share)
+    image, norm, send = weigh(trade_halves(rows), hessian)
+
+    sums = sum_examples(backward(core, trade(send), turned, classes))
     lifted, part, rough = step(total, sums, blocks, residual, norm)
-    high, last_low = forward(core, lifted, over_cores(lifted), part, over_cores(part), tile, share)
-    last, scales, curve = last_curve(trade(high), hessian, image, norm, rough)
-
-    curve, last_low = tie(curve, last_low)
-    last_low = trade(last_low)
+    rows = forward(core, lifted, over_cores(lifted), part, over_cores(part), tile, share)
+    last, scales, curve = last_curve(trade_halves(rows), hessian, image, norm, rough)
+
     curve = curve + over_cores(curve)
     curve = curve + over_y(curve, 1)
     curve = curve + over_y(curve, 3)
-    curve, last_low = tie(curve, last_low)
     curve = trade(jnp.broadcast_to(curve, (n_ctr,) + curve.shape))
-    return margins(total, curve, scales, base, base_low, image, image_low, last, last_low)
+    return margins(total, curve, scales, base, image, last)
 
 
 def solution(mesh):

time: 228 us -> 186 us (0.82)
  local copies, waits for them, and re-layouts: 35.8 us -> 8.12 us
  blocking collectives: 64.7 us -> 87.4 us
  starting transfers between devices: 42.6 us -> 21.6 us
  Pallas kernels: 24.2 us -> 16.7 us
  other arithmetic: 5.96 us -> 0.97 us
    unnamed x62 -> x18, local copies, waits for them, and re-layouts: 33.3 us -> 5.63 us
    all_to_all x6 -> x1, waiting for transfers between devices: 31.3 us -> 6.27 us  [trade(): return lax.all_to_all(parts, 'ctr', 0, 0)]
    ppermute x10, waiting for transfers between devices: 13.8 us -> 36.9 us  [over_y(): return lax.ppermute(array, 'ex', pairs)]
    all_to_all x4 -> x6, blocking collectives: 64.7 us -> 87.4 us  [trade(): return lax.all_to_all(parts, 'ctr', 0, 0)]
    all_to_all x6 -> x1, starting transfers between devices: 28.5 us -> 8.1 us  [trade(): return lax.all_to_all(parts, 'ctr', 0, 0)]
    pallas_call x5 -> x4, Pallas kernels: 14.8 us -> 8.49 us  [the longest x1 5.54 us: make_tile(): call(tile_kernel, 'tile', [shape((count, examples), BF16), shape((example...]
    add x2, other arithmetic: 2.86 us -> 0.08 us  [sum_examples(): two = two + over_y(two, 3)]
  transfers between devices with their start and end apart: 23 -> 18, of which waited for: 17 -> 14; matrix products, arithmetic and copies ran while one was open for 3% -> 1% of each run, Pallas kernels for 2% -> 1%
where the time goes in v3:
time: 186 us
  blocking collectives  87.4 us (47%)
  waiting for transfers between devices  50.5 us (27%)
  starting transfers between devices  21.6 us (12%)
  Pallas kernels  16.7 us (9%)
  local copies, waits for them, and re-layouts  8.12 us (4%)
    all_to_all x6, blocking collectives, trade(): return lax.all_to_all(parts, 'ctr', 0, 0)  87.4 us
    ppermute x10, waiting for transfers between devices, over_y(): return lax.ppermute(array, 'ex', pairs)  36.9 us
    ppermute x10, starting transfers between devices, over_y(): return lax.ppermute(array, 'ex', pairs)  12.1 us
    all_to_all x1, starting transfers between devices, trade(): return lax.all_to_all(parts, 'ctr', 0, 0)  8.1 us
    ppermute x7, waiting for transfers between devices, over_cores(): return lax.ppermute(array, 'ex', core_pairs)  7.36 us
    all_to_all x1, waiting for transfers between devices, trade(): return lax.all_to_all(parts, 'ctr', 0, 0)  6.27 us
    unnamed x18, local copies, waits for them, and re-layouts  5.63 us
    pallas_call x1, Pallas kernels, make_tile(): call(tile_kernel, 'tile', [shape((count, examples), BF16), shape((example...  5.54 us
  transfers between devices with their start and end apart: 18, of which 14 were waited for; matrix products, arithmetic and copies ran while one was open for 1% of the time, Pallas kernels for 1%

profile of v3, /device:TPU:0, one launch (start us, length us, event | category | flops | bytes accessed | tf_op | source)
XLA Modules:
  0.0 185.5 jit_solution(8810359542669896067)
XLA Ops:
  0.0 1.6 broadcast_in_dim.6
  1.6 8.1 %all-to-all-start = ((bf16[16,64,256]{2,1,0:T(8,128)(2,1)}), bf16[16,64,256]{2,1,0:T(8,128)(2,1)S(1)}, u32[]{:S(2)}, u32[]{:S(2)}) async-start(bf16[16,64,256]{2,1,0:T(8,128)(2,1)} %broadcast_in_dim.6), calls=%async_computation | async-start | bytes 1048576 | tf_op jit(solution)/shard_map/all_to_all | solution.py:509
  9.8 0.7 prepare.1
  10.5 1.0 copy-done.4
  11.4 0.8 copy-done.7
  12.2 1.6 copy-done.1
  13.8 0.3 factors.1
  14.2 0.1 dynamic-slice_bitcast_fusion.1.label_ref
  14.3 0.8 dynamic-slice_bitcast_fusion.weight_ref
  15.0 6.3 %all-to-all-done.pool_ref = bf16[16,64,256]{2,1,0:T(8,128)(2,1)S(1)} async-done(((bf16[16,64,256]{2,1,0:T(8,128)(2,1)}), bf16[16,64,256]{2,1,0:T(8,128)(2,1)S(1)}, u32[]{:S(2)}, u32[]{:S(2)}) %all-to-all-start) | async-done | bytes 524320 | tf_op jit(solution)/shard_map/all_to_all | solution.py:509
  21.3 1.2 copy-done.5
  22.5 1.0 copy-done.8
  23.6 5.5 %tile.1 = (bf16[2048,2048]{1,0:T(8,128)(2,1)S(1)}, bf16[2048,2048]{1,0:T(8,128)(2,1)S(1)}, f32[16,144,128]{2,1,0:T(8,128)S(1)}) custom-call(s32[1,2048]{1,0:T(1,128)S(1)} %bitcast.7, bf16[16,64,256]{2,1,0:T(8,128)(2,1)S(1)} %all-to-all-done.pool_ref, bf16[256,2048]{1,0:T(8,128)(2,1)S(1)} %copy-done.5, bf16[2048,128]{1,0:T(8,128)(2,1)S(1)} %copy-done.8, ...), custom_call_target="tpu_custom_call" | custom-call | flops 4294967296 | bytes 17956864 | tf_op jit(solution)/shard_map/tile/pallas_call | solution.py:201
  29.2 14.4 %all_to_all.35 = f16[16,144,128]{2,1,0:T(8,128)(2,1)S(1)} all-to-all(f16[16,144,128]{2,1,0:T(8,128)(2,1)S(1)} %convert_element_type.18), channel_id=1, replica_groups=mesh['ex'=8,'ctr'=16] {'ctr'}, dimensions={0} | all-to-all | bytes 1179648 | tf_op jit(solution)/shard_map/all_to_all | solution.py:509
  43.6 0.1 convert_reduce_fusion.base_ref
  43.8 13.7 %all_to_all.36.values_ref = bf16[16,144,128]{2,1,0:T(8,128)(2,1)S(1)} all-to-all(bf16[16,144,128]{2,1,0:T(8,128)(2,1)S(1)} %get-tuple-element.59), channel_id=1, replica_groups=mesh['ex'=8,'ctr'=16] {'ctr'}, dimensions={0} | all-to-all | bytes 1179648 | tf_op jit(solution)/shard_map/all_to_all | solution.py:509
  57.4 1.5 backward.2
  58.9 0.1 collective-permute-start
  59.0 2.0 %collective-permute-done = f32[144,1024]{1,0:T(8,128)S(1)} collective-permute-done((f32[144,1024]{1,0:T(8,128)S(1)}, f32[144,1024]{1,0:T(8,128)S(1)}, u32[]{:S(2)}, u32[]{:S(2)}) %collective-permute-start) | collective-permute-done | bytes 589856 | tf_op jit(solution)/shard_map/ppermute | solution.py:506
  61.0 0.1 slice_add_fusion.2
  61.1 3.1 %collective-permute-start.3 = (f32[144,512]{1,0:T(8,128)S(1)}, f32[144,512]{1,0:T(8,128)S(1)}, u32[]{:S(2)}, u32[]{:S(2)}) collective-permute-start(f32[144,512]{1,0:T(8,128)S(1)} %get-tuple-element.85), channel_id=1, source_target_pairs={{0,96},{16,112},{32,64},{48,80},{64,32},{80,48},{96,0},{112,16},{1... | collective-permute-start | bytes 884744 | tf_op jit(solution)/shard_map/ppermute | solution.py:503
  64.2 0.1 collective-permute-start.1
  64.3 7.2 %collective-permute-done.3 = f32[144,512]{1,0:T(8,128)S(1)} collective-permute-done((f32[144,512]{1,0:T(8,128)S(1)}, f32[144,512]{1,0:T(8,128)S(1)}, u32[]{:S(2)}, u32[]{:S(2)}) %collective-permute-start.3) | collective-permute-done | bytes 294944 | tf_op jit(solution)/shard_map/ppermute | solution.py:503
  71.5 0.4 collective-permute-start.4
  71.9 1.0 collective-permute-done.1
  73.0 1.7 collective-permute-start.2
  74.7 5.2 %collective-permute-done.4.two_in_ref = f32[144,512]{1,0:T(8,128)S(1)} collective-permute-done((f32[144,512]{1,0:T(8,128)S(1)}, f32[144,512]{1,0:T(8,128)S(1)}, u32[]{:S(2)}, u32[]{:S(2)}) %collective-permute-start.4) | collective-permute-done | bytes 294944 | tf_op jit(solution)/shard_map/ppermute | solution.py:503
  79.9 2.3 %collective-permute-done.2.one_in_ref = f32[144,512]{1,0:T(8,128)S(1)} collective-permute-done((f32[144,512]{1,0:T(8,128)S(1)}, f32[144,512]{1,0:T(8,128)S(1)}, u32[]{:S(2)}, u32[]{:S(2)}) %collective-permute-start.2) | collective-permute-done | bytes 294944 | tf_op jit(solution)/shard_map/ppermute | solution.py:503
  82.2 0.9 residual.1
  83.1 0.1 collective-permute-start.5
  83.2 0.5 collective-permute-start.6
  83.7 1.1 collective-permute-done.6.other_part_ref
  84.7 1.4 forward.2
  86.2 0.1 convert_element_type.20
  86.3 16.3 %all_to_all.37 = f16[16,160,128]{2,1,0:T(8,128)(2,1)S(1)} all-to-all(f16[16,160,128]{2,1,0:T(8,128)(2,1)S(1)} %convert_element_type.20), channel_id=1, replica_groups=mesh['ex'=8,'ctr'=16] {'ctr'}, dimensions={0} | all-to-all | bytes 1310720 | tf_op jit(solution)/shard_map/all_to_all | solution.py:509
  102.6 0.1 convert_element_type.21.parts_ref
  102.8 0.7 weigh.1
  103.5 15.6 %all_to_all.38.values_ref = bf16[16,160,128]{2,1,0:T(8,128)(2,1)S(1)} all-to-all(bf16[16,160,128]{2,1,0:T(8,128)(2,1)S(1)} %get-tuple-element.72), channel_id=1, replica_groups=mesh['ex'=8,'ctr'=16] {'ctr'}, dimensions={0} | all-to-all | bytes 1310720 | tf_op jit(solution)/shard_map/all_to_all | solution.py:509
  119.0 1.5 backward.3
  120.5 0.1 collective-permute-start.7
  120.6 2.0 %collective-permute-done.7 = f32[152,1024]{1,0:T(8,128)S(1)} collective-permute-done((f32[152,1024]{1,0:T(8,128)S(1)}, f32[152,1024]{1,0:T(8,128)S(1)}, u32[]{:S(2)}, u32[]{:S(2)}) %collective-permute-start.7) | collective-permute-done | bytes 622624 | tf_op jit(solution)/shard_map/ppermute | solution.py:506
  122.7 0.2 collective-permute-start.8
  123.0 2.4 %collective-permute-start.10 = (f32[144,512]{1,0:T(8,128)S(1)}, f32[144,512]{1,0:T(8,128)S(1)}, u32[]{:S(2)}, u32[]{:S(2)}) collective-permute-start(f32[144,512]{1,0:T(8,128)S(1)} %slice_add_fusion.1), channel_id=1, source_target_pairs={{0,96},{16,112},{32,64},{48,80},{64,32},{80,48},{96,0},{112,16},{1... | collective-permute-start | bytes 884744 | tf_op jit(solution)/shard_map/ppermute | solution.py:503
  125.4 6.8 %collective-permute-done.8 = f32[152,512]{1,0:T(8,128)S(1)} collective-permute-done((f32[152,512]{1,0:T(8,128)S(1)}, f32[152,512]{1,0:T(8,128)S(1)}, u32[]{:S(2)}, u32[]{:S(2)}) %collective-permute-start.8) | collective-permute-done | bytes 311328 | tf_op jit(solution)/shard_map/ppermute | solution.py:503
  132.2 2.0 %collective-permute-start.9 = (f32[152,512]{1,0:T(8,128)S(1)}, f32[152,512]{1,0:T(8,128)S(1)}, u32[]{:S(2)}, u32[]{:S(2)}) collective-permute-start(f32[152,512]{1,0:T(8,128)S(1)} %add.48.one_ref), channel_id=1, source_target_pairs={{0,96},{16,112},{32,64},{48,80},{64,32},{80,48},{96,0},{112,16},{1... | collective-permute-start | bytes 933896 | tf_op jit(solution)/shard_map/ppermute | solution.py:503
  134.3 0.1 collective-permute-start.11
  134.4 7.9 %collective-permute-done.11.two_in_ref = f32[144,512]{1,0:T(8,128)S(1)} collective-permute-done((f32[144,512]{1,0:T(8,128)S(1)}, f32[144,512]{1,0:T(8,128)S(1)}, u32[]{:S(2)}, u32[]{:S(2)}) %collective-permute-start.11) | collective-permute-done | bytes 294944 | tf_op jit(solution)/shard_map/ppermute | solution.py:503
  142.3 1.1 step.1
  143.4 0.1 collective-permute-start.12
  143.5 0.5 collective-permute-start.13
  144.0 1.1 collective-permute-done.13.other_part_ref
  145.1 1.4 forward.3
  146.5 0.1 convert_element_type.22
  146.6 16.3 %all_to_all.39 = f16[16,160,128]{2,1,0:T(8,128)(2,1)S(1)} all-to-all(f16[16,160,128]{2,1,0:T(8,128)(2,1)S(1)} %convert_element_type.22), channel_id=1, replica_groups=mesh['ex'=8,'ctr'=16] {'ctr'}, dimensions={0} | all-to-all | bytes 1310720 | tf_op jit(solution)/shard_map/all_to_all | solution.py:509
  162.9 0.1 convert_element_type.23.parts_ref
  163.1 0.7 curve.1
  163.8 0.1 collective-permute-start.14
  163.9 1.2 collective-permute-done.14
  165.1 0.3 collective-permute-start.15
  165.3 3.4 %collective-permute-done.15 = f32[8,256]{1,0:T(8,128)S(1)} collective-permute-done((f32[8,256]{1,0:T(8,128)S(1)}, f32[8,256]{1,0:T(8,128)S(1)}, u32[]{:S(2)}, u32[]{:S(2)}) %collective-permute-start.15) | collective-permute-done | bytes 8224 | tf_op jit(solution)/shard_map/ppermute | solution.py:503
  168.7 1.7 collective-permute-start.16
  170.4 3.1 %collective-permute-done.16 = f32[8,256]{1,0:T(8,128)S(1)} collective-permute-done((f32[8,256]{1,0:T(8,128)S(1)}, f32[8,256]{1,0:T(8,128)S(1)}, u32[]{:S(2)}, u32[]{:S(2)}) %collective-permute-start.16) | collective-permute-done | bytes 8224 | tf_op jit(solution)/shard_map/ppermute | solution.py:503
  173.6 11.1 %all_to_all.40.curve_ref = f32[16,8,256]{2,1,0:T(8,128)S(1)} all-to-all(f32[16,8,256]{2,1,0:T(8,128)S(1)} %broadcast_in_dim.7), channel_id=1, replica_groups=mesh['ex'=8,'ctr'=16] {'ctr'}, dimensions={0} | all-to-all | bytes 262144 | tf_op jit(solution)/shard_map/all_to_all | solution.py:509
  184.7 0.9 margins.1
  (29 shorter events, 0.5 us)
Async XLA Ops:
  0.0 14.2 %copy-start = (s32[2048]{0:T(1024)S(1)}, s32[2048]{0:T(1024)}, u32[]{:S(2)}) copy-start(s32[2048]{0:T(1024)} %param.9) | copy-start | bytes 24580
  0.0 9.8 %copy-start.2 = (bf16[64,2048]{1,0:T(8,128)(2,1)S(1)}, bf16[64,2048]{1,0:T(8,128)(2,1)}, u32[]{:S(2)}) copy-start(bf16[64,2048]{1,0:T(8,128)(2,1)} %centers_ref.1) | copy-start | bytes 786436
  0.0 9.8 %copy-start.3 = (s32[2048]{0:T(1024)S(1)}, s32[2048]{0:T(1024)}, u32[]{:S(2)}) copy-start(s32[2048]{0:T(1024)} %param.8) | copy-start | bytes 24580
  1.6 19.6 %copy-start.6 = (bf16[144,2048]{1,0:T(8,128)(2,1)S(1)}, bf16[144,2048]{1,0:T(8,128)(2,1)}, u32[]{:S(2)}) copy-start(bf16[144,2048]{1,0:T(8,128)(2,1)} %alpha_ref.1) | copy-start | bytes 1769476
  1.6 19.6 %all-to-all-start = ((bf16[16,64,256]{2,1,0:T(8,128)(2,1)}), bf16[16,64,256]{2,1,0:T(8,128)(2,1)S(1)}, u32[]{:S(2)}, u32[]{:S(2)}) async-start(bf16[16,64,256]{2,1,0:T(8,128)(2,1)} %broadcast_in_dim.6), calls=%async_computation | async-start | bytes 1048576 | tf_op jit(solution)/shard_map/all_to_all | solution.py:509
  10.5 1.0 copy-start.4
  11.4 0.8 copy-start.7
  12.2 1.6 copy-start.1
  21.3 1.2 copy-start.5
  22.5 1.0 copy-start.8
  58.9 2.1 %collective-permute-start = (f32[144,1024]{1,0:T(8,128)S(1)}, f32[144,1024]{1,0:T(8,128)S(1)}, u32[]{:S(2)}, u32[]{:S(2)}) collective-permute-start(f32[144,1024]{1,0:T(8,128)S(1)} %get-tuple-element.62), channel_id=1, source_target_pairs={{0,16},{16,0},{32,48},{48,32},{64,80},{80,64},{96,112},{112,96},{1... | collective-permute-start | bytes 1769480 | tf_op jit(solution)/shard_map/ppermute | solution.py:506
  61.1 10.4 %collective-permute-start.3 = (f32[144,512]{1,0:T(8,128)S(1)}, f32[144,512]{1,0:T(8,128)S(1)}, u32[]{:S(2)}, u32[]{:S(2)}) collective-permute-start(f32[144,512]{1,0:T(8,128)S(1)} %get-tuple-element.85), channel_id=1, source_target_pairs={{0,96},{16,112},{32,64},{48,80},{64,32},{80,48},{96,0},{112,16},{1... | collective-permute-start | bytes 884744 | tf_op jit(solution)/shard_map/ppermute | solution.py:503
  64.2 8.8 %collective-permute-start.1 = (f32[144,512]{1,0:T(8,128)S(1)}, f32[144,512]{1,0:T(8,128)S(1)}, u32[]{:S(2)}, u32[]{:S(2)}) collective-permute-start(f32[144,512]{1,0:T(8,128)S(1)} %get-tuple-element.86), channel_id=1, source_target_pairs={{0,32},{16,48},{32,0},{48,16},{64,96},{80,112},{96,64},{112,80},{1... | collective-permute-start | bytes 884744 | tf_op jit(solution)/shard_map/ppermute | solution.py:503
  71.5 8.4 %collective-permute-start.4 = (f32[144,512]{1,0:T(8,128)S(1)}, f32[144,512]{1,0:T(8,128)S(1)}, u32[]{:S(2)}, u32[]{:S(2)}) collective-permute-start(f32[144,512]{1,0:T(8,128)S(1)} %add.46.two_ref), channel_id=1, source_target_pairs={{0,32},{16,48},{32,0},{48,16},{64,96},{80,112},{96,64},{112,80},{1... | collective-permute-start | bytes 884744 | tf_op jit(solution)/shard_map/ppermute | solution.py:503
  73.0 9.2 %collective-permute-start.2 = (f32[144,512]{1,0:T(8,128)S(1)}, f32[144,512]{1,0:T(8,128)S(1)}, u32[]{:S(2)}, u32[]{:S(2)}) collective-permute-start(f32[144,512]{1,0:T(8,128)S(1)} %add.44.one_ref), channel_id=1, source_target_pairs={{0,96},{16,112},{32,64},{48,80},{64,32},{80,48},{96,0},{112,16},{1... | collective-permute-start | bytes 884744 | tf_op jit(solution)/shard_map/ppermute | solution.py:503
  83.1 1.7 collective-permute-start.5
  83.2 1.6 collective-permute-start.6
  120.5 2.1 %collective-permute-start.7 = (f32[152,1024]{1,0:T(8,128)S(1)}, f32[152,1024]{1,0:T(8,128)S(1)}, u32[]{:S(2)}, u32[]{:S(2)}) collective-permute-start(f32[152,1024]{1,0:T(8,128)S(1)} %get-tuple-element.74), channel_id=1, source_target_pairs={{0,16},{16,0},{32,48},{48,32},{64,80},{80,64},{96,112},{112,96},{1... | collective-permute-start | bytes 1867784 | tf_op jit(solution)/shard_map/ppermute | solution.py:506
  122.7 9.5 %collective-permute-start.8 = (f32[152,512]{1,0:T(8,128)S(1)}, f32[152,512]{1,0:T(8,128)S(1)}, u32[]{:S(2)}, u32[]{:S(2)}) collective-permute-start(f32[152,512]{1,0:T(8,128)S(1)} %slice_add_fusion), channel_id=1, source_target_pairs={{0,32},{16,48},{32,0},{48,16},{64,96},{80,112},{96,64},{112,80},{1... | collective-permute-start | bytes 933896 | tf_op jit(solution)/shard_map/ppermute | solution.py:503
  123.0 11.3 %collective-permute-start.10 = (f32[144,512]{1,0:T(8,128)S(1)}, f32[144,512]{1,0:T(8,128)S(1)}, u32[]{:S(2)}, u32[]{:S(2)}) collective-permute-start(f32[144,512]{1,0:T(8,128)S(1)} %slice_add_fusion.1), channel_id=1, source_target_pairs={{0,96},{16,112},{32,64},{48,80},{64,32},{80,48},{96,0},{112,16},{1... | collective-permute-start | bytes 884744 | tf_op jit(solution)/shard_map/ppermute | solution.py:503
  132.2 10.1 %collective-permute-start.9 = (f32[152,512]{1,0:T(8,128)S(1)}, f32[152,512]{1,0:T(8,128)S(1)}, u32[]{:S(2)}, u32[]{:S(2)}) collective-permute-start(f32[152,512]{1,0:T(8,128)S(1)} %add.48.one_ref), channel_id=1, source_target_pairs={{0,96},{16,112},{32,64},{48,80},{64,32},{80,48},{96,0},{112,16},{1... | collective-permute-start | bytes 933896 | tf_op jit(solution)/shard_map/ppermute | solution.py:503
  134.3 8.0 %collective-permute-start.11 = (f32[144,512]{1,0:T(8,128)S(1)}, f32[144,512]{1,0:T(8,128)S(1)}, u32[]{:S(2)}, u32[]{:S(2)}) collective-permute-start(f32[144,512]{1,0:T(8,128)S(1)} %add.50.two_ref), channel_id=1, source_target_pairs={{0,32},{16,48},{32,0},{48,16},{64,96},{80,112},{96,64},{112,80},{1... | collective-permute-start | bytes 884744 | tf_op jit(solution)/shard_map/ppermute | solution.py:503
  143.4 1.7 collective-permute-start.12
  143.5 1.6 collective-permute-start.13
  163.8 1.3 collective-permute-start.14
  165.1 3.7 %collective-permute-start.15 = (f32[8,256]{1,0:T(8,128)S(1)}, f32[8,256]{1,0:T(8,128)S(1)}, u32[]{:S(2)}, u32[]{:S(2)}) collective-permute-start(f32[8,256]{1,0:T(8,128)S(1)} %add.51), channel_id=1, source_target_pairs={{0,32},{16,48},{32,0},{48,16},{64,96},{80,112},{96,64},{112,80},{1... | collective-permute-start | bytes 24584 | tf_op jit(solution)/shard_map/ppermute | solution.py:503
  168.7 4.9 %collective-permute-start.16 = (f32[8,256]{1,0:T(8,128)S(1)}, f32[8,256]{1,0:T(8,128)S(1)}, u32[]{:S(2)}, u32[]{:S(2)}) collective-permute-start(f32[8,256]{1,0:T(8,128)S(1)} %add.52), channel_id=1, source_target_pairs={{0,96},{16,112},{32,64},{48,80},{64,32},{80,48},{96,0},{112,16},{1... | collective-permute-start | bytes 24584 | tf_op jit(solution)/shard_map/ppermute | solution.py:503

commit v4 on v3

--- a/solution.py
+++ b/solution.py
@@ -31,16 +31,17 @@
 
 SCALAR = pl.BlockSpec(memory_space=pltpu.SMEM)
 WHOLE = pl.BlockSpec(memory_space=pltpu.VMEM)
-
-
-def call(kernel, name, out_shape, flops, scratch=(), scalars=0, arrays=0):
+ANYWHERE = pl.BlockSpec(memory_space=pl.ANY)
+
+
+def call(kernel, name, out_shape, flops, scratch=(), scalars=0, anywhere=0, arrays=0):
     shapes = out_shape if isinstance(out_shape, list) else [out_shape]
     size = sum(math.prod(s.shape) * s.dtype.itemsize for s in shapes)
     return pl.pallas_call(
         kernel,
         out_shape=out_shape,
         scratch_shapes=list(scratch),
-        in_specs=[SCALAR] * scalars + [WHOLE] * arrays,
+        in_specs=[SCALAR] * scalars + [ANYWHERE] * anywhere + [WHOLE] * arrays,
         compiler_params=pltpu.CompilerParams(vmem_limit_bytes=VMEM_BYTES),
         cost_estimate=pl.CostEstimate(flops=flops, bytes_accessed=size, transcendentals=0),
         name=name,
@@ -69,16 +70,20 @@
     return jnp.ceil(jnp.log2(jnp.maximum(bounds, 1e-30)))
 
 
-def half_rows(powers, vectors):
-    row = lax.broadcasted_iota(jnp.int32, (EXTRA, LANES), 0)
+def half_pieces(powers, vectors):
     pieces = [powers]
     for vector in vectors:
         power = exponents(jnp.abs(vector)) + 1.0
         scaled = vector * jnp.exp2(-power) * 2048.0
         high = jnp.floor(scaled + 0.5)
         pieces += [power, high / 2048.0, jnp.floor((scaled - high) * 2048.0 + 0.5) / 2048.0]
+    return pieces
+
+
+def half_rows(powers, vectors):
+    row = lax.broadcasted_iota(jnp.int32, (EXTRA, LANES), 0)
     out = jnp.zeros((EXTRA, LANES), F32)
-    for p, piece in enumerate(pieces):
+    for p, piece in enumerate(half_pieces(powers, vectors)):
         for q in range(2):
             out = jnp.where(row == 2 * p + q, piece[:, q * LANES : (q + 1) * LANES], out)
     return out
@@ -140,13 +145,25 @@
     return out
 
 
-def prepare_kernel(index_ref, centers_ref, sides_ref, one_hot_ref):
+def copies_kernel(block_ref, copies_ref):
+    for k in range(copies_ref.shape[0]):
+        copies_ref[k] = block_ref[...]
+
+
+def copies(block, number):
+    return call(copies_kernel, "copies", shape((number,) + block.shape, block.dtype), 1 << 20, arrays=1)(
+        block
+    )
+
+
+def prepare_kernel(index_ref, centers_ref, sides_ref, one_hot_ref, chunk_ref):
     features, count = centers_ref.shape
     lanes = one_hot_ref.shape[0]
     center_float = centers_ref[...].astype(F32)
     center_sq = jnp.sum(center_float * center_float, axis=0, keepdims=True)
     side = jnp.concatenate([center_float, tail(center_sq, 3, DEPTH - features)], axis=0)
     sides_ref[...] = side.T.astype(BF16)
+    chunk_ref[...] = index_ref[...] // lanes
     within = index_ref[...] % lanes
     row = lax.broadcasted_iota(jnp.int32, (lanes, index_ref.shape[1]), 0)
     one_hot_ref[...] = (row == within).astype(F32).astype(BF16)
@@ -158,15 +175,18 @@
     return call(
         prepare_kernel,
         "prepare",
-        [shape((count, DEPTH), BF16), shape((lanes, examples), BF16)],
+        [shape((count, DEPTH), BF16), shape((lanes, examples), BF16), shape(index.shape, jnp.int32)],
         1 << 20,
         arrays=2,
     )(index, centers)
 
 
 def tile_kernel(
-    index_ref, pool_ref, one_hot_ref, sides_ref, alpha_ref, tile_ref, turned_ref, rows_ref, side_ref
+    alpha_hbm, chunk_ref, pool_ref, one_hot_ref, sides_ref, tile_ref, turned_ref, rows_ref,
+    side_ref, alpha_ref, alpha_sem,
 ):
+    fetch = pltpu.make_async_copy(alpha_hbm, alpha_ref, alpha_sem)
+    fetch.start()
     chunks, features, lanes = pool_ref.shape
     count, examples = tile_ref.shape
     share = rows_ref.shape[2]
@@ -174,7 +194,7 @@
     pool = pool_ref[...].reshape(chunks * features, lanes)
     for b in range(examples // BAND):
         here = slice(b * BAND, (b + 1) * BAND)
-        chunk = index_ref[:, here] // lanes
+        chunk = chunk_ref[:, here]
         picked = jnp.dot(pool, one_hot_ref[:, here], preferred_element_type=F32)
         points = jnp.where(chunk == 0, picked[:features], 0.0)
         for k in range(1, chunks):
@@ -188,6 +208,7 @@
         values = jnp.exp2(near * scale).astype(BF16)
         tile_ref[here, :] = values
         turned_ref[:, here] = values.T
+    fetch.wait()
     for b in range(examples // BAND):
         here = slice(b * BAND, (b + 1) * BAND)
         rows = jnp.dot(alpha_ref[...], tile_ref[:, here], preferred_element_type=F32)
@@ -195,8 +216,8 @@
             rows_ref[b * (BAND // share) + k] = rows[:, k * share : (k + 1) * share]
 
 
-def make_tile(index, row_pool, one_hot, sides, alpha, share):
-    examples, count = index.shape[1], sides.shape[0]
+def make_tile(chunk, row_pool, one_hot, sides, alpha, share):
+    examples, count = chunk.shape[1], sides.shape[0]
     classes = alpha.shape[0]
     return call(
         tile_kernel,
@@ -207,9 +228,14 @@
             shape((examples // share, classes, share), F32),
         ],
         4 << 30,
-        [pltpu.VMEM((DEPTH, examples), BF16)],
-        arrays=5,
-    )(index, row_pool, one_hot, sides, alpha)
+        [
+            pltpu.VMEM((DEPTH, examples), BF16),
+            pltpu.VMEM(alpha.shape, BF16),
+            pltpu.SemaphoreType.DMA,
+        ],
+        anywhere=1,
+        arrays=4,
+    )(alpha, chunk, row_pool, one_hot, sides)
 
 
 def factors_kernel(core_ref, precond_ref, high_ref, low_ref, high_turned_ref, low_turned_ref):
@@ -284,47 +310,92 @@
     )(core, own, other, own_part, other_part, tile)
 
 
-def backward_kernel(core_ref, values_ref, turned_ref, other_ref, one_ref, two_ref, flat_ref):
+def backward_kernel(core_ref, values_ref, turned_ref, other_ref, own_ref, flat_ref):
     shares, height, share = values_ref.shape
     classes, examples = flat_ref.shape
     half = other_ref.shape[1]
-    wide = half // 2
     for k in range(shares):
         flat_ref[:, k * share : (k + 1) * share] = values_ref[k, :classes]
     if height > classes:
         total = values_ref[0, classes:].astype(F32)
         for k in range(1, shares):
             total = total + values_ref[k, classes:].astype(F32)
-        row = read_rows(total, 0)
-        other_ref[classes:, : 2 * LANES] = jnp.broadcast_to(row, (8, 2 * LANES))
-        other_ref[classes:, 2 * LANES :] = jnp.zeros((8, half - 2 * LANES), F32)
-        one_ref[classes:, : 2 * LANES] = jnp.broadcast_to(row, (8, 2 * LANES))
-        one_ref[classes:, 2 * LANES :] = jnp.zeros((8, wide - 2 * LANES), F32)
-    for h, first in enumerate(((1 - core_ref[0]) * half, core_ref[0] * half)):
+        row = jnp.broadcast_to(read_rows(total, 0), (8, 2 * LANES))
+        for ref in (other_ref, own_ref):
+            ref[classes:, : 2 * LANES] = row
+            ref[classes:, 2 * LANES :] = jnp.zeros((8, half - 2 * LANES), F32)
+    for first, ref in (((1 - core_ref[0]) * half, other_ref), (core_ref[0] * half, own_ref)):
         for b in range(half // BAND):
             there = pl.ds(pl.multiple_of(first + b * BAND, BAND), BAND)
-            sums = jnp.dot(flat_ref[...], turned_ref[:, there], preferred_element_type=F32)
-            if h == 0:
-                other_ref[:classes, b * BAND : (b + 1) * BAND] = sums
-            elif b * BAND < wide:
-                one_ref[:classes, b * BAND : (b + 1) * BAND] = sums
-            else:
-                two_ref[:, b * BAND - wide : (b + 1) * BAND - wide] = sums
+            ref[:classes, b * BAND : (b + 1) * BAND] = jnp.dot(
+                flat_ref[...], turned_ref[:, there], preferred_element_type=F32
+            )
 
 
 def backward(core, values, turned, classes):
     examples, count = turned.shape
     height = classes + (8 if values.shape[1] > classes else 0)
-    half = count // 2
+    half = shape((height, count // 2), F32)
     return call(
         backward_kernel,
         "backward",
-        [shape((height, half), F32), shape((height, half // 2), F32), shape((classes, half // 2), F32)],
+        [half, half],
         1208 << 20,
         [pltpu.VMEM((classes, examples), BF16)],
         scalars=1,
         arrays=2,
     )(core, values, turned)
+
+
+def pack_halves(ref, values, vectors):
+    classes, wide = values.shape
+    size = jnp.max(jnp.abs(values), axis=1, keepdims=True)
+    powers = exponents(size) - 14.0
+    ref[:classes] = values * jnp.exp2(-powers)
+    empty = jnp.zeros((2 * LANES - classes, LANES), F32)
+    powers = jnp.concatenate([jnp.broadcast_to(powers, (classes, LANES)), empty], axis=0).T[:1]
+    row = lax.broadcasted_iota(jnp.int32, (EXTRA, 2 * LANES), 0)
+    out = jnp.zeros((EXTRA, 2 * LANES), F32)
+    for p, piece in enumerate(half_pieces(powers, vectors)):
+        out = jnp.where(row == p, piece, out)
+    ref[classes:, : 2 * LANES] = out
+    ref[classes:, 2 * LANES :] = jnp.zeros((EXTRA, wide - 2 * LANES), F32)
+
+
+def unpack_halves(ref):
+    classes = ref.shape[0] - EXTRA
+    return ref[:classes] * column(jnp.exp2(ref[classes : classes + 1, : 2 * LANES]), classes)
+
+
+def unpack_vector(ref):
+    classes = ref.shape[0] - EXTRA
+    power, high, low = (ref[classes + p : classes + p + 1, : 2 * LANES] for p in range(1, 4))
+    return jnp.exp2(power) * (high + low / 2048.0)
+
+
+def join_kernel(own_ref, got_ref, one_ref, two_ref):
+    classes, wide = one_ref.shape[0] - EXTRA, one_ref.shape[1]
+    for k, ref in enumerate((one_ref, two_ref)):
+        here = slice(k * wide, (k + 1) * wide)
+        vectors = []
+        if k == 0 and own_ref.shape[0] > classes:
+            row = slice(classes, classes + 1)
+            vectors = [own_ref[row, : 2 * LANES] + got_ref[row, : 2 * LANES]]
+        pack_halves(ref, own_ref[:classes, here] + got_ref[:classes, here], vectors)
+
+
+def join(own, got, classes):
+    half = shape((classes + EXTRA, own.shape[1] // 2), F32)
+    return call(join_kernel, "join", [half, half], 1 << 20, arrays=2)(own, got)
+
+
+def add_kernel(own_ref, got_ref, sum_ref):
+    vector = unpack_vector(own_ref) + unpack_vector(got_ref)
+    pack_halves(sum_ref, unpack_halves(own_ref) + unpack_halves(got_ref), [vector])
+
+
+def add_halves(own, got):
+    return call(add_kernel, "add", shape(own.shape, F32), 1 << 20, arrays=2)(own, got)
 
 
 def gradient_kernel(base_ref, label_ref, weight_ref, hessian_ref, send_ref):
@@ -353,7 +424,9 @@
     total, one_ref, one_in_ref, two_ref, two_in_ref, high_ref, low_ref, high_turned_ref,
     low_turned_ref, residual_ref, lifted_ref, part_ref,
 ):
-    sums = jnp.concatenate([one_ref[...] + one_in_ref[...], two_ref[...] + two_in_ref[...]], axis=1)
+    one = unpack_halves(one_ref) + unpack_halves(one_in_ref)
+    two = unpack_halves(two_ref) + unpack_halves(two_in_ref)
+    sums = jnp.concatenate([one, two], axis=1)
     residual = block_products(sums, high_ref, low_ref) * (-1.0 / total)
     residual_ref[...] = residual
     lifted = block_products(residual, high_turned_ref, low_turned_ref).astype(BF16)
@@ -365,7 +438,7 @@
 
 
 def first_residual(total, sums, blocks):
-    classes, wide = sums[2].shape
+    classes, wide = sums[2].shape[0] - EXTRA, sums[2].shape[1]
     return call(
         functools.partial(residual_kernel, total),
         "residual",
@@ -406,13 +479,14 @@
     low_turned_ref, residual_ref, norm_ref, lifted_ref, part_ref, rough_ref,
 ):
     classes = residual_ref.shape[0]
-    one = one_ref[...] + one_in_ref[...]
-    curve = one[classes : classes + 1, : 2 * LANES] / total
+    one = unpack_halves(one_ref) + unpack_halves(one_in_ref)
+    two = unpack_halves(two_ref) + unpack_halves(two_in_ref)
+    curve = (unpack_vector(one_ref) + unpack_vector(one_in_ref)) / total
     norm = norm_ref[:1]
     lane = lax.broadcasted_iota(jnp.int32, (1, 2 * LANES), 1)
     rough = jnp.where(lane < classes, norm / (curve + RIDGE * norm), 0.0)
     rough_ref[...] = stack_rows([rough])
-    sums = jnp.concatenate([one[:classes], two_ref[...] + two_in_ref[...]], axis=1)
+    sums = jnp.concatenate([one, two], axis=1)
     old = residual_ref[...]
     image = block_products(sums, high_ref, low_ref) / total + RIDGE * old
     new = old - column(rough, classes) * image
@@ -511,43 +585,46 @@
     def trade_halves(parts):
         return trade(parts.astype(F16)).astype(F32)
 
-    def sum_examples(products):
-        other, one, two = products
-        got = over_cores(other)
-        wide = one.shape[1]
-        one = one + got[:, :wide]
-        two = two + got[:classes, wide:]
-        one = one + over_y(one, 1)
-        two = two + over_y(two, 3)
-        return one, over_y(one, 3), two, over_y(two, 1)
+    def swap(array, flip):
+        array = lax.reduce_precision(array, 5, 10)
+        return array, over_y(array.astype(F16), flip).astype(F32)
+
+    def sum_examples(own, got):
+        one, two = join(own, got, classes)
+        one, two = swap(one, 1), swap(two, 3)
+        one, two = add_halves(*one), add_halves(*two)
+        return *swap(one, 3), *swap(two, 1)
 
     offset = lax.axis_index("ctr") * share
     label = lax.dynamic_slice_in_dim(labels, offset, share, 0).reshape(1, share)
     weight = lax.dynamic_slice_in_dim(example_weight, offset, share, 0).reshape(1, share)
     index = indices.reshape(1, examples)
-    sides, one_hot = prepare(index, centers, pool.shape[1])
-    blocks = factors(core, precond)
-    row_pool = trade(jnp.broadcast_to(pool, (n_ctr,) + pool.shape))
-    row_pool, sides, one_hot, index, label, weight, core, *blocks = lax.optimization_barrier(
-        (row_pool, sides, one_hot, index, label, weight, core, *blocks)
-    )
-    tile, turned, rows = make_tile(index, row_pool, one_hot, sides, alpha, share)
+    sides, one_hot, chunk = prepare(index, centers, pool.shape[1])
+    row_pool = trade(copies(pool, n_ctr))
+    row_pool, sides, one_hot, chunk, label, weight, core = lax.optimization_barrier(
+        (row_pool, sides, one_hot, chunk, label, weight, core)
+    )
+    tile, turned, rows = make_tile(chunk, row_pool, one_hot, sides, alpha, share)
     base = jnp.sum(trade_halves(rows), axis=0)
     hessian, send = gradient(base, label, weight, n_ctr)
 
-    sums = sum_examples(backward(core, trade(send), turned, classes))
+    other, own = backward(core, trade(send), turned, classes)
+    got = over_cores(other)
+    got, late_core = lax.optimization_barrier((got, core))
+    blocks = factors(late_core, precond)
+    sums = sum_examples(own, got)
     residual, lifted, part = first_residual(total, sums, blocks)
     rows = forward(core, lifted, over_cores(lifted), part, over_cores(part), tile, share)
     image, norm, send = weigh(trade_halves(rows), hessian)
 
-    sums = sum_examples(backward(core, trade(send), turned, classes))
+    other, own = backward(core, trade(send), turned, classes)
+    sums = sum_examples(own, over_cores(other))
     lifted, part, rough = step(total, sums, blocks, residual, norm)
     rows = forward(core, lifted, over_cores(lifted), part, over_cores(part), tile, share)
     last, scales, curve = last_curve(trade_halves(rows), hessian, image, norm, rough)
 
-    curve = curve + over_cores(curve)
-    curve = curve + over_y(curve, 1)
-    curve = curve + over_y(curve, 3)
+    curve = lax.all_to_all(jnp.broadcast_to(curve, (n_ex,) + curve.shape), "ex", 0, 0)
+    curve = jnp.sum(curve, axis=0)
     curve = trade(jnp.broadcast_to(curve, (n_ctr,) + curve.shape))
     return margins(total, curve, scales, base, image, last)
 

time: 186 us -> 174 us (0.935)
  waiting for transfers between devices: 50.5 us -> 33 us
  blocking collectives: 87.4 us -> 96 us
  local copies, waits for them, and re-layouts: 8.12 us -> 1.68 us
  Pallas kernels: 16.7 us -> 20 us
  starting transfers between devices: 21.6 us -> 19.7 us
    ppermute x10 -> x8, waiting for transfers between devices: 36.9 us -> 16.9 us  [over_y(): return lax.ppermute(array, 'ex', pairs)]
    all_to_all x0 -> x1, blocking collectives: none -> 8.68 us  [shards(): lax.all_to_all(jnp.broadcast_to(curve, (n_ex,) + curve.shape), 'ex', 0, 0)]
    unnamed x18 -> x12, local copies, waits for them, and re-layouts: 5.63 us -> 0.82 us
    all_to_all x1, waiting for transfers between devices: 6.27 us -> 9.98 us  [trade(): return lax.all_to_all(parts, 'ctr', 0, 0)]
    pallas_call x2 -> x9, Pallas kernels: 2.95 us -> 5.64 us  [the longest x2 2.95 us: backward(): call(backward_kernel, 'backward', [half, half], 1208 << 20, [pltpu.VMEM((...]
    ppermute x10 -> x8, starting transfers between devices: 12.1 us -> 10.4 us  [over_y(): return lax.ppermute(array, 'ex', pairs)]
    ppermute x7 -> x6, waiting for transfers between devices: 7.36 us -> 6.2 us  [over_cores(): return lax.ppermute(array, 'ex', core_pairs)]
  transfers between devices with their start and end apart: 18 -> 15, of which waited for: 14 -> 11; matrix products, arithmetic and copies ran while one was open for 1% -> 1% of each run, Pallas kernels for 1% -> 1%
where the time goes in v4:
time: 174 us; the launch traced here: 173 us
  blocking collectives  96 us (55%)
  waiting for transfers between devices  33 us (19%)
  Pallas kernels  20 us (11%)
  starting transfers between devices  19.7 us (11%)
  other arithmetic  2.2 us (1%)
    all_to_all x6, blocking collectives, trade(): return lax.all_to_all(parts, 'ctr', 0, 0)  87.4 us
    ppermute x8, waiting for transfers between devices, over_y(): return lax.ppermute(array, 'ex', pairs)  16.9 us
    ppermute x8, starting transfers between devices, over_y(): return lax.ppermute(array, 'ex', pairs)  10.4 us
    all_to_all x1, waiting for transfers between devices, trade(): return lax.all_to_all(parts, 'ctr', 0, 0)  9.98 us
    all_to_all x1, blocking collectives, shards(): lax.all_to_all(jnp.broadcast_to(curve, (n_ex,) + curve.shape), 'ex', 0, 0)  8.68 us
    all_to_all x1, starting transfers between devices, trade(): return lax.all_to_all(parts, 'ctr', 0, 0)  7.96 us
    ppermute x6, waiting for transfers between devices, over_cores(): return lax.ppermute(array, 'ex', core_pairs)  6.2 us
    pallas_call x1, Pallas kernels, make_tile(): call(tile_kernel, 'tile', [shape((count, examples), BF16), shape((example...  5.93 us
  transfers between devices with their start and end apart: 15, of which 11 were waited for; matrix products, arithmetic and copies ran while one was open for 1% of the time, Pallas kernels for 1%

profile of v4, /device:TPU:0, one launch (start us, length us, event | category | flops | bytes accessed | tf_op | source)
XLA Modules:
  0.0 173.1 jit_solution(13645726721315532384)
XLA Ops:
  0.0 0.8 copy-done.3
  0.8 0.8 copies.1
  1.6 8.0 %all-to-all-start = ((bf16[16,64,256]{2,1,0:T(8,128)(2,1)}), bf16[16,64,256]{2,1,0:T(8,128)(2,1)S(1)}, u32[]{:S(2)}, u32[]{:S(2)}) async-start(bf16[16,64,256]{2,1,0:T(8,128)(2,1)} %copies.1), calls=%async_computation | async-start | bytes 1048576 | tf_op jit(solution)/shard_map/all_to_all | solution.py:583
  9.6 0.7 prepare.1
  10.4 0.8 dynamic-slice_bitcast_fusion.weight_ref
  11.2 10.0 %all-to-all-done.pool_ref = bf16[16,64,256]{2,1,0:T(8,128)(2,1)S(1)} async-done(((bf16[16,64,256]{2,1,0:T(8,128)(2,1)}), bf16[16,64,256]{2,1,0:T(8,128)(2,1)S(1)}, u32[]{:S(2)}, u32[]{:S(2)}) %all-to-all-start) | async-done | bytes 524320 | tf_op jit(solution)/shard_map/all_to_all | solution.py:583
  21.1 5.9 %tile.1 = (bf16[2048,2048]{1,0:T(8,128)(2,1)S(1)}, bf16[2048,2048]{1,0:T(8,128)(2,1)S(1)}, f32[16,144,128]{2,1,0:T(8,128)S(1)}) custom-call(bf16[144,2048]{1,0:T(8,128)(2,1)S(1)} %copy-done.5, s32[1,2048]{1,0:T(1,128)S(1)} %get-tuple-element.50.chunk_ref, bf16[16,64,256]{2,1,0:T(8,128)(2,1)S(1)} %all-to-all-done.pool_ref, ...), custom_call_target="tpu_custom_call" | custom-call | flops 4294967296 | bytes 17956864 | tf_op jit(solution)/shard_map/tile/pallas_call | solution.py:222
  27.2 14.4 %all_to_all.40 = f16[16,144,128]{2,1,0:T(8,128)(2,1)S(1)} all-to-all(f16[16,144,128]{2,1,0:T(8,128)(2,1)S(1)} %convert_element_type.66), channel_id=1, replica_groups=mesh['ex'=8,'ctr'=16] {'ctr'}, dimensions={0} | all-to-all | bytes 1179648 | tf_op jit(solution)/shard_map/all_to_all | solution.py:583
  41.7 13.7 %all_to_all.41.values_ref = bf16[16,144,128]{2,1,0:T(8,128)(2,1)S(1)} all-to-all(bf16[16,144,128]{2,1,0:T(8,128)(2,1)S(1)} %get-tuple-element.57), channel_id=1, replica_groups=mesh['ex'=8,'ctr'=16] {'ctr'}, dimensions={0} | all-to-all | bytes 1179648 | tf_op jit(solution)/shard_map/all_to_all | solution.py:583
  55.4 1.5 backward.2
  56.9 0.1 collective-permute-start
  57.0 2.0 %collective-permute-done.got_ref = f32[144,1024]{1,0:T(8,128)S(1)} collective-permute-done((f32[144,1024]{1,0:T(8,128)S(1)}, f32[144,1024]{1,0:T(8,128)S(1)}, u32[]{:S(2)}, u32[]{:S(2)}) %collective-permute-start) | collective-permute-done | bytes 589856 | tf_op jit(solution)/shard_map/ppermute | solution.py:580
  59.0 0.2 join.2
  59.2 0.2 reduce-precision_convert_fusion.7
  59.4 1.7 collective-permute-start.1
  61.0 0.2 reduce-precision_convert_fusion.5
  61.2 2.3 %collective-permute-start.3 = (f16[160,512]{1,0:T(8,128)(2,1)S(1)}, f16[160,512]{1,0:T(8,128)(2,1)S(1)}, u32[]{:S(2)}, u32[]{:S(2)}) collective-permute-start(f16[160,512]{1,0:T(8,128)(2,1)S(1)} %get-tuple-element.97), channel_id=1, source_target_pairs={{0,96},{16,112},{32,64},{48,80},{64,32},{80,48},{96,0},{112,16},{1... | collective-permute-start | bytes 491528 | tf_op jit(solution)/shard_map/ppermute | solution.py:577
  63.5 2.2 %collective-permute-done.1 = f16[160,512]{1,0:T(8,128)(2,1)S(1)} collective-permute-done((f16[160,512]{1,0:T(8,128)(2,1)S(1)}, f16[160,512]{1,0:T(8,128)(2,1)S(1)}, u32[]{:S(2)}, u32[]{:S(2)}) %collective-permute-start.1) | collective-permute-done | bytes 163872 | tf_op jit(solution)/shard_map/ppermute | solution.py:577
  65.7 0.4 add.14
  66.1 0.2 reduce-precision_convert_fusion.6
  66.3 3.1 %collective-permute-start.2 = (f16[160,512]{1,0:T(8,128)(2,1)S(1)}, f16[160,512]{1,0:T(8,128)(2,1)S(1)}, u32[]{:S(2)}, u32[]{:S(2)}) collective-permute-start(f16[160,512]{1,0:T(8,128)(2,1)S(1)} %get-tuple-element.99), channel_id=1, source_target_pairs={{0,96},{16,112},{32,64},{48,80},{64,32},{80,48},{96,0},{112,16},{1... | collective-permute-start | bytes 491528 | tf_op jit(solution)/shard_map/ppermute | solution.py:577
  69.4 0.4 add.15
  69.8 0.2 reduce-precision_convert_fusion.4
  69.9 0.4 collective-permute-start.4
  70.3 0.3 factors.1
  70.7 2.3 %collective-permute-done.2 = f16[160,512]{1,0:T(8,128)(2,1)S(1)} collective-permute-done((f16[160,512]{1,0:T(8,128)(2,1)S(1)}, f16[160,512]{1,0:T(8,128)(2,1)S(1)}, u32[]{:S(2)}, u32[]{:S(2)}) %collective-permute-start.2) | collective-permute-done | bytes 163872 | tf_op jit(solution)/shard_map/ppermute | solution.py:577
  73.1 2.4 %collective-permute-done.4 = f16[160,512]{1,0:T(8,128)(2,1)S(1)} collective-permute-done((f16[160,512]{1,0:T(8,128)(2,1)S(1)}, f16[160,512]{1,0:T(8,128)(2,1)S(1)}, u32[]{:S(2)}, u32[]{:S(2)}) %collective-permute-start.4) | collective-permute-done | bytes 163872 | tf_op jit(solution)/shard_map/ppermute | solution.py:577
  75.5 1.0 residual.1
  76.7 0.5 collective-permute-start.6
  77.2 1.1 collective-permute-done.6.other_part_ref
  78.3 1.4 forward.2
  79.7 0.1 convert_element_type.76
  79.8 16.3 %all_to_all.42 = f16[16,160,128]{2,1,0:T(8,128)(2,1)S(1)} all-to-all(f16[16,160,128]{2,1,0:T(8,128)(2,1)S(1)} %convert_element_type.76), channel_id=1, replica_groups=mesh['ex'=8,'ctr'=16] {'ctr'}, dimensions={0} | all-to-all | bytes 1310720 | tf_op jit(solution)/shard_map/all_to_all | solution.py:583
  96.1 0.1 convert_element_type.77.parts_ref
  96.3 0.7 weigh.1
  97.0 15.6 %all_to_all.43.values_ref = bf16[16,160,128]{2,1,0:T(8,128)(2,1)S(1)} all-to-all(bf16[16,160,128]{2,1,0:T(8,128)(2,1)S(1)} %get-tuple-element.73), channel_id=1, replica_groups=mesh['ex'=8,'ctr'=16] {'ctr'}, dimensions={0} | all-to-all | bytes 1310720 | tf_op jit(solution)/shard_map/all_to_all | solution.py:583
  112.6 1.5 backward.3
  114.0 0.1 collective-permute-start.7
  114.1 2.0 %collective-permute-done.7.got_ref = f32[152,1024]{1,0:T(8,128)S(1)} collective-permute-done((f32[152,1024]{1,0:T(8,128)S(1)}, f32[152,1024]{1,0:T(8,128)S(1)}, u32[]{:S(2)}, u32[]{:S(2)}) %collective-permute-start.7) | collective-permute-done | bytes 622624 | tf_op jit(solution)/shard_map/ppermute | solution.py:580
  116.2 0.2 join.3
  116.4 0.2 reduce-precision_convert_fusion.3
  116.6 0.2 collective-permute-start.8
  116.8 0.2 reduce-precision_convert_fusion.1
  117.0 1.3 collective-permute-start.10
  118.2 4.7 %collective-permute-done.8 = f16[160,512]{1,0:T(8,128)(2,1)S(1)} collective-permute-done((f16[160,512]{1,0:T(8,128)(2,1)S(1)}, f16[160,512]{1,0:T(8,128)(2,1)S(1)}, u32[]{:S(2)}, u32[]{:S(2)}) %collective-permute-start.8) | collective-permute-done | bytes 163872 | tf_op jit(solution)/shard_map/ppermute | solution.py:577
  122.9 0.4 add.16
  123.3 0.2 reduce-precision_convert_fusion.2
  123.5 1.3 collective-permute-start.9
  124.8 0.4 add.17
  125.2 0.2 reduce-precision_convert_fusion
  125.4 0.2 collective-permute-start.11
  125.5 4.6 %collective-permute-done.9 = f16[160,512]{1,0:T(8,128)(2,1)S(1)} collective-permute-done((f16[160,512]{1,0:T(8,128)(2,1)S(1)}, f16[160,512]{1,0:T(8,128)(2,1)S(1)}, u32[]{:S(2)}, u32[]{:S(2)}) %collective-permute-start.9) | collective-permute-done | bytes 163872 | tf_op jit(solution)/shard_map/ppermute | solution.py:577
  130.2 0.6 collective-permute-done.11
  130.8 1.2 step.1
  132.1 0.5 collective-permute-start.13
  132.6 1.1 collective-permute-done.13.other_part_ref
  133.7 1.4 forward.3
  135.1 0.1 convert_element_type.86
  135.2 16.3 %all_to_all.44 = f16[16,160,128]{2,1,0:T(8,128)(2,1)S(1)} all-to-all(f16[16,160,128]{2,1,0:T(8,128)(2,1)S(1)} %convert_element_type.86), channel_id=1, replica_groups=mesh['ex'=8,'ctr'=16] {'ctr'}, dimensions={0} | all-to-all | bytes 1310720 | tf_op jit(solution)/shard_map/all_to_all | solution.py:583
  151.5 0.1 convert_element_type.87.parts_ref
  151.7 0.7 curve.1
  152.4 8.7 %all_to_all.45 = f32[8,8,256]{2,1,0:T(8,128)S(1)} all-to-all(f32[8,8,256]{2,1,0:T(8,128)S(1)} %broadcast_in_dim.6), channel_id=1, replica_groups=mesh['ex'=8,'ctr'=16] {'ex'}, dimensions={0} | all-to-all | bytes 131072 | tf_op jit(solution)/shard_map/all_to_all | solution.py:626
  161.1 11.1 %all_to_all.46.curve_ref = f32[16,8,256]{2,1,0:T(8,128)S(1)} all-to-all(f32[16,8,256]{2,1,0:T(8,128)S(1)} %broadcast_in_dim.7), channel_id=1, replica_groups=mesh['ex'=8,'ctr'=16] {'ctr'}, dimensions={0} | all-to-all | bytes 262144 | tf_op jit(solution)/shard_map/all_to_all | solution.py:583
  172.2 0.9 margins.1
  (32 shorter events, 0.7 us)
Async XLA Ops:
  0.0 10.3 %copy-start = (s32[2048]{0:T(1024)S(1)}, s32[2048]{0:T(1024)}, u32[]{:S(2)}) copy-start(s32[2048]{0:T(1024)} %param.9) | copy-start | bytes 24580
  0.0 9.6 %copy-start.2 = (bf16[64,2048]{1,0:T(8,128)(2,1)S(1)}, bf16[64,2048]{1,0:T(8,128)(2,1)}, u32[]{:S(2)}) copy-start(bf16[64,2048]{1,0:T(8,128)(2,1)} %centers_ref.1) | copy-start | bytes 786436
  0.0 0.8 copy-start.3
  0.8 8.8 %copy-start.4 = (s32[2048]{0:T(1024)S(1)}, s32[2048]{0:T(1024)}, u32[]{:S(2)}) copy-start(s32[2048]{0:T(1024)} %param.8) | copy-start | bytes 24580
  0.8 20.3 %copy-start.5 = (bf16[144,2048]{1,0:T(8,128)(2,1)S(1)}, bf16[144,2048]{1,0:T(8,128)(2,1)}, u32[]{:S(2)}) copy-start(bf16[144,2048]{1,0:T(8,128)(2,1)} %alpha_hbm.1) | copy-start | bytes 1769476
  1.6 19.5 %all-to-all-start = ((bf16[16,64,256]{2,1,0:T(8,128)(2,1)}), bf16[16,64,256]{2,1,0:T(8,128)(2,1)S(1)}, u32[]{:S(2)}, u32[]{:S(2)}) async-start(bf16[16,64,256]{2,1,0:T(8,128)(2,1)} %copies.1), calls=%async_computation | async-start | bytes 1048576 | tf_op jit(solution)/shard_map/all_to_all | solution.py:583
  56.9 2.1 %collective-permute-start = (f32[144,1024]{1,0:T(8,128)S(1)}, f32[144,1024]{1,0:T(8,128)S(1)}, u32[]{:S(2)}, u32[]{:S(2)}) collective-permute-start(f32[144,1024]{1,0:T(8,128)S(1)} %get-tuple-element.60), channel_id=1, source_target_pairs={{0,16},{16,0},{32,48},{48,32},{64,80},{80,64},{96,112},{112,96},{1... | collective-permute-start | bytes 1769480 | tf_op jit(solution)/shard_map/ppermute | solution.py:580
  59.4 6.3 %collective-permute-start.1 = (f16[160,512]{1,0:T(8,128)(2,1)S(1)}, f16[160,512]{1,0:T(8,128)(2,1)S(1)}, u32[]{:S(2)}, u32[]{:S(2)}) collective-permute-start(f16[160,512]{1,0:T(8,128)(2,1)S(1)} %get-tuple-element.101), channel_id=1, source_target_pairs={{0,32},{16,48},{32,0},{48,16},{64,96},{80,112},{96,64},{112,80},{1... | collective-permute-start | bytes 491528 | tf_op jit(solution)/shard_map/ppermute | solution.py:577
  61.2 8.2 %collective-permute-start.3 = (f16[160,512]{1,0:T(8,128)(2,1)S(1)}, f16[160,512]{1,0:T(8,128)(2,1)S(1)}, u32[]{:S(2)}, u32[]{:S(2)}) collective-permute-start(f16[160,512]{1,0:T(8,128)(2,1)S(1)} %get-tuple-element.97), channel_id=1, source_target_pairs={{0,96},{16,112},{32,64},{48,80},{64,32},{80,48},{96,0},{112,16},{1... | collective-permute-start | bytes 491528 | tf_op jit(solution)/shard_map/ppermute | solution.py:577
  66.3 4.1 %copy-start.1 = (f32[2048,256]{1,0:T(8,128)S(1)}, f32[2048,256]{1,0:T(8,128)}, u32[]{:S(2)}) copy-start(f32[2048,256]{1,0:T(8,128)} %precond_ref.1) | copy-start | bytes 6291460
  66.3 6.8 %collective-permute-start.2 = (f16[160,512]{1,0:T(8,128)(2,1)S(1)}, f16[160,512]{1,0:T(8,128)(2,1)S(1)}, u32[]{:S(2)}, u32[]{:S(2)}) collective-permute-start(f16[160,512]{1,0:T(8,128)(2,1)S(1)} %get-tuple-element.99), channel_id=1, source_target_pairs={{0,96},{16,112},{32,64},{48,80},{64,32},{80,48},{96,0},{112,16},{1... | collective-permute-start | bytes 491528 | tf_op jit(solution)/shard_map/ppermute | solution.py:577
  69.9 5.6 %collective-permute-start.4 = (f16[160,512]{1,0:T(8,128)(2,1)S(1)}, f16[160,512]{1,0:T(8,128)(2,1)S(1)}, u32[]{:S(2)}, u32[]{:S(2)}) collective-permute-start(f16[160,512]{1,0:T(8,128)(2,1)S(1)} %get-tuple-element.95), channel_id=1, source_target_pairs={{0,32},{16,48},{32,0},{48,16},{64,96},{80,112},{96,64},{112,80},{1... | collective-permute-start | bytes 491528 | tf_op jit(solution)/shard_map/ppermute | solution.py:577
  76.6 1.7 collective-permute-start.5
  76.7 1.6 collective-permute-start.6
  114.0 2.1 %collective-permute-start.7 = (f32[152,1024]{1,0:T(8,128)S(1)}, f32[152,1024]{1,0:T(8,128)S(1)}, u32[]{:S(2)}, u32[]{:S(2)}) collective-permute-start(f32[152,1024]{1,0:T(8,128)S(1)} %get-tuple-element.75), channel_id=1, source_target_pairs={{0,16},{16,0},{32,48},{48,32},{64,80},{80,64},{96,112},{112,96},{1... | collective-permute-start | bytes 1867784 | tf_op jit(solution)/shard_map/ppermute | solution.py:580
  116.6 6.3 %collective-permute-start.8 = (f16[160,512]{1,0:T(8,128)(2,1)S(1)}, f16[160,512]{1,0:T(8,128)(2,1)S(1)}, u32[]{:S(2)}, u32[]{:S(2)}) collective-permute-start(f16[160,512]{1,0:T(8,128)(2,1)S(1)} %get-tuple-element.93), channel_id=1, source_target_pairs={{0,32},{16,48},{32,0},{48,16},{64,96},{80,112},{96,64},{112,80},{1... | collective-permute-start | bytes 491528 | tf_op jit(solution)/shard_map/ppermute | solution.py:577
  117.0 7.8 %collective-permute-start.10 = (f16[160,512]{1,0:T(8,128)(2,1)S(1)}, f16[160,512]{1,0:T(8,128)(2,1)S(1)}, u32[]{:S(2)}, u32[]{:S(2)}) collective-permute-start(f16[160,512]{1,0:T(8,128)(2,1)S(1)} %get-tuple-element.89), channel_id=1, source_target_pairs={{0,96},{16,112},{32,64},{48,80},{64,32},{80,48},{96,0},{112,16},{1... | collective-permute-start | bytes 491528 | tf_op jit(solution)/shard_map/ppermute | solution.py:577
  123.5 6.7 %collective-permute-start.9 = (f16[160,512]{1,0:T(8,128)(2,1)S(1)}, f16[160,512]{1,0:T(8,128)(2,1)S(1)}, u32[]{:S(2)}, u32[]{:S(2)}) collective-permute-start(f16[160,512]{1,0:T(8,128)(2,1)S(1)} %get-tuple-element.91), channel_id=1, source_target_pairs={{0,96},{16,112},{32,64},{48,80},{64,32},{80,48},{96,0},{112,16},{1... | collective-permute-start | bytes 491528 | tf_op jit(solution)/shard_map/ppermute | solution.py:577
  125.4 5.4 %collective-permute-start.11 = (f16[160,512]{1,0:T(8,128)(2,1)S(1)}, f16[160,512]{1,0:T(8,128)(2,1)S(1)}, u32[]{:S(2)}, u32[]{:S(2)}) collective-permute-start(f16[160,512]{1,0:T(8,128)(2,1)S(1)} %get-tuple-element.87), channel_id=1, source_target_pairs={{0,32},{16,48},{32,0},{48,16},{64,96},{80,112},{96,64},{112,80},{1... | collective-permute-start | bytes 491528 | tf_op jit(solution)/shard_map/ppermute | solution.py:577
  132.0 1.7 collective-permute-start.12
  132.1 1.6 collective-permute-start.13

commit v5 on v4

--- a/solution.py
+++ b/solution.py
@@ -16,6 +16,7 @@
 DEPTH = 128
 BAND = 256
 EXTRA = 16
+SCALARS = 8
 LANES = 128
 NT = (((1,), (1,)), ((), ()))
 TN = (((0,), (0,)), ((), ()))
@@ -81,17 +82,21 @@
 
 
 def half_rows(powers, vectors):
-    row = lax.broadcasted_iota(jnp.int32, (EXTRA, LANES), 0)
-    out = jnp.zeros((EXTRA, LANES), F32)
+    row = lax.broadcasted_iota(jnp.int32, (SCALARS, LANES), 0)
+    lane = lax.broadcasted_iota(jnp.int32, (SCALARS, LANES), 1)
+    out = jnp.zeros((SCALARS, LANES), F32)
     for p, piece in enumerate(half_pieces(powers, vectors)):
-        for q in range(2):
-            out = jnp.where(row == 2 * p + q, piece[:, q * LANES : (q + 1) * LANES], out)
+        out = jnp.where(row == p, piece[:, :LANES], out)
+        rest = piece[:, LANES : LANES + 16]
+        rest = jnp.concatenate([rest] * (LANES // 16), axis=1)
+        out = jnp.where((row == SCALARS - 1) & (lane // 16 == p), rest, out)
     return out
 
 
 def half_row(parts_ref, first, p):
-    rows = [parts_ref[:, first + 2 * p + q, :] for q in range(2)]
-    return jnp.concatenate(rows, axis=1)
+    rest = parts_ref[:, first + SCALARS - 1, :][:, 16 * p : 16 * p + 16]
+    empty = jnp.zeros((parts_ref.shape[0], LANES - 16), F32)
+    return jnp.concatenate([parts_ref[:, first + p, :], rest, empty], axis=1)
 
 
 def half_vector(parts_ref, first, k):
@@ -146,14 +151,17 @@
 
 
 def copies_kernel(block_ref, copies_ref):
+    features, lanes = block_ref.shape
     for k in range(copies_ref.shape[0]):
-        copies_ref[k] = block_ref[...]
+        for q in range(lanes // LANES):
+            copies_ref[k, q * features : (q + 1) * features] = block_ref[
+                :, q * LANES : (q + 1) * LANES
+            ]
 
 
 def copies(block, number):
-    return call(copies_kernel, "copies", shape((number,) + block.shape, block.dtype), 1 << 20, arrays=1)(
-        block
-    )
+    out = shape((number, block.size // LANES, LANES), block.dtype)
+    return call(copies_kernel, "copies", out, 1 << 20, arrays=1)(block)
 
 
 def prepare_kernel(index_ref, centers_ref, sides_ref, one_hot_ref, chunk_ref):
@@ -187,11 +195,19 @@
 ):
     fetch = pltpu.make_async_copy(alpha_hbm, alpha_ref, alpha_sem)
     fetch.start()
-    chunks, features, lanes = pool_ref.shape
+    chunks, height, _ = pool_ref.shape
+    lanes = one_hot_ref.shape[0]
+    features = height * LANES // lanes
     count, examples = tile_ref.shape
     share = rows_ref.shape[2]
     scale = 4.0 / features * math.log2(math.e)
-    pool = pool_ref[...].reshape(chunks * features, lanes)
+    pool = jnp.concatenate(
+        [
+            pool_ref[:, q * features : (q + 1) * features, :].reshape(chunks * features, LANES)
+            for q in range(lanes // LANES)
+        ],
+        axis=1,
+    )
     for b in range(examples // BAND):
         here = slice(b * BAND, (b + 1) * BAND)
         chunk = chunk_ref[:, here]
@@ -274,13 +290,20 @@
     return jnp.concatenate(out, axis=1)
 
 
+def forward_own_kernel(core_ref, own_ref, tile_ref, first_ref):
+    half = own_ref.shape[1]
+    mine = pl.ds(pl.multiple_of(core_ref[0] * half, half), half)
+    for b in range(first_ref.shape[1] // BAND):
+        here = slice(b * BAND, (b + 1) * BAND)
+        first_ref[:, here] = jnp.dot(own_ref[...], tile_ref[mine, here], preferred_element_type=F32)
+
+
 def forward_kernel(
-    core_ref, own_ref, other_ref, own_part_ref, other_part_ref, tile_ref, rows_ref
+    core_ref, first_ref, other_ref, own_part_ref, other_part_ref, tile_ref, rows_ref
 ):
-    classes, half = own_ref.shape
+    classes, half = other_ref.shape
     share = rows_ref.shape[2]
     examples = tile_ref.shape[1]
-    mine = pl.ds(pl.multiple_of(core_ref[0] * half, half), half)
     theirs = pl.ds(pl.multiple_of((1 - core_ref[0]) * half, half), half)
     part = own_part_ref[...] + other_part_ref[...]
     powers = exponents(part[2:3]) - 14.0
@@ -288,63 +311,91 @@
     scales = column(jnp.exp2(-powers), classes)
     for b in range(examples // BAND):
         here = slice(b * BAND, (b + 1) * BAND)
-        rows = jnp.dot(own_ref[...], tile_ref[mine, here], preferred_element_type=F32)
-        rows += jnp.dot(other_ref[...], tile_ref[theirs, here], preferred_element_type=F32)
-        rows *= scales
+        rows = jnp.dot(other_ref[...], tile_ref[theirs, here], preferred_element_type=F32)
+        rows = (rows + first_ref[:, here]) * scales
         for k in range(BAND // share):
             at = b * (BAND // share) + k
             rows_ref[at, :classes] = rows[:, k * share : (k + 1) * share]
             rows_ref[at, classes:] = extra
 
 
-def forward(core, own, other, own_part, other_part, tile, share):
-    classes = own.shape[0]
-    shares = tile.shape[1] // share
+def forward(core, lifted, other, own_part, other_part, tile, share):
+    classes = lifted.shape[0]
+    examples = tile.shape[1]
+    first = call(
+        forward_own_kernel,
+        "forward_own",
+        shape((classes, examples), F32),
+        604 << 20,
+        scalars=1,
+        arrays=2,
+    )(core, lifted, tile)
     return call(
         forward_kernel,
         "forward",
-        shape((shares, classes + EXTRA, share), F32),
-        1208 << 20,
+        shape((examples // share, classes + SCALARS, share), F32),
+        604 << 20,
         scalars=1,
         arrays=5,
-    )(core, own, other, own_part, other_part, tile)
-
-
-def backward_kernel(core_ref, values_ref, turned_ref, other_ref, own_ref, flat_ref):
+    )(core, first, other, own_part, other_part, tile)
+
+
+def backward_other_kernel(core_ref, values_ref, turned_ref, other_ref, flat_ref, row_ref):
     shares, height, share = values_ref.shape
     classes, examples = flat_ref.shape
     half = other_ref.shape[1]
     for k in range(shares):
         flat_ref[:, k * share : (k + 1) * share] = values_ref[k, :classes]
+    row = jnp.zeros((8, 2 * LANES), F32)
     if height > classes:
         total = values_ref[0, classes:].astype(F32)
         for k in range(1, shares):
             total = total + values_ref[k, classes:].astype(F32)
         row = jnp.broadcast_to(read_rows(total, 0), (8, 2 * LANES))
-        for ref in (other_ref, own_ref):
-            ref[classes:, : 2 * LANES] = row
-            ref[classes:, 2 * LANES :] = jnp.zeros((8, half - 2 * LANES), F32)
-    for first, ref in (((1 - core_ref[0]) * half, other_ref), (core_ref[0] * half, own_ref)):
-        for b in range(half // BAND):
-            there = pl.ds(pl.multiple_of(first + b * BAND, BAND), BAND)
-            ref[:classes, b * BAND : (b + 1) * BAND] = jnp.dot(
-                flat_ref[...], turned_ref[:, there], preferred_element_type=F32
-            )
-
-
-def backward(core, values, turned, classes):
+    row_ref[...] = row
+    other_ref[classes:, : 2 * LANES] = row
+    other_ref[classes:, 2 * LANES :] = jnp.zeros((8, half - 2 * LANES), F32)
+    for b in range(half // BAND):
+        there = pl.ds(pl.multiple_of((1 - core_ref[0]) * half + b * BAND, BAND), BAND)
+        other_ref[:classes, b * BAND : (b + 1) * BAND] = jnp.dot(
+            flat_ref[...], turned_ref[:, there], preferred_element_type=F32
+        )
+
+
+def backward_own_kernel(core_ref, flat_ref, turned_ref, own_ref):
+    half = own_ref.shape[1]
+    for b in range(half // BAND):
+        there = pl.ds(pl.multiple_of(core_ref[0] * half + b * BAND, BAND), BAND)
+        own_ref[:, b * BAND : (b + 1) * BAND] = jnp.dot(
+            flat_ref[...], turned_ref[:, there], preferred_element_type=F32
+        )
+
+
+def backward_other(core, values, turned, classes):
     examples, count = turned.shape
-    height = classes + (8 if values.shape[1] > classes else 0)
-    half = shape((height, count // 2), F32)
-    return call(
-        backward_kernel,
-        "backward",
-        [half, half],
-        1208 << 20,
-        [pltpu.VMEM((classes, examples), BF16)],
+    return call(
+        backward_other_kernel,
+        "backward_other",
+        [
+            shape((classes + 8, count // 2), F32),
+            shape((classes, examples), BF16),
+            shape((8, 2 * LANES), F32),
+        ],
+        604 << 20,
         scalars=1,
         arrays=2,
     )(core, values, turned)
+
+
+def backward_own(core, flat, turned):
+    return call(
+        backward_own_kernel,
+        "backward_own",
+        shape((flat.shape[0], turned.shape[1] // 2), F32),
+        604 << 20,
+        scalars=1,
+        arrays=2,
+    )(core, flat, turned)
 
 
 def pack_halves(ref, values, vectors):
@@ -373,20 +424,17 @@
     return jnp.exp2(power) * (high + low / 2048.0)
 
 
-def join_kernel(own_ref, got_ref, one_ref, two_ref):
-    classes, wide = one_ref.shape[0] - EXTRA, one_ref.shape[1]
+def join_kernel(own_ref, row_ref, got_ref, one_ref, two_ref):
+    classes, wide = own_ref.shape[0], one_ref.shape[1]
     for k, ref in enumerate((one_ref, two_ref)):
         here = slice(k * wide, (k + 1) * wide)
-        vectors = []
-        if k == 0 and own_ref.shape[0] > classes:
-            row = slice(classes, classes + 1)
-            vectors = [own_ref[row, : 2 * LANES] + got_ref[row, : 2 * LANES]]
-        pack_halves(ref, own_ref[:classes, here] + got_ref[:classes, here], vectors)
-
-
-def join(own, got, classes):
-    half = shape((classes + EXTRA, own.shape[1] // 2), F32)
-    return call(join_kernel, "join", [half, half], 1 << 20, arrays=2)(own, got)
+        vectors = [row_ref[:1] + got_ref[classes : classes + 1, : 2 * LANES]] if k == 0 else []
+        pack_halves(ref, own_ref[:, here] + got_ref[:classes, here], vectors)
+
+
+def join(own, row, got):
+    half = shape((own.shape[0] + EXTRA, own.shape[1] // 2), F32)
+    return call(join_kernel, "join", [half, half], 1 << 20, arrays=3)(own, row, got)
 
 
 def add_kernel(own_ref, got_ref, sum_ref):
@@ -468,7 +516,11 @@
     return call(
         weigh_kernel,
         "weigh",
-        [shape(hessian.shape, F32), shape((8, 2 * LANES), F32), shape(parts.shape, BF16)],
+        [
+            shape(hessian.shape, F32),
+            shape((8, 2 * LANES), F32),
+            shape((parts.shape[0], hessian.shape[0] + EXTRA, hessian.shape[1]), BF16),
+        ],
         1 << 20,
         arrays=2,
     )(parts, hessian)
@@ -528,7 +580,7 @@
     )
     rows = column(grown, classes) * last + column(ratio - excess, classes) * image_ref[...]
     weighted = (hessian_ref[...] * rows).astype(BF16).astype(F32)
-    curve_ref[...] = stack_rows([lane_sums(weighted * rows)])
+    curve_ref[...] = lane_sums(weighted * rows)
 
 
 def last_curve(parts, hessian, image, norm, rough):
@@ -536,7 +588,7 @@
     return call(
         curve_kernel,
         "curve",
-        [shape(hessian.shape, F32), row, row],
+        [shape(hessian.shape, F32), row, shape((1, 2 * LANES), F32)],
         1 << 20,
         arrays=5,
     )(parts, hessian, image, norm, rough)
@@ -589,8 +641,8 @@
         array = lax.reduce_precision(array, 5, 10)
         return array, over_y(array.astype(F16), flip).astype(F32)
 
-    def sum_examples(own, got):
-        one, two = join(own, got, classes)
+    def sum_examples(own, row, got):
+        one, two = join(own, row, got)
         one, two = swap(one, 1), swap(two, 3)
         one, two = add_halves(*one), add_halves(*two)
         return *swap(one, 3), *swap(two, 1)
@@ -608,17 +660,19 @@
     base = jnp.sum(trade_halves(rows), axis=0)
     hessian, send = gradient(base, label, weight, n_ctr)
 
-    other, own = backward(core, trade(send), turned, classes)
+    other, flat, row = backward_other(core, trade(send), turned, classes)
     got = over_cores(other)
+    own = backward_own(core, flat, turned)
     got, late_core = lax.optimization_barrier((got, core))
     blocks = factors(late_core, precond)
-    sums = sum_examples(own, got)
+    sums = sum_examples(own, row, got)
     residual, lifted, part = first_residual(total, sums, blocks)
     rows = forward(core, lifted, over_cores(lifted), part, over_cores(part), tile, share)
     image, norm, send = weigh(trade_halves(rows), hessian)
 
-    other, own = backward(core, trade(send), turned, classes)
-    sums = sum_examples(own, over_cores(other))
+    other, flat, row = backward_other(core, trade(send), turned, classes)
+    got = over_cores(other)
+    sums = sum_examples(backward_own(core, flat, turned), row, got)
     lifted, part, rough = step(total, sums, blocks, residual, norm)
     rows = forward(core, lifted, over_cores(lifted), part, over_cores(part), tile, share)
     last, scales, curve = last_curve(trade_halves(rows), hessian, image, norm, rough)

time: 174 us -> 170 us (0.977)
  waiting for transfers between devices: 33 us -> 29.9 us
    ppermute x6, waiting for transfers between devices: 6.2 us -> 3 us  [over_cores(): return lax.ppermute(array, 'ex', core_pairs)]
    pallas_call x8 -> x12, Pallas kernels: 7.85 us -> 8.89 us  [the longest x2 1.74 us: forward(): call(forward_kernel, 'forward', shape((examples // share, classes + SCALA...]
  transfers between devices with their start and end apart: 15 -> 15, of which waited for: 11 -> 11; matrix products, arithmetic and copies ran while one was open for 1% -> 1% of each run, Pallas kernels for 1% -> 3%
where the time goes in v5:
time: 170 us
  blocking collectives  94.7 us (56%)
  waiting for transfers between devices  29.9 us (18%)
  Pallas kernels  21.1 us (12%)
  starting transfers between devices  19.7 us (12%)
  other arithmetic  2.13 us (1%)
    all_to_all x6, blocking collectives, trade(): return lax.all_to_all(parts, 'ctr', 0, 0)  86.4 us
    ppermute x8, waiting for transfers between devices, over_y(): return lax.ppermute(array, 'ex', pairs)  16.9 us
    ppermute x8, starting transfers between devices, over_y(): return lax.ppermute(array, 'ex', pairs)  10.4 us
    all_to_all x1, waiting for transfers between devices, trade(): return lax.all_to_all(parts, 'ctr', 0, 0)  9.98 us
    all_to_all x1, blocking collectives, shards(): lax.all_to_all(jnp.broadcast_to(curve, (n_ex,) + curve.shape), 'ex', 0, 0)  8.35 us
    all_to_all x1, starting transfers between devices, trade(): return lax.all_to_all(parts, 'ctr', 0, 0)  7.96 us
    pallas_call x1, Pallas kernels, make_tile(): call(tile_kernel, 'tile', [shape((count, examples), BF16), shape((example...  5.91 us
  transfers between devices with their start and end apart: 15, of which 11 were waited for; matrix products, arithmetic and copies ran while one was open for 1% of the time, Pallas kernels for 3%

profile of v5, /device:TPU:0, one launch (start us, length us, event | category | flops | bytes accessed | tf_op | source)
XLA Modules:
  0.0 169.5 jit_solution(14905125448318449945)
XLA Ops:
  0.0 0.8 copy-done.3
  0.8 0.9 copies.1
  1.7 8.0 %all-to-all-start = ((bf16[16,128,128]{2,1,0:T(8,128)(2,1)}), bf16[16,128,128]{2,1,0:T(8,128)(2,1)S(1)}, u32[]{:S(2)}, u32[]{:S(2)}) async-start(bf16[16,128,128]{2,1,0:T(8,128)(2,1)} %copies.1), calls=%async_computation | async-start | bytes 1048576 | tf_op jit(solution)/shard_map/all_to_all | solution.py:635
  9.7 0.7 prepare.1
  10.4 0.8 dynamic-slice_bitcast_fusion.weight_ref
  11.2 10.0 %all-to-all-done.pool_ref = bf16[16,128,128]{2,1,0:T(8,128)(2,1)S(1)} async-done(((bf16[16,128,128]{2,1,0:T(8,128)(2,1)}), bf16[16,128,128]{2,1,0:T(8,128)(2,1)S(1)}, u32[]{:S(2)}, u32[]{:S(2)}) %all-to-all-start) | async-done | bytes 524320 | tf_op jit(solution)/shard_map/all_to_all | solution.py:635
  21.2 5.9 %tile.1 = (bf16[2048,2048]{1,0:T(8,128)(2,1)S(1)}, bf16[2048,2048]{1,0:T(8,128)(2,1)S(1)}, f32[16,144,128]{2,1,0:T(8,128)S(1)}) custom-call(bf16[144,2048]{1,0:T(8,128)(2,1)S(1)} %copy-done.5, s32[1,2048]{1,0:T(1,128)S(1)} %get-tuple-element.52.chunk_ref, bf16[16,128,128]{2,1,0:T(8,128)(2,1)S(1)} %all-to-all-done.pool_ref, ...), custom_call_target="tpu_custom_call" | custom-call | flops 4294967296 | bytes 17956864 | tf_op jit(solution)/shard_map/tile/pallas_call | solution.py:238
  27.2 14.4 %all_to_all.40 = f16[16,144,128]{2,1,0:T(8,128)(2,1)S(1)} all-to-all(f16[16,144,128]{2,1,0:T(8,128)(2,1)S(1)} %convert_element_type.66), channel_id=1, replica_groups=mesh['ex'=8,'ctr'=16] {'ctr'}, dimensions={0} | all-to-all | bytes 1179648 | tf_op jit(solution)/shard_map/all_to_all | solution.py:635
  41.8 13.7 %all_to_all.41.values_ref = bf16[16,144,128]{2,1,0:T(8,128)(2,1)S(1)} all-to-all(bf16[16,144,128]{2,1,0:T(8,128)(2,1)S(1)} %get-tuple-element.59), channel_id=1, replica_groups=mesh['ex'=8,'ctr'=16] {'ctr'}, dimensions={0} | all-to-all | bytes 1179648 | tf_op jit(solution)/shard_map/all_to_all | solution.py:635
  55.4 0.8 backward_other.2
  56.3 0.1 collective-permute-start
  56.4 0.8 backward_own.2.own_ref
  57.2 1.2 collective-permute-done.got_ref
  58.4 0.2 join.2
  58.6 0.2 reduce-precision_convert_fusion.7
  58.8 1.7 collective-permute-start.1
  60.4 0.2 reduce-precision_convert_fusion.5
  60.6 2.3 %collective-permute-start.3 = (f16[160,512]{1,0:T(8,128)(2,1)S(1)}, f16[160,512]{1,0:T(8,128)(2,1)S(1)}, u32[]{:S(2)}, u32[]{:S(2)}) collective-permute-start(f16[160,512]{1,0:T(8,128)(2,1)S(1)} %get-tuple-element.101), channel_id=1, source_target_pairs={{0,96},{16,112},{32,64},{48,80},{64,32},{80,48},{96,0},{112,16},{1... | collective-permute-start | bytes 491528 | tf_op jit(solution)/shard_map/ppermute | solution.py:629
  62.9 2.2 %collective-permute-done.1 = f16[160,512]{1,0:T(8,128)(2,1)S(1)} collective-permute-done((f16[160,512]{1,0:T(8,128)(2,1)S(1)}, f16[160,512]{1,0:T(8,128)(2,1)S(1)}, u32[]{:S(2)}, u32[]{:S(2)}) %collective-permute-start.1) | collective-permute-done | bytes 163872 | tf_op jit(solution)/shard_map/ppermute | solution.py:629
  65.1 0.4 add.14
  65.5 0.2 reduce-precision_convert_fusion.6
  65.7 3.1 %collective-permute-start.2 = (f16[160,512]{1,0:T(8,128)(2,1)S(1)}, f16[160,512]{1,0:T(8,128)(2,1)S(1)}, u32[]{:S(2)}, u32[]{:S(2)}) collective-permute-start(f16[160,512]{1,0:T(8,128)(2,1)S(1)} %get-tuple-element.103), channel_id=1, source_target_pairs={{0,96},{16,112},{32,64},{48,80},{64,32},{80,48},{96,0},{112,16},{1... | collective-permute-start | bytes 491528 | tf_op jit(solution)/shard_map/ppermute | solution.py:629
  68.8 0.4 add.15
  69.2 0.2 reduce-precision_convert_fusion.4
  69.4 0.4 collective-permute-start.4
  69.8 0.3 factors.1
  70.1 2.3 %collective-permute-done.2 = f16[160,512]{1,0:T(8,128)(2,1)S(1)} collective-permute-done((f16[160,512]{1,0:T(8,128)(2,1)S(1)}, f16[160,512]{1,0:T(8,128)(2,1)S(1)}, u32[]{:S(2)}, u32[]{:S(2)}) %collective-permute-start.2) | collective-permute-done | bytes 163872 | tf_op jit(solution)/shard_map/ppermute | solution.py:629
  72.5 2.4 %collective-permute-done.4 = f16[160,512]{1,0:T(8,128)(2,1)S(1)} collective-permute-done((f16[160,512]{1,0:T(8,128)(2,1)S(1)}, f16[160,512]{1,0:T(8,128)(2,1)S(1)}, u32[]{:S(2)}, u32[]{:S(2)}) %collective-permute-start.4) | collective-permute-done | bytes 163872 | tf_op jit(solution)/shard_map/ppermute | solution.py:629
  75.0 1.0 residual.1
  76.1 0.5 collective-permute-start.6
  76.6 0.8 forward_own.2.first_ref
  77.4 0.3 collective-permute-done.6.other_part_ref
  77.7 0.9 forward.2
  78.6 16.0 %all_to_all.42 = f16[16,152,128]{2,1,0:T(8,128)(2,1)S(1)} all-to-all(f16[16,152,128]{2,1,0:T(8,128)(2,1)S(1)} %convert_element_type.76), channel_id=1, replica_groups=mesh['ex'=8,'ctr'=16] {'ctr'}, dimensions={0} | all-to-all | bytes 1245184 | tf_op jit(solution)/shard_map/all_to_all | solution.py:635
  94.7 0.7 weigh.1
  95.4 15.7 %all_to_all.43.values_ref = bf16[16,160,128]{2,1,0:T(8,128)(2,1)S(1)} all-to-all(bf16[16,160,128]{2,1,0:T(8,128)(2,1)S(1)} %get-tuple-element.76), channel_id=1, replica_groups=mesh['ex'=8,'ctr'=16] {'ctr'}, dimensions={0} | all-to-all | bytes 1310720 | tf_op jit(solution)/shard_map/all_to_all | solution.py:635
  111.1 0.8 backward_other.3
  111.9 0.1 collective-permute-start.7
  112.0 0.8 backward_own.3.own_ref
  112.8 1.2 collective-permute-done.7.got_ref
  114.1 0.2 join.3
  114.3 0.2 reduce-precision_convert_fusion.3
  114.4 0.2 collective-permute-start.8
  114.7 0.2 reduce-precision_convert_fusion.1
  114.8 1.3 collective-permute-start.10
  116.1 4.7 %collective-permute-done.8 = f16[160,512]{1,0:T(8,128)(2,1)S(1)} collective-permute-done((f16[160,512]{1,0:T(8,128)(2,1)S(1)}, f16[160,512]{1,0:T(8,128)(2,1)S(1)}, u32[]{:S(2)}, u32[]{:S(2)}) %collective-permute-start.8) | collective-permute-done | bytes 163872 | tf_op jit(solution)/shard_map/ppermute | solution.py:629
  120.8 0.4 add.16
  121.2 0.2 reduce-precision_convert_fusion.2
  121.3 1.3 collective-permute-start.9
  122.7 0.4 add.17
  123.1 0.2 reduce-precision_convert_fusion
  123.2 0.2 collective-permute-start.11
  123.4 4.6 %collective-permute-done.9 = f16[160,512]{1,0:T(8,128)(2,1)S(1)} collective-permute-done((f16[160,512]{1,0:T(8,128)(2,1)S(1)}, f16[160,512]{1,0:T(8,128)(2,1)S(1)}, u32[]{:S(2)}, u32[]{:S(2)}) %collective-permute-start.9) | collective-permute-done | bytes 163872 | tf_op jit(solution)/shard_map/ppermute | solution.py:629
  128.1 0.6 collective-permute-done.11
  128.7 1.2 step.1
  129.9 0.5 collective-permute-start.13
  130.4 0.8 forward_own.3.first_ref
  131.2 0.3 collective-permute-done.13.other_part_ref
  131.5 0.9 forward.3
  132.5 16.0 %all_to_all.44 = f16[16,152,128]{2,1,0:T(8,128)(2,1)S(1)} all-to-all(f16[16,152,128]{2,1,0:T(8,128)(2,1)S(1)} %convert_element_type.86), channel_id=1, replica_groups=mesh['ex'=8,'ctr'=16] {'ctr'}, dimensions={0} | all-to-all | bytes 1245184 | tf_op jit(solution)/shard_map/all_to_all | solution.py:635
  148.6 0.9 curve.1
  149.5 8.4 %all_to_all.45 = f32[8,1,256]{2,1,0:T(1,128)S(1)} all-to-all(f32[8,1,256]{2,1,0:T(1,128)S(1)} %broadcast_in_dim.6), channel_id=1, replica_groups=mesh['ex'=8,'ctr'=16] {'ex'}, dimensions={0} | all-to-all | bytes 16384 | tf_op jit(solution)/shard_map/all_to_all | solution.py:680
  157.9 10.7 %all_to_all.46.curve_ref = f32[16,1,256]{2,1,0:T(1,128)S(1)} all-to-all(f32[16,1,256]{2,1,0:T(1,128)S(1)} %broadcast_in_dim.7), channel_id=1, replica_groups=mesh['ex'=8,'ctr'=16] {'ctr'}, dimensions={0} | all-to-all | bytes 32768 | tf_op jit(solution)/shard_map/all_to_all | solution.py:635
  168.6 0.9 margins.1
  (36 shorter events, 1.1 us)
Async XLA Ops:
  0.0 10.4 %copy-start = (s32[2048]{0:T(1024)S(1)}, s32[2048]{0:T(1024)}, u32[]{:S(2)}) copy-start(s32[2048]{0:T(1024)} %param.9) | copy-start | bytes 24580
  0.0 9.7 %copy-start.2 = (bf16[64,2048]{1,0:T(8,128)(2,1)S(1)}, bf16[64,2048]{1,0:T(8,128)(2,1)}, u32[]{:S(2)}) copy-start(bf16[64,2048]{1,0:T(8,128)(2,1)} %centers_ref.1) | copy-start | bytes 786436
  0.0 0.8 copy-start.3
  0.8 8.9 %copy-start.4 = (s32[2048]{0:T(1024)S(1)}, s32[2048]{0:T(1024)}, u32[]{:S(2)}) copy-start(s32[2048]{0:T(1024)} %param.8) | copy-start | bytes 24580
  0.8 20.4 %copy-start.5 = (bf16[144,2048]{1,0:T(8,128)(2,1)S(1)}, bf16[144,2048]{1,0:T(8,128)(2,1)}, u32[]{:S(2)}) copy-start(bf16[144,2048]{1,0:T(8,128)(2,1)} %alpha_hbm.1) | copy-start | bytes 1769476
  1.7 19.5 %all-to-all-start = ((bf16[16,128,128]{2,1,0:T(8,128)(2,1)}), bf16[16,128,128]{2,1,0:T(8,128)(2,1)S(1)}, u32[]{:S(2)}, u32[]{:S(2)}) async-start(bf16[16,128,128]{2,1,0:T(8,128)(2,1)} %copies.1), calls=%async_computation | async-start | bytes 1048576 | tf_op jit(solution)/shard_map/all_to_all | solution.py:635
  56.3 2.1 %collective-permute-start = (f32[152,1024]{1,0:T(8,128)S(1)}, f32[152,1024]{1,0:T(8,128)S(1)}, u32[]{:S(2)}, u32[]{:S(2)}) collective-permute-start(f32[152,1024]{1,0:T(8,128)S(1)} %get-tuple-element.63), channel_id=1, source_target_pairs={{0,16},{16,0},{32,48},{48,32},{64,80},{80,64},{96,112},{112,96},{1... | collective-permute-start | bytes 1867784 | tf_op jit(solution)/shard_map/ppermute | solution.py:632
  58.8 6.3 %collective-permute-start.1 = (f16[160,512]{1,0:T(8,128)(2,1)S(1)}, f16[160,512]{1,0:T(8,128)(2,1)S(1)}, u32[]{:S(2)}, u32[]{:S(2)}) collective-permute-start(f16[160,512]{1,0:T(8,128)(2,1)S(1)} %get-tuple-element.105), channel_id=1, source_target_pairs={{0,32},{16,48},{32,0},{48,16},{64,96},{80,112},{96,64},{112,80},{1... | collective-permute-start | bytes 491528 | tf_op jit(solution)/shard_map/ppermute | solution.py:629
  60.6 8.2 %collective-permute-start.3 = (f16[160,512]{1,0:T(8,128)(2,1)S(1)}, f16[160,512]{1,0:T(8,128)(2,1)S(1)}, u32[]{:S(2)}, u32[]{:S(2)}) collective-permute-start(f16[160,512]{1,0:T(8,128)(2,1)S(1)} %get-tuple-element.101), channel_id=1, source_target_pairs={{0,96},{16,112},{32,64},{48,80},{64,32},{80,48},{96,0},{112,16},{1... | collective-permute-start | bytes 491528 | tf_op jit(solution)/shard_map/ppermute | solution.py:629
  65.7 4.1 %copy-start.1 = (f32[2048,256]{1,0:T(8,128)S(1)}, f32[2048,256]{1,0:T(8,128)}, u32[]{:S(2)}) copy-start(f32[2048,256]{1,0:T(8,128)} %precond_ref.1) | copy-start | bytes 6291460
  65.7 6.8 %collective-permute-start.2 = (f16[160,512]{1,0:T(8,128)(2,1)S(1)}, f16[160,512]{1,0:T(8,128)(2,1)S(1)}, u32[]{:S(2)}, u32[]{:S(2)}) collective-permute-start(f16[160,512]{1,0:T(8,128)(2,1)S(1)} %get-tuple-element.103), channel_id=1, source_target_pairs={{0,96},{16,112},{32,64},{48,80},{64,32},{80,48},{96,0},{112,16},{1... | collective-permute-start | bytes 491528 | tf_op jit(solution)/shard_map/ppermute | solution.py:629
  69.4 5.6 %collective-permute-start.4 = (f16[160,512]{1,0:T(8,128)(2,1)S(1)}, f16[160,512]{1,0:T(8,128)(2,1)S(1)}, u32[]{:S(2)}, u32[]{:S(2)}) collective-permute-start(f16[160,512]{1,0:T(8,128)(2,1)S(1)} %get-tuple-element.99), channel_id=1, source_target_pairs={{0,32},{16,48},{32,0},{48,16},{64,96},{80,112},{96,64},{112,80},{1... | collective-permute-start | bytes 491528 | tf_op jit(solution)/shard_map/ppermute | solution.py:629
  76.0 1.7 collective-permute-start.5
  76.1 1.6 collective-permute-start.6
  111.9 2.1 %collective-permute-start.7 = (f32[152,1024]{1,0:T(8,128)S(1)}, f32[152,1024]{1,0:T(8,128)S(1)}, u32[]{:S(2)}, u32[]{:S(2)}) collective-permute-start(f32[152,1024]{1,0:T(8,128)S(1)} %get-tuple-element.79), channel_id=1, source_target_pairs={{0,16},{16,0},{32,48},{48,32},{64,80},{80,64},{96,112},{112,96},{1... | collective-permute-start | bytes 1867784 | tf_op jit(solution)/shard_map/ppermute | solution.py:632
  114.4 6.3 %collective-permute-start.8 = (f16[160,512]{1,0:T(8,128)(2,1)S(1)}, f16[160,512]{1,0:T(8,128)(2,1)S(1)}, u32[]{:S(2)}, u32[]{:S(2)}) collective-permute-start(f16[160,512]{1,0:T(8,128)(2,1)S(1)} %get-tuple-element.97), channel_id=1, source_target_pairs={{0,32},{16,48},{32,0},{48,16},{64,96},{80,112},{96,64},{112,80},{1... | collective-permute-start | bytes 491528 | tf_op jit(solution)/shard_map/ppermute | solution.py:629
  114.8 7.8 %collective-permute-start.10 = (f16[160,512]{1,0:T(8,128)(2,1)S(1)}, f16[160,512]{1,0:T(8,128)(2,1)S(1)}, u32[]{:S(2)}, u32[]{:S(2)}) collective-permute-start(f16[160,512]{1,0:T(8,128)(2,1)S(1)} %get-tuple-element.93), channel_id=1, source_target_pairs={{0,96},{16,112},{32,64},{48,80},{64,32},{80,48},{96,0},{112,16},{1... | collective-permute-start | bytes 491528 | tf_op jit(solution)/shard_map/ppermute | solution.py:629
  121.3 6.7 %collective-permute-start.9 = (f16[160,512]{1,0:T(8,128)(2,1)S(1)}, f16[160,512]{1,0:T(8,128)(2,1)S(1)}, u32[]{:S(2)}, u32[]{:S(2)}) collective-permute-start(f16[160,512]{1,0:T(8,128)(2,1)S(1)} %get-tuple-element.95), channel_id=1, source_target_pairs={{0,96},{16,112},{32,64},{48,80},{64,32},{80,48},{96,0},{112,16},{1... | collective-permute-start | bytes 491528 | tf_op jit(solution)/shard_map/ppermute | solution.py:629
  123.2 5.4 %collective-permute-start.11 = (f16[160,512]{1,0:T(8,128)(2,1)S(1)}, f16[160,512]{1,0:T(8,128)(2,1)S(1)}, u32[]{:S(2)}, u32[]{:S(2)}) collective-permute-start(f16[160,512]{1,0:T(8,128)(2,1)S(1)} %get-tuple-element.91), channel_id=1, source_target_pairs={{0,32},{16,48},{32,0},{48,16},{64,96},{80,112},{96,64},{112,80},{1... | collective-permute-start | bytes 491528 | tf_op jit(solution)/shard_map/ppermute | solution.py:629
  129.9 1.7 collective-permute-start.12
  129.9 1.6 collective-permute-start.13

commit v6 on v5

--- a/solution.py
+++ b/solution.py
@@ -405,21 +405,21 @@
     ref[:classes] = values * jnp.exp2(-powers)
     empty = jnp.zeros((2 * LANES - classes, LANES), F32)
     powers = jnp.concatenate([jnp.broadcast_to(powers, (classes, LANES)), empty], axis=0).T[:1]
-    row = lax.broadcasted_iota(jnp.int32, (EXTRA, 2 * LANES), 0)
-    out = jnp.zeros((EXTRA, 2 * LANES), F32)
+    row = lax.broadcasted_iota(jnp.int32, (SCALARS, 2 * LANES), 0)
+    out = jnp.zeros((SCALARS, 2 * LANES), F32)
     for p, piece in enumerate(half_pieces(powers, vectors)):
         out = jnp.where(row == p, piece, out)
     ref[classes:, : 2 * LANES] = out
-    ref[classes:, 2 * LANES :] = jnp.zeros((EXTRA, wide - 2 * LANES), F32)
+    ref[classes:, 2 * LANES :] = jnp.zeros((SCALARS, wide - 2 * LANES), F32)
 
 
 def unpack_halves(ref):
-    classes = ref.shape[0] - EXTRA
+    classes = ref.shape[0] - SCALARS
     return ref[:classes] * column(jnp.exp2(ref[classes : classes + 1, : 2 * LANES]), classes)
 
 
 def unpack_vector(ref):
-    classes = ref.shape[0] - EXTRA
+    classes = ref.shape[0] - SCALARS
     power, high, low = (ref[classes + p : classes + p + 1, : 2 * LANES] for p in range(1, 4))
     return jnp.exp2(power) * (high + low / 2048.0)
 
@@ -433,7 +433,7 @@
 
 
 def join(own, row, got):
-    half = shape((own.shape[0] + EXTRA, own.shape[1] // 2), F32)
+    half = shape((own.shape[0] + SCALARS, own.shape[1] // 2), F32)
     return call(join_kernel, "join", [half, half], 1 << 20, arrays=3)(own, row, got)
 
 
@@ -486,7 +486,7 @@
 
 
 def first_residual(total, sums, blocks):
-    classes, wide = sums[2].shape[0] - EXTRA, sums[2].shape[1]
+    classes, wide = sums[2].shape[0] - SCALARS, sums[2].shape[1]
     return call(
         functools.partial(residual_kernel, total),
         "residual",
@@ -677,9 +677,8 @@
     rows = forward(core, lifted, over_cores(lifted), part, over_cores(part), tile, share)
     last, scales, curve = last_curve(trade_halves(rows), hessian, image, norm, rough)
 
-    curve = lax.all_to_all(jnp.broadcast_to(curve, (n_ex,) + curve.shape), "ex", 0, 0)
-    curve = jnp.sum(curve, axis=0)
-    curve = trade(jnp.broadcast_to(curve, (n_ctr,) + curve.shape))
+    curve = jnp.broadcast_to(curve, (n_ex * n_ctr,) + curve.shape)
+    curve = lax.all_to_all(curve, ("ex", "ctr"), 0, 0)
     return margins(total, curve, scales, base, image, last)
 
 

time: 170 us -> 166 us (0.976)
  blocking collectives: 94.7 us -> 90.6 us
    all_to_all x6 -> x5, blocking collectives: 86.4 us -> 75.7 us  [trade(): return lax.all_to_all(parts, 'ctr', 0, 0)]
    all_to_all x1, blocking collectives: 8.35 us -> 14.9 us  [shards(): curve = lax.all_to_all(curve, ('ex', 'ctr'), 0, 0)]
where the time goes in v6:
time: 166 us; the launch traced here: 165 us
  blocking collectives  90.6 us (55%)
  waiting for transfers between devices  29.4 us (18%)
  Pallas kernels  21.2 us (13%)
  starting transfers between devices  19.7 us (12%)
  other arithmetic  2.02 us (1%)
  local copies, waits for them, and re-layouts  1.74 us (1%)
    all_to_all x5, blocking collectives, trade(): return lax.all_to_all(parts, 'ctr', 0, 0)  75.7 us
    ppermute x8, waiting for transfers between devices, over_y(): return lax.ppermute(array, 'ex', pairs)  16.4 us
    all_to_all x1, blocking collectives, shards(): curve = lax.all_to_all(curve, ('ex', 'ctr'), 0, 0)  14.9 us
    ppermute x8, starting transfers between devices, over_y(): return lax.ppermute(array, 'ex', pairs)  10.4 us
    all_to_all x1, waiting for transfers between devices, trade(): return lax.all_to_all(parts, 'ctr', 0, 0)  9.98 us
    all_to_all x1, starting transfers between devices, trade(): return lax.all_to_all(parts, 'ctr', 0, 0)  7.96 us
    pallas_call x1, Pallas kernels, make_tile(): call(tile_kernel, 'tile', [shape((count, examples), BF16), shape((example...  5.9 us
  transfers between devices with their start and end apart: 15, of which 11 were waited for; matrix products, arithmetic and copies ran while one was open for 1% of the time, Pallas kernels for 3%

profile of v6, /device:TPU:0, one launch (start us, length us, event | category | flops | bytes accessed | tf_op | source)
XLA Modules:
  0.0 164.9 jit_solution(14404841296641572808)
XLA Ops:
  0.0 0.8 copy-done.3
  0.8 0.9 copies.1
  1.7 8.0 %all-to-all-start = ((bf16[16,128,128]{2,1,0:T(8,128)(2,1)}), bf16[16,128,128]{2,1,0:T(8,128)(2,1)S(1)}, u32[]{:S(2)}, u32[]{:S(2)}) async-start(bf16[16,128,128]{2,1,0:T(8,128)(2,1)} %copies.1), calls=%async_computation | async-start | bytes 1048576 | tf_op jit(solution)/shard_map/all_to_all | solution.py:635
  9.7 0.7 prepare.1
  10.4 0.8 dynamic-slice_bitcast_fusion.weight_ref
  11.2 10.0 %all-to-all-done.pool_ref = bf16[16,128,128]{2,1,0:T(8,128)(2,1)S(1)} async-done(((bf16[16,128,128]{2,1,0:T(8,128)(2,1)}), bf16[16,128,128]{2,1,0:T(8,128)(2,1)S(1)}, u32[]{:S(2)}, u32[]{:S(2)}) %all-to-all-start) | async-done | bytes 524320 | tf_op jit(solution)/shard_map/all_to_all | solution.py:635
  21.2 5.9 %tile.1 = (bf16[2048,2048]{1,0:T(8,128)(2,1)S(1)}, bf16[2048,2048]{1,0:T(8,128)(2,1)S(1)}, f32[16,144,128]{2,1,0:T(8,128)S(1)}) custom-call(bf16[144,2048]{1,0:T(8,128)(2,1)S(1)} %copy-done.5, s32[1,2048]{1,0:T(1,128)S(1)} %get-tuple-element.52.chunk_ref, bf16[16,128,128]{2,1,0:T(8,128)(2,1)S(1)} %all-to-all-done.pool_ref, ...), custom_call_target="tpu_custom_call" | custom-call | flops 4294967296 | bytes 17956864 | tf_op jit(solution)/shard_map/tile/pallas_call | solution.py:238
  27.2 14.4 %all_to_all.35 = f16[16,144,128]{2,1,0:T(8,128)(2,1)S(1)} all-to-all(f16[16,144,128]{2,1,0:T(8,128)(2,1)S(1)} %convert_element_type.66), channel_id=1, replica_groups=mesh['ex'=8,'ctr'=16] {'ctr'}, dimensions={0} | all-to-all | bytes 1179648 | tf_op jit(solution)/shard_map/all_to_all | solution.py:635
  41.7 13.7 %all_to_all.36.values_ref = bf16[16,144,128]{2,1,0:T(8,128)(2,1)S(1)} all-to-all(bf16[16,144,128]{2,1,0:T(8,128)(2,1)S(1)} %get-tuple-element.59), channel_id=1, replica_groups=mesh['ex'=8,'ctr'=16] {'ctr'}, dimensions={0} | all-to-all | bytes 1179648 | tf_op jit(solution)/shard_map/all_to_all | solution.py:635
  55.4 0.9 backward_other.2
  56.3 0.1 collective-permute-start
  56.3 0.8 backward_own.2.own_ref
  57.2 1.2 collective-permute-done.got_ref
  58.4 0.2 join.2
  58.6 0.2 reduce-precision_convert_fusion.7
  58.8 1.7 %collective-permute-start.1 = (f16[152,512]{1,0:T(8,128)(2,1)S(1)}, f16[152,512]{1,0:T(8,128)(2,1)S(1)}, u32[]{:S(2)}, u32[]{:S(2)}) collective-permute-start(f16[152,512]{1,0:T(8,128)(2,1)S(1)} %get-tuple-element.105), channel_id=1, source_target_pairs={{0,32},{16,48},{32,0},{48,16},{64,96},{80,112},{96,64},{112,80},{1... | collective-permute-start | bytes 466952 | tf_op jit(solution)/shard_map/ppermute | solution.py:629
  60.4 0.2 reduce-precision_convert_fusion.5
  60.6 2.3 %collective-permute-start.3 = (f16[152,512]{1,0:T(8,128)(2,1)S(1)}, f16[152,512]{1,0:T(8,128)(2,1)S(1)}, u32[]{:S(2)}, u32[]{:S(2)}) collective-permute-start(f16[152,512]{1,0:T(8,128)(2,1)S(1)} %get-tuple-element.101), channel_id=1, source_target_pairs={{0,96},{16,112},{32,64},{48,80},{64,32},{80,48},{96,0},{112,16},{1... | collective-permute-start | bytes 466952 | tf_op jit(solution)/shard_map/ppermute | solution.py:629
  62.9 2.1 %collective-permute-done.1 = f16[152,512]{1,0:T(8,128)(2,1)S(1)} collective-permute-done((f16[152,512]{1,0:T(8,128)(2,1)S(1)}, f16[152,512]{1,0:T(8,128)(2,1)S(1)}, u32[]{:S(2)}, u32[]{:S(2)}) %collective-permute-start.1) | collective-permute-done | bytes 155680 | tf_op jit(solution)/shard_map/ppermute | solution.py:629
  64.9 0.4 add.14
  65.3 0.2 reduce-precision_convert_fusion.6
  65.5 3.1 %collective-permute-start.2 = (f16[152,512]{1,0:T(8,128)(2,1)S(1)}, f16[152,512]{1,0:T(8,128)(2,1)S(1)}, u32[]{:S(2)}, u32[]{:S(2)}) collective-permute-start(f16[152,512]{1,0:T(8,128)(2,1)S(1)} %get-tuple-element.103), channel_id=1, source_target_pairs={{0,96},{16,112},{32,64},{48,80},{64,32},{80,48},{96,0},{112,16},{1... | collective-permute-start | bytes 466952 | tf_op jit(solution)/shard_map/ppermute | solution.py:629
  68.6 0.4 add.15
  69.0 0.2 reduce-precision_convert_fusion.4
  69.1 0.4 collective-permute-start.4
  69.5 0.3 factors.1
  69.9 2.2 %collective-permute-done.2 = f16[152,512]{1,0:T(8,128)(2,1)S(1)} collective-permute-done((f16[152,512]{1,0:T(8,128)(2,1)S(1)}, f16[152,512]{1,0:T(8,128)(2,1)S(1)}, u32[]{:S(2)}, u32[]{:S(2)}) %collective-permute-start.2) | collective-permute-done | bytes 155680 | tf_op jit(solution)/shard_map/ppermute | solution.py:629
  72.1 2.5 %collective-permute-done.4 = f16[152,512]{1,0:T(8,128)(2,1)S(1)} collective-permute-done((f16[152,512]{1,0:T(8,128)(2,1)S(1)}, f16[152,512]{1,0:T(8,128)(2,1)S(1)}, u32[]{:S(2)}, u32[]{:S(2)}) %collective-permute-start.4) | collective-permute-done | bytes 155680 | tf_op jit(solution)/shard_map/ppermute | solution.py:629
  74.7 1.1 residual.1
  75.8 0.5 collective-permute-start.6
  76.3 0.8 forward_own.2.first_ref
  77.1 0.3 collective-permute-done.6.other_part_ref
  77.4 0.9 forward.2
  78.4 16.0 %all_to_all.37 = f16[16,152,128]{2,1,0:T(8,128)(2,1)S(1)} all-to-all(f16[16,152,128]{2,1,0:T(8,128)(2,1)S(1)} %convert_element_type.76), channel_id=1, replica_groups=mesh['ex'=8,'ctr'=16] {'ctr'}, dimensions={0} | all-to-all | bytes 1245184 | tf_op jit(solution)/shard_map/all_to_all | solution.py:635
  94.4 0.7 weigh.1
  95.2 15.7 %all_to_all.38.values_ref = bf16[16,160,128]{2,1,0:T(8,128)(2,1)S(1)} all-to-all(bf16[16,160,128]{2,1,0:T(8,128)(2,1)S(1)} %get-tuple-element.76), channel_id=1, replica_groups=mesh['ex'=8,'ctr'=16] {'ctr'}, dimensions={0} | all-to-all | bytes 1310720 | tf_op jit(solution)/shard_map/all_to_all | solution.py:635
  110.8 0.8 backward_other.3
  111.7 0.1 collective-permute-start.7
  111.8 0.8 backward_own.3.own_ref
  112.6 1.2 collective-permute-done.7.got_ref
  113.8 0.2 join.3
  114.0 0.2 reduce-precision_convert_fusion.3
  114.2 0.2 collective-permute-start.8
  114.4 0.2 reduce-precision_convert_fusion.1
  114.6 1.3 collective-permute-start.10
  115.8 4.5 %collective-permute-done.8 = f16[152,512]{1,0:T(8,128)(2,1)S(1)} collective-permute-done((f16[152,512]{1,0:T(8,128)(2,1)S(1)}, f16[152,512]{1,0:T(8,128)(2,1)S(1)}, u32[]{:S(2)}, u32[]{:S(2)}) %collective-permute-start.8) | collective-permute-done | bytes 155680 | tf_op jit(solution)/shard_map/ppermute | solution.py:629
  120.4 0.4 add.16
  120.7 0.2 reduce-precision_convert_fusion.2
  120.9 1.3 collective-permute-start.9
  122.3 0.4 add.17
  122.6 0.2 reduce-precision_convert_fusion
  122.8 0.2 collective-permute-start.11
  123.0 4.5 %collective-permute-done.9 = f16[152,512]{1,0:T(8,128)(2,1)S(1)} collective-permute-done((f16[152,512]{1,0:T(8,128)(2,1)S(1)}, f16[152,512]{1,0:T(8,128)(2,1)S(1)}, u32[]{:S(2)}, u32[]{:S(2)}) %collective-permute-start.9) | collective-permute-done | bytes 155680 | tf_op jit(solution)/shard_map/ppermute | solution.py:629
  127.4 0.7 collective-permute-done.11
  128.1 1.2 step.1
  129.3 0.1 collective-permute-start.12
  129.4 0.5 collective-permute-start.13
  129.9 0.8 forward_own.3.first_ref
  130.7 0.3 collective-permute-done.13.other_part_ref
  131.0 0.9 forward.3
  132.0 16.0 %all_to_all.39 = f16[16,152,128]{2,1,0:T(8,128)(2,1)S(1)} all-to-all(f16[16,152,128]{2,1,0:T(8,128)(2,1)S(1)} %convert_element_type.86), channel_id=1, replica_groups=mesh['ex'=8,'ctr'=16] {'ctr'}, dimensions={0} | all-to-all | bytes 1245184 | tf_op jit(solution)/shard_map/all_to_all | solution.py:635
  148.0 0.9 curve.1
  149.1 14.9 %all_to_all.40.curve_ref = f32[128,1,256]{2,1,0:T(1,128)S(1)} all-to-all(f32[128,1,256]{2,1,0:T(1,128)S(1)} %broadcast_in_dim.3), channel_id=1, replica_groups=mesh['ex'=8,'ctr'=16] {'ex','ctr'}, dimensions={0} | all-to-all | bytes 262144 | tf_op jit(solution)/shard_map/all_to_all | solution.py:681
  164.0 0.9 margins.1
  (33 shorter events, 1.0 us)
Async XLA Ops:
  0.0 10.3 %copy-start = (s32[2048]{0:T(1024)S(1)}, s32[2048]{0:T(1024)}, u32[]{:S(2)}) copy-start(s32[2048]{0:T(1024)} %param.9) | copy-start | bytes 24580
  0.0 9.7 %copy-start.2 = (bf16[64,2048]{1,0:T(8,128)(2,1)S(1)}, bf16[64,2048]{1,0:T(8,128)(2,1)}, u32[]{:S(2)}) copy-start(bf16[64,2048]{1,0:T(8,128)(2,1)} %centers_ref.1) | copy-start | bytes 786436
  0.0 0.8 copy-start.3
  0.8 8.9 %copy-start.4 = (s32[2048]{0:T(1024)S(1)}, s32[2048]{0:T(1024)}, u32[]{:S(2)}) copy-start(s32[2048]{0:T(1024)} %param.8) | copy-start | bytes 24580
  0.8 20.4 %copy-start.5 = (bf16[144,2048]{1,0:T(8,128)(2,1)S(1)}, bf16[144,2048]{1,0:T(8,128)(2,1)}, u32[]{:S(2)}) copy-start(bf16[144,2048]{1,0:T(8,128)(2,1)} %alpha_hbm.1) | copy-start | bytes 1769476
  1.7 19.5 %all-to-all-start = ((bf16[16,128,128]{2,1,0:T(8,128)(2,1)}), bf16[16,128,128]{2,1,0:T(8,128)(2,1)S(1)}, u32[]{:S(2)}, u32[]{:S(2)}) async-start(bf16[16,128,128]{2,1,0:T(8,128)(2,1)} %copies.1), calls=%async_computation | async-start | bytes 1048576 | tf_op jit(solution)/shard_map/all_to_all | solution.py:635
  56.3 2.1 %collective-permute-start = (f32[152,1024]{1,0:T(8,128)S(1)}, f32[152,1024]{1,0:T(8,128)S(1)}, u32[]{:S(2)}, u32[]{:S(2)}) collective-permute-start(f32[152,1024]{1,0:T(8,128)S(1)} %get-tuple-element.63), channel_id=1, source_target_pairs={{0,16},{16,0},{32,48},{48,32},{64,80},{80,64},{96,112},{112,96},{1... | collective-permute-start | bytes 1867784 | tf_op jit(solution)/shard_map/ppermute | solution.py:632
  58.8 6.1 %collective-permute-start.1 = (f16[152,512]{1,0:T(8,128)(2,1)S(1)}, f16[152,512]{1,0:T(8,128)(2,1)S(1)}, u32[]{:S(2)}, u32[]{:S(2)}) collective-permute-start(f16[152,512]{1,0:T(8,128)(2,1)S(1)} %get-tuple-element.105), channel_id=1, source_target_pairs={{0,32},{16,48},{32,0},{48,16},{64,96},{80,112},{96,64},{112,80},{1... | collective-permute-start | bytes 466952 | tf_op jit(solution)/shard_map/ppermute | solution.py:629
  60.6 8.0 %collective-permute-start.3 = (f16[152,512]{1,0:T(8,128)(2,1)S(1)}, f16[152,512]{1,0:T(8,128)(2,1)S(1)}, u32[]{:S(2)}, u32[]{:S(2)}) collective-permute-start(f16[152,512]{1,0:T(8,128)(2,1)S(1)} %get-tuple-element.101), channel_id=1, source_target_pairs={{0,96},{16,112},{32,64},{48,80},{64,32},{80,48},{96,0},{112,16},{1... | collective-permute-start | bytes 466952 | tf_op jit(solution)/shard_map/ppermute | solution.py:629
  65.5 4.1 %copy-start.1 = (f32[2048,256]{1,0:T(8,128)S(1)}, f32[2048,256]{1,0:T(8,128)}, u32[]{:S(2)}) copy-start(f32[2048,256]{1,0:T(8,128)} %precond_ref.1) | copy-start | bytes 6291460
  65.5 6.6 %collective-permute-start.2 = (f16[152,512]{1,0:T(8,128)(2,1)S(1)}, f16[152,512]{1,0:T(8,128)(2,1)S(1)}, u32[]{:S(2)}, u32[]{:S(2)}) collective-permute-start(f16[152,512]{1,0:T(8,128)(2,1)S(1)} %get-tuple-element.103), channel_id=1, source_target_pairs={{0,96},{16,112},{32,64},{48,80},{64,32},{80,48},{96,0},{112,16},{1... | collective-permute-start | bytes 466952 | tf_op jit(solution)/shard_map/ppermute | solution.py:629
  69.1 5.5 %collective-permute-start.4 = (f16[152,512]{1,0:T(8,128)(2,1)S(1)}, f16[152,512]{1,0:T(8,128)(2,1)S(1)}, u32[]{:S(2)}, u32[]{:S(2)}) collective-permute-start(f16[152,512]{1,0:T(8,128)(2,1)S(1)} %get-tuple-element.99), channel_id=1, source_target_pairs={{0,32},{16,48},{32,0},{48,16},{64,96},{80,112},{96,64},{112,80},{1... | collective-permute-start | bytes 466952 | tf_op jit(solution)/shard_map/ppermute | solution.py:629
  75.7 1.7 %collective-permute-start.5 = (bf16[144,1024]{1,0:T(8,128)(2,1)S(1)}, bf16[144,1024]{1,0:T(8,128)(2,1)S(1)}, u32[]{:S(2)}, u32[]{:S(2)}) collective-permute-start(bf16[144,1024]{1,0:T(8,128)(2,1)S(1)} %get-tuple-element.72.own_ref), channel_id=1, source_target_pairs={{0,16},{16,0},{32,48},{48,32},{64,80},{80,64},{96,112},{112,96},{1... | collective-permute-start | bytes 884744 | tf_op jit(solution)/shard_map/ppermute | solution.py:632
  75.8 1.6 collective-permute-start.6
  111.7 2.1 %collective-permute-start.7 = (f32[152,1024]{1,0:T(8,128)S(1)}, f32[152,1024]{1,0:T(8,128)S(1)}, u32[]{:S(2)}, u32[]{:S(2)}) collective-permute-start(f32[152,1024]{1,0:T(8,128)S(1)} %get-tuple-element.79), channel_id=1, source_target_pairs={{0,16},{16,0},{32,48},{48,32},{64,80},{80,64},{96,112},{112,96},{1... | collective-permute-start | bytes 1867784 | tf_op jit(solution)/shard_map/ppermute | solution.py:632
  114.2 6.1 %collective-permute-start.8 = (f16[152,512]{1,0:T(8,128)(2,1)S(1)}, f16[152,512]{1,0:T(8,128)(2,1)S(1)}, u32[]{:S(2)}, u32[]{:S(2)}) collective-permute-start(f16[152,512]{1,0:T(8,128)(2,1)S(1)} %get-tuple-element.97), channel_id=1, source_target_pairs={{0,32},{16,48},{32,0},{48,16},{64,96},{80,112},{96,64},{112,80},{1... | collective-permute-start | bytes 466952 | tf_op jit(solution)/shard_map/ppermute | solution.py:629
  114.6 7.7 %collective-permute-start.10 = (f16[152,512]{1,0:T(8,128)(2,1)S(1)}, f16[152,512]{1,0:T(8,128)(2,1)S(1)}, u32[]{:S(2)}, u32[]{:S(2)}) collective-permute-start(f16[152,512]{1,0:T(8,128)(2,1)S(1)} %get-tuple-element.93), channel_id=1, source_target_pairs={{0,96},{16,112},{32,64},{48,80},{64,32},{80,48},{96,0},{112,16},{1... | collective-permute-start | bytes 466952 | tf_op jit(solution)/shard_map/ppermute | solution.py:629
  120.9 6.5 %collective-permute-start.9 = (f16[152,512]{1,0:T(8,128)(2,1)S(1)}, f16[152,512]{1,0:T(8,128)(2,1)S(1)}, u32[]{:S(2)}, u32[]{:S(2)}) collective-permute-start(f16[152,512]{1,0:T(8,128)(2,1)S(1)} %get-tuple-element.95), channel_id=1, source_target_pairs={{0,96},{16,112},{32,64},{48,80},{64,32},{80,48},{96,0},{112,16},{1... | collective-permute-start | bytes 466952 | tf_op jit(solution)/shard_map/ppermute | solution.py:629
  122.8 5.3 %collective-permute-start.11 = (f16[152,512]{1,0:T(8,128)(2,1)S(1)}, f16[152,512]{1,0:T(8,128)(2,1)S(1)}, u32[]{:S(2)}, u32[]{:S(2)}) collective-permute-start(f16[152,512]{1,0:T(8,128)(2,1)S(1)} %get-tuple-element.91), channel_id=1, source_target_pairs={{0,32},{16,48},{32,0},{48,16},{64,96},{80,112},{96,64},{112,80},{1... | collective-permute-start | bytes 466952 | tf_op jit(solution)/shard_map/ppermute | solution.py:629
  129.3 1.7 %collective-permute-start.12 = (bf16[144,1024]{1,0:T(8,128)(2,1)S(1)}, bf16[144,1024]{1,0:T(8,128)(2,1)S(1)}, u32[]{:S(2)}, u32[]{:S(2)}) collective-permute-start(bf16[144,1024]{1,0:T(8,128)(2,1)S(1)} %get-tuple-element.84.own_ref), channel_id=1, source_target_pairs={{0,16},{16,0},{32,48},{48,32},{64,80},{80,64},{96,112},{112,96},{1... | collective-permute-start | bytes 884744 | tf_op jit(solution)/shard_map/ppermute | solution.py:632
  129.4 1.6 collective-permute-start.13

commit v7 on v6

--- a/solution.py
+++ b/solution.py
@@ -191,7 +191,7 @@
 
 def tile_kernel(
     alpha_hbm, chunk_ref, pool_ref, one_hot_ref, sides_ref, tile_ref, turned_ref, rows_ref,
-    side_ref, alpha_ref, alpha_sem,
+    side_ref, base_ref, alpha_ref, alpha_sem,
 ):
     fetch = pltpu.make_async_copy(alpha_hbm, alpha_ref, alpha_sem)
     fetch.start()
@@ -218,18 +218,17 @@
         point_sq = jnp.sum(points * points, axis=0, keepdims=True)
         side = jnp.concatenate([points, tail(point_sq, 0, DEPTH - features)], axis=0)
         side_ref[:, here] = side.astype(BF16)
+    fetch.wait()
     for b in range(count // BAND):
         here = slice(b * BAND, (b + 1) * BAND)
         near = jnp.dot(sides_ref[here, :], side_ref[...], preferred_element_type=F32)
         values = jnp.exp2(near * scale).astype(BF16)
         tile_ref[here, :] = values
         turned_ref[:, here] = values.T
-    fetch.wait()
-    for b in range(examples // BAND):
-        here = slice(b * BAND, (b + 1) * BAND)
-        rows = jnp.dot(alpha_ref[...], tile_ref[:, here], preferred_element_type=F32)
-        for k in range(BAND // share):
-            rows_ref[b * (BAND // share) + k] = rows[:, k * share : (k + 1) * share]
+        rows = jnp.dot(alpha_ref[:, here], values, preferred_element_type=F32)
+        base_ref[...] = rows if b == 0 else base_ref[...] + rows
+    for k in range(examples // share):
+        rows_ref[k] = base_ref[:, k * share : (k + 1) * share]
 
 
 def make_tile(chunk, row_pool, one_hot, sides, alpha, share):
@@ -246,6 +245,7 @@
         4 << 30,
         [
             pltpu.VMEM((DEPTH, examples), BF16),
+            pltpu.VMEM((classes, examples), F32),
             pltpu.VMEM(alpha.shape, BF16),
             pltpu.SemaphoreType.DMA,
         ],
@@ -290,28 +290,42 @@
     return jnp.concatenate(out, axis=1)
 
 
+def put_lifted(ref, lifted, vectors):
+    classes, half = lifted.shape
+    ref[:classes] = lifted
+    row = lax.broadcasted_iota(jnp.int32, (EXTRA, 2 * LANES), 0)
+    out = jnp.zeros((EXTRA, 2 * LANES), F32)
+    for k, vector in enumerate(vectors):
+        for p, piece in enumerate(split3(vector)):
+            out = jnp.where(row == 3 * k + p, piece.astype(F32), out)
+    ref[classes:, : 2 * LANES] = out.astype(BF16)
+    ref[classes:, 2 * LANES :] = jnp.zeros((EXTRA, half - 2 * LANES), BF16)
+
+
 def forward_own_kernel(core_ref, own_ref, tile_ref, first_ref):
-    half = own_ref.shape[1]
+    classes, half = first_ref.shape[0], own_ref.shape[1]
     mine = pl.ds(pl.multiple_of(core_ref[0] * half, half), half)
     for b in range(first_ref.shape[1] // BAND):
         here = slice(b * BAND, (b + 1) * BAND)
-        first_ref[:, here] = jnp.dot(own_ref[...], tile_ref[mine, here], preferred_element_type=F32)
-
-
-def forward_kernel(
-    core_ref, first_ref, other_ref, own_part_ref, other_part_ref, tile_ref, rows_ref
-):
-    classes, half = other_ref.shape
+        first_ref[:, here] = jnp.dot(
+            own_ref[:classes], tile_ref[mine, here], preferred_element_type=F32
+        )
+
+
+def forward_kernel(core_ref, first_ref, own_ref, other_ref, tile_ref, rows_ref):
+    classes, half = first_ref.shape[0], other_ref.shape[1]
     share = rows_ref.shape[2]
     examples = tile_ref.shape[1]
     theirs = pl.ds(pl.multiple_of((1 - core_ref[0]) * half, half), half)
-    part = own_part_ref[...] + other_part_ref[...]
-    powers = exponents(part[2:3]) - 14.0
-    extra = half_rows(powers, [part[:1], part[1:2]])
+    part = [ref[classes:, : 2 * LANES].astype(F32) for ref in (own_ref, other_ref)]
+    part = part[0] + part[1]
+    part = [part[3 * k : 3 * k + 1] + part[3 * k + 1 : 3 * k + 2] + part[3 * k + 2 : 3 * k + 3] for k in range(3)]
+    powers = exponents(part[2]) - 14.0
+    extra = half_rows(powers, part[:2])
     scales = column(jnp.exp2(-powers), classes)
     for b in range(examples // BAND):
         here = slice(b * BAND, (b + 1) * BAND)
-        rows = jnp.dot(other_ref[...], tile_ref[theirs, here], preferred_element_type=F32)
+        rows = jnp.dot(other_ref[:classes], tile_ref[theirs, here], preferred_element_type=F32)
         rows = (rows + first_ref[:, here]) * scales
         for k in range(BAND // share):
             at = b * (BAND // share) + k
@@ -319,8 +333,8 @@
             rows_ref[at, classes:] = extra
 
 
-def forward(core, lifted, other, own_part, other_part, tile, share):
-    classes = lifted.shape[0]
+def forward(core, lifted, other, tile, share):
+    classes = lifted.shape[0] - EXTRA
     examples = tile.shape[1]
     first = call(
         forward_own_kernel,
@@ -336,8 +350,8 @@
         shape((examples // share, classes + SCALARS, share), F32),
         604 << 20,
         scalars=1,
-        arrays=5,
-    )(core, first, other, own_part, other_part, tile)
+        arrays=4,
+    )(core, first, lifted, other, tile)
 
 
 def backward_other_kernel(core_ref, values_ref, turned_ref, other_ref, flat_ref, row_ref):
@@ -470,7 +484,7 @@
 
 def residual_kernel(
     total, one_ref, one_in_ref, two_ref, two_in_ref, high_ref, low_ref, high_turned_ref,
-    low_turned_ref, residual_ref, lifted_ref, part_ref,
+    low_turned_ref, residual_ref, lifted_ref,
 ):
     one = unpack_halves(one_ref) + unpack_halves(one_in_ref)
     two = unpack_halves(two_ref) + unpack_halves(two_in_ref)
@@ -478,11 +492,9 @@
     residual = block_products(sums, high_ref, low_ref) * (-1.0 / total)
     residual_ref[...] = residual
     lifted = block_products(residual, high_turned_ref, low_turned_ref).astype(BF16)
-    lifted_ref[...] = lifted
     zero = jnp.zeros((1, 2 * LANES), F32)
-    part_ref[...] = stack_rows(
-        [lane_sums(residual * residual), zero, lane_sums(jnp.abs(lifted.astype(F32)))]
-    )
+    sizes = lane_sums(jnp.abs(lifted.astype(F32)))
+    put_lifted(lifted_ref, lifted, [lane_sums(residual * residual), zero, sizes])
 
 
 def first_residual(total, sums, blocks):
@@ -492,8 +504,7 @@
         "residual",
         [
             shape((classes, 2 * wide), F32),
-            shape((classes, 2 * wide), BF16),
-            shape((8, 2 * LANES), F32),
+            shape((classes + EXTRA, 2 * wide), BF16),
         ],
         450 << 20,
         arrays=8,
@@ -528,7 +539,7 @@
 
 def step_kernel(
     total, one_ref, one_in_ref, two_ref, two_in_ref, high_ref, low_ref, high_turned_ref,
-    low_turned_ref, residual_ref, norm_ref, lifted_ref, part_ref, rough_ref,
+    low_turned_ref, residual_ref, norm_ref, lifted_ref, rough_ref,
 ):
     classes = residual_ref.shape[0]
     one = unpack_halves(one_ref) + unpack_halves(one_in_ref)
@@ -543,18 +554,16 @@
     image = block_products(sums, high_ref, low_ref) / total + RIDGE * old
     new = old - column(rough, classes) * image
     lifted = block_products(new, high_turned_ref, low_turned_ref).astype(BF16)
-    lifted_ref[...] = lifted
-    part_ref[...] = stack_rows(
-        [lane_sums(old * new), lane_sums(new * new), lane_sums(jnp.abs(lifted.astype(F32)))]
-    )
+    sizes = lane_sums(jnp.abs(lifted.astype(F32)))
+    put_lifted(lifted_ref, lifted, [lane_sums(old * new), lane_sums(new * new), sizes])
 
 
 def step(total, sums, blocks, residual, norm):
-    row = shape((8, 2 * LANES), F32)
+    classes, half = residual.shape
     return call(
         functools.partial(step_kernel, total),
         "step",
-        [shape(residual.shape, BF16), row, row],
+        [shape((classes + EXTRA, half), BF16), shape((8, 2 * LANES), F32)],
         450 << 20,
         arrays=10,
     )(*sums, *blocks, residual, norm)
@@ -666,15 +675,15 @@
     got, late_core = lax.optimization_barrier((got, core))
     blocks = factors(late_core, precond)
     sums = sum_examples(own, row, got)
-    residual, lifted, part = first_residual(total, sums, blocks)
-    rows = forward(core, lifted, over_cores(lifted), part, over_cores(part), tile, share)
+    residual, lifted = first_residual(total, sums, blocks)
+    rows = forward(core, lifted, over_cores(lifted), tile, share)
     image, norm, send = weigh(trade_halves(rows), hessian)
 
     other, flat, row = backward_other(core, trade(send), turned, classes)
     got = over_cores(other)
     sums = sum_examples(backward_own(core, flat, turned), row, got)
-    lifted, part, rough = step(total, sums, blocks, residual, norm)
-    rows = forward(core, lifted, over_cores(lifted), part, over_cores(part), tile, share)
+    lifted, rough = step(total, sums, blocks, residual, norm)
+    rows = forward(core, lifted, over_cores(lifted), tile, share)
     last, scales, curve = last_curve(trade_halves(rows), hessian, image, norm, rough)
 
     curve = jnp.broadcast_to(curve, (n_ex * n_ctr,) + curve.shape)

time: 166 us -> 166 us (level)
    ppermute x6 -> x4, waiting for transfers between devices: 3.01 us -> 4.04 us  [over_cores(): return lax.ppermute(array, 'ex', core_pairs)]
  transfers between devices with their start and end apart: 15 -> 13, of which waited for: 11 -> 11; matrix products, arithmetic and copies ran while one was open for 1% -> 1% of each run, Pallas kernels for 3% -> 3%
where the time goes in v7:
time: 166 us; the launch traced here: 165 us
  blocking collectives  90.6 us (55%)
  waiting for transfers between devices  30.4 us (18%)
  Pallas kernels  20.9 us (13%)
  starting transfers between devices  18.7 us (11%)
  other arithmetic  2.02 us (1%)
  local copies, waits for them, and re-layouts  1.74 us (1%)
    all_to_all x5, blocking collectives, trade(): return lax.all_to_all(parts, 'ctr', 0, 0)  75.7 us
    ppermute x8, waiting for transfers between devices, over_y(): return lax.ppermute(array, 'ex', pairs)  16.4 us
    all_to_all x1, blocking collectives, shards(): curve = lax.all_to_all(curve, ('ex', 'ctr'), 0, 0)  14.9 us
    ppermute x8, starting transfers between devices, over_y(): return lax.ppermute(array, 'ex', pairs)  10.4 us
    all_to_all x1, waiting for transfers between devices, trade(): return lax.all_to_all(parts, 'ctr', 0, 0)  9.98 us
    all_to_all x1, starting transfers between devices, trade(): return lax.all_to_all(parts, 'ctr', 0, 0)  7.96 us
    pallas_call x1, Pallas kernels, make_tile(): call(tile_kernel, 'tile', [shape((count, examples), BF16), shape((example...  5.66 us
    ppermute x4, waiting for transfers between devices, over_cores(): return lax.ppermute(array, 'ex', core_pairs)  4.04 us
  transfers between devices with their start and end apart: 13, of which 11 were waited for; matrix products, arithmetic and copies ran while one was open for 1% of the time, Pallas kernels for 3%

profile of v7, /device:TPU:0, one launch (start us, length us, event | category | flops | bytes accessed | tf_op | source)
XLA Modules:
  0.0 164.7 jit_solution(12105792303342081209)
XLA Ops:
  0.0 0.8 copy-done.3
  0.8 0.9 copies.1
  1.7 8.0 %all-to-all-start = ((bf16[16,128,128]{2,1,0:T(8,128)(2,1)}), bf16[16,128,128]{2,1,0:T(8,128)(2,1)S(1)}, u32[]{:S(2)}, u32[]{:S(2)}) async-start(bf16[16,128,128]{2,1,0:T(8,128)(2,1)} %copies.1), calls=%async_computation | async-start | bytes 1048576 | tf_op jit(solution)/shard_map/all_to_all | solution.py:644
  9.7 0.7 prepare.1
  10.4 0.8 dynamic-slice_bitcast_fusion.weight_ref
  11.2 10.0 %all-to-all-done.pool_ref = bf16[16,128,128]{2,1,0:T(8,128)(2,1)S(1)} async-done(((bf16[16,128,128]{2,1,0:T(8,128)(2,1)}), bf16[16,128,128]{2,1,0:T(8,128)(2,1)S(1)}, u32[]{:S(2)}, u32[]{:S(2)}) %all-to-all-start) | async-done | bytes 524320 | tf_op jit(solution)/shard_map/all_to_all | solution.py:644
  21.2 5.7 %tile.1 = (bf16[2048,2048]{1,0:T(8,128)(2,1)S(1)}, bf16[2048,2048]{1,0:T(8,128)(2,1)S(1)}, f32[16,144,128]{2,1,0:T(8,128)S(1)}) custom-call(bf16[144,2048]{1,0:T(8,128)(2,1)S(1)} %copy-done.5, s32[1,2048]{1,0:T(1,128)S(1)} %get-tuple-element.50.chunk_ref, bf16[16,128,128]{2,1,0:T(8,128)(2,1)S(1)} %all-to-all-done.pool_ref, ...), custom_call_target="tpu_custom_call" | custom-call | flops 4294967296 | bytes 17956864 | tf_op jit(solution)/shard_map/tile/pallas_call | solution.py:237
  26.9 14.4 %all_to_all.35 = f16[16,144,128]{2,1,0:T(8,128)(2,1)S(1)} all-to-all(f16[16,144,128]{2,1,0:T(8,128)(2,1)S(1)} %convert_element_type.66), channel_id=1, replica_groups=mesh['ex'=8,'ctr'=16] {'ctr'}, dimensions={0} | all-to-all | bytes 1179648 | tf_op jit(solution)/shard_map/all_to_all | solution.py:644
  41.3 0.1 convert_reduce_fusion.base_ref
  41.5 13.7 %all_to_all.36.values_ref = bf16[16,144,128]{2,1,0:T(8,128)(2,1)S(1)} all-to-all(bf16[16,144,128]{2,1,0:T(8,128)(2,1)S(1)} %get-tuple-element.57), channel_id=1, replica_groups=mesh['ex'=8,'ctr'=16] {'ctr'}, dimensions={0} | all-to-all | bytes 1179648 | tf_op jit(solution)/shard_map/all_to_all | solution.py:644
  55.1 0.8 backward_other.2
  56.0 0.1 collective-permute-start
  56.1 0.8 backward_own.2.own_ref
  56.9 1.2 collective-permute-done.got_ref
  58.1 0.2 join.2
  58.3 0.2 reduce-precision_convert_fusion.7
  58.5 1.7 %collective-permute-start.1 = (f16[152,512]{1,0:T(8,128)(2,1)S(1)}, f16[152,512]{1,0:T(8,128)(2,1)S(1)}, u32[]{:S(2)}, u32[]{:S(2)}) collective-permute-start(f16[152,512]{1,0:T(8,128)(2,1)S(1)} %get-tuple-element.101), channel_id=1, source_target_pairs={{0,32},{16,48},{32,0},{48,16},{64,96},{80,112},{96,64},{112,80},{1... | collective-permute-start | bytes 466952 | tf_op jit(solution)/shard_map/ppermute | solution.py:638
  60.2 0.2 reduce-precision_convert_fusion.5
  60.3 2.3 %collective-permute-start.3 = (f16[152,512]{1,0:T(8,128)(2,1)S(1)}, f16[152,512]{1,0:T(8,128)(2,1)S(1)}, u32[]{:S(2)}, u32[]{:S(2)}) collective-permute-start(f16[152,512]{1,0:T(8,128)(2,1)S(1)} %get-tuple-element.97), channel_id=1, source_target_pairs={{0,96},{16,112},{32,64},{48,80},{64,32},{80,48},{96,0},{112,16},{1... | collective-permute-start | bytes 466952 | tf_op jit(solution)/shard_map/ppermute | solution.py:638
  62.6 2.1 %collective-permute-done.1 = f16[152,512]{1,0:T(8,128)(2,1)S(1)} collective-permute-done((f16[152,512]{1,0:T(8,128)(2,1)S(1)}, f16[152,512]{1,0:T(8,128)(2,1)S(1)}, u32[]{:S(2)}, u32[]{:S(2)}) %collective-permute-start.1) | collective-permute-done | bytes 155680 | tf_op jit(solution)/shard_map/ppermute | solution.py:638
  64.7 0.4 add.14
  65.0 0.2 reduce-precision_convert_fusion.6
  65.2 3.1 %collective-permute-start.2 = (f16[152,512]{1,0:T(8,128)(2,1)S(1)}, f16[152,512]{1,0:T(8,128)(2,1)S(1)}, u32[]{:S(2)}, u32[]{:S(2)}) collective-permute-start(f16[152,512]{1,0:T(8,128)(2,1)S(1)} %get-tuple-element.99), channel_id=1, source_target_pairs={{0,96},{16,112},{32,64},{48,80},{64,32},{80,48},{96,0},{112,16},{1... | collective-permute-start | bytes 466952 | tf_op jit(solution)/shard_map/ppermute | solution.py:638
  68.4 0.4 add.15
  68.7 0.2 reduce-precision_convert_fusion.4
  68.9 0.4 collective-permute-start.4
  69.3 0.3 factors.1
  69.6 2.2 %collective-permute-done.2 = f16[152,512]{1,0:T(8,128)(2,1)S(1)} collective-permute-done((f16[152,512]{1,0:T(8,128)(2,1)S(1)}, f16[152,512]{1,0:T(8,128)(2,1)S(1)}, u32[]{:S(2)}, u32[]{:S(2)}) %collective-permute-start.2) | collective-permute-done | bytes 155680 | tf_op jit(solution)/shard_map/ppermute | solution.py:638
  71.9 2.5 %collective-permute-done.4 = f16[152,512]{1,0:T(8,128)(2,1)S(1)} collective-permute-done((f16[152,512]{1,0:T(8,128)(2,1)S(1)}, f16[152,512]{1,0:T(8,128)(2,1)S(1)}, u32[]{:S(2)}, u32[]{:S(2)}) %collective-permute-start.4) | collective-permute-done | bytes 155680 | tf_op jit(solution)/shard_map/ppermute | solution.py:638
  74.4 1.0 residual.1
  75.4 0.1 collective-permute-start.5
  75.5 0.8 forward_own.2.first_ref
  76.4 0.8 collective-permute-done.5.other_ref
  77.2 0.9 forward.2
  78.2 16.0 %all_to_all.37 = f16[16,152,128]{2,1,0:T(8,128)(2,1)S(1)} all-to-all(f16[16,152,128]{2,1,0:T(8,128)(2,1)S(1)} %convert_element_type.76), channel_id=1, replica_groups=mesh['ex'=8,'ctr'=16] {'ctr'}, dimensions={0} | all-to-all | bytes 1245184 | tf_op jit(solution)/shard_map/all_to_all | solution.py:644
  94.2 0.7 weigh.1
  94.9 15.7 %all_to_all.38.values_ref = bf16[16,160,128]{2,1,0:T(8,128)(2,1)S(1)} all-to-all(bf16[16,160,128]{2,1,0:T(8,128)(2,1)S(1)} %get-tuple-element.73), channel_id=1, replica_groups=mesh['ex'=8,'ctr'=16] {'ctr'}, dimensions={0} | all-to-all | bytes 1310720 | tf_op jit(solution)/shard_map/all_to_all | solution.py:644
  110.6 0.8 backward_other.3
  111.4 0.1 collective-permute-start.6
  111.5 0.8 backward_own.3.own_ref
  112.3 1.2 collective-permute-done.6.got_ref
  113.6 0.2 join.3
  113.8 0.2 reduce-precision_convert_fusion.3
  114.0 0.2 collective-permute-start.7
  114.2 0.2 reduce-precision_convert_fusion.1
  114.3 1.3 collective-permute-start.9
  115.6 4.5 %collective-permute-done.7 = f16[152,512]{1,0:T(8,128)(2,1)S(1)} collective-permute-done((f16[152,512]{1,0:T(8,128)(2,1)S(1)}, f16[152,512]{1,0:T(8,128)(2,1)S(1)}, u32[]{:S(2)}, u32[]{:S(2)}) %collective-permute-start.7) | collective-permute-done | bytes 155680 | tf_op jit(solution)/shard_map/ppermute | solution.py:638
  120.1 0.4 add.16
  120.5 0.2 reduce-precision_convert_fusion.2
  120.7 1.3 collective-permute-start.8
  122.0 0.4 add.17
  122.4 0.2 reduce-precision_convert_fusion
  122.6 0.2 collective-permute-start.10
  122.7 4.5 %collective-permute-done.8 = f16[152,512]{1,0:T(8,128)(2,1)S(1)} collective-permute-done((f16[152,512]{1,0:T(8,128)(2,1)S(1)}, f16[152,512]{1,0:T(8,128)(2,1)S(1)}, u32[]{:S(2)}, u32[]{:S(2)}) %collective-permute-start.8) | collective-permute-done | bytes 155680 | tf_op jit(solution)/shard_map/ppermute | solution.py:638
  127.2 0.7 collective-permute-done.10
  127.9 1.2 step.1
  129.1 0.1 collective-permute-start.11
  129.2 0.8 forward_own.3.first_ref
  130.0 0.8 collective-permute-done.11.other_ref
  130.8 0.9 forward.3
  131.8 16.0 %all_to_all.39 = f16[16,152,128]{2,1,0:T(8,128)(2,1)S(1)} all-to-all(f16[16,152,128]{2,1,0:T(8,128)(2,1)S(1)} %convert_element_type.86), channel_id=1, replica_groups=mesh['ex'=8,'ctr'=16] {'ctr'}, dimensions={0} | all-to-all | bytes 1245184 | tf_op jit(solution)/shard_map/all_to_all | solution.py:644
  147.9 0.9 curve.1
  148.9 14.9 %all_to_all.40.curve_ref = f32[128,1,256]{2,1,0:T(1,128)S(1)} all-to-all(f32[128,1,256]{2,1,0:T(1,128)S(1)} %broadcast_in_dim.3), channel_id=1, replica_groups=mesh['ex'=8,'ctr'=16] {'ex','ctr'}, dimensions={0} | all-to-all | bytes 262144 | tf_op jit(solution)/shard_map/all_to_all | solution.py:690
  163.8 0.9 margins.1
  (29 shorter events, 0.9 us)
Async XLA Ops:
  0.0 10.3 %copy-start = (s32[2048]{0:T(1024)S(1)}, s32[2048]{0:T(1024)}, u32[]{:S(2)}) copy-start(s32[2048]{0:T(1024)} %param.9) | copy-start | bytes 24580
  0.0 9.7 %copy-start.2 = (bf16[64,2048]{1,0:T(8,128)(2,1)S(1)}, bf16[64,2048]{1,0:T(8,128)(2,1)}, u32[]{:S(2)}) copy-start(bf16[64,2048]{1,0:T(8,128)(2,1)} %centers_ref.1) | copy-start | bytes 786436
  0.0 0.8 copy-start.3
  0.8 8.9 %copy-start.4 = (s32[2048]{0:T(1024)S(1)}, s32[2048]{0:T(1024)}, u32[]{:S(2)}) copy-start(s32[2048]{0:T(1024)} %param.8) | copy-start | bytes 24580
  0.8 20.4 %copy-start.5 = (bf16[144,2048]{1,0:T(8,128)(2,1)S(1)}, bf16[144,2048]{1,0:T(8,128)(2,1)}, u32[]{:S(2)}) copy-start(bf16[144,2048]{1,0:T(8,128)(2,1)} %alpha_hbm.1) | copy-start | bytes 1769476
  1.7 19.5 %all-to-all-start = ((bf16[16,128,128]{2,1,0:T(8,128)(2,1)}), bf16[16,128,128]{2,1,0:T(8,128)(2,1)S(1)}, u32[]{:S(2)}, u32[]{:S(2)}) async-start(bf16[16,128,128]{2,1,0:T(8,128)(2,1)} %copies.1), calls=%async_computation | async-start | bytes 1048576 | tf_op jit(solution)/shard_map/all_to_all | solution.py:644
  56.0 2.1 %collective-permute-start = (f32[152,1024]{1,0:T(8,128)S(1)}, f32[152,1024]{1,0:T(8,128)S(1)}, u32[]{:S(2)}, u32[]{:S(2)}) collective-permute-start(f32[152,1024]{1,0:T(8,128)S(1)} %get-tuple-element.61), channel_id=1, source_target_pairs={{0,16},{16,0},{32,48},{48,32},{64,80},{80,64},{96,112},{112,96},{1... | collective-permute-start | bytes 1867784 | tf_op jit(solution)/shard_map/ppermute | solution.py:641
  58.5 6.1 %collective-permute-start.1 = (f16[152,512]{1,0:T(8,128)(2,1)S(1)}, f16[152,512]{1,0:T(8,128)(2,1)S(1)}, u32[]{:S(2)}, u32[]{:S(2)}) collective-permute-start(f16[152,512]{1,0:T(8,128)(2,1)S(1)} %get-tuple-element.101), channel_id=1, source_target_pairs={{0,32},{16,48},{32,0},{48,16},{64,96},{80,112},{96,64},{112,80},{1... | collective-permute-start | bytes 466952 | tf_op jit(solution)/shard_map/ppermute | solution.py:638
  60.3 8.0 %collective-permute-start.3 = (f16[152,512]{1,0:T(8,128)(2,1)S(1)}, f16[152,512]{1,0:T(8,128)(2,1)S(1)}, u32[]{:S(2)}, u32[]{:S(2)}) collective-permute-start(f16[152,512]{1,0:T(8,128)(2,1)S(1)} %get-tuple-element.97), channel_id=1, source_target_pairs={{0,96},{16,112},{32,64},{48,80},{64,32},{80,48},{96,0},{112,16},{1... | collective-permute-start | bytes 466952 | tf_op jit(solution)/shard_map/ppermute | solution.py:638
  65.2 4.1 %copy-start.1 = (f32[2048,256]{1,0:T(8,128)S(1)}, f32[2048,256]{1,0:T(8,128)}, u32[]{:S(2)}) copy-start(f32[2048,256]{1,0:T(8,128)} %precond_ref.1) | copy-start | bytes 6291460
  65.2 6.6 %collective-permute-start.2 = (f16[152,512]{1,0:T(8,128)(2,1)S(1)}, f16[152,512]{1,0:T(8,128)(2,1)S(1)}, u32[]{:S(2)}, u32[]{:S(2)}) collective-permute-start(f16[152,512]{1,0:T(8,128)(2,1)S(1)} %get-tuple-element.99), channel_id=1, source_target_pairs={{0,96},{16,112},{32,64},{48,80},{64,32},{80,48},{96,0},{112,16},{1... | collective-permute-start | bytes 466952 | tf_op jit(solution)/shard_map/ppermute | solution.py:638
  68.9 5.5 %collective-permute-start.4 = (f16[152,512]{1,0:T(8,128)(2,1)S(1)}, f16[152,512]{1,0:T(8,128)(2,1)S(1)}, u32[]{:S(2)}, u32[]{:S(2)}) collective-permute-start(f16[152,512]{1,0:T(8,128)(2,1)S(1)} %get-tuple-element.95), channel_id=1, source_target_pairs={{0,32},{16,48},{32,0},{48,16},{64,96},{80,112},{96,64},{112,80},{1... | collective-permute-start | bytes 466952 | tf_op jit(solution)/shard_map/ppermute | solution.py:638
  75.4 1.7 %collective-permute-start.5 = (bf16[160,1024]{1,0:T(8,128)(2,1)S(1)}, bf16[160,1024]{1,0:T(8,128)(2,1)S(1)}, u32[]{:S(2)}, u32[]{:S(2)}) collective-permute-start(bf16[160,1024]{1,0:T(8,128)(2,1)S(1)} %get-tuple-element.70.own_ref), channel_id=1, source_target_pairs={{0,16},{16,0},{32,48},{48,32},{64,80},{80,64},{96,112},{112,96},{1... | collective-permute-start | bytes 983048 | tf_op jit(solution)/shard_map/ppermute | solution.py:641
  111.4 2.1 %collective-permute-start.6 = (f32[152,1024]{1,0:T(8,128)S(1)}, f32[152,1024]{1,0:T(8,128)S(1)}, u32[]{:S(2)}, u32[]{:S(2)}) collective-permute-start(f32[152,1024]{1,0:T(8,128)S(1)} %get-tuple-element.76), channel_id=1, source_target_pairs={{0,16},{16,0},{32,48},{48,32},{64,80},{80,64},{96,112},{112,96},{1... | collective-permute-start | bytes 1867784 | tf_op jit(solution)/shard_map/ppermute | solution.py:641
  114.0 6.1 %collective-permute-start.7 = (f16[152,512]{1,0:T(8,128)(2,1)S(1)}, f16[152,512]{1,0:T(8,128)(2,1)S(1)}, u32[]{:S(2)}, u32[]{:S(2)}) collective-permute-start(f16[152,512]{1,0:T(8,128)(2,1)S(1)} %get-tuple-element.93), channel_id=1, source_target_pairs={{0,32},{16,48},{32,0},{48,16},{64,96},{80,112},{96,64},{112,80},{1... | collective-permute-start | bytes 466952 | tf_op jit(solution)/shard_map/ppermute | solution.py:638
  114.3 7.7 %collective-permute-start.9 = (f16[152,512]{1,0:T(8,128)(2,1)S(1)}, f16[152,512]{1,0:T(8,128)(2,1)S(1)}, u32[]{:S(2)}, u32[]{:S(2)}) collective-permute-start(f16[152,512]{1,0:T(8,128)(2,1)S(1)} %get-tuple-element.89), channel_id=1, source_target_pairs={{0,96},{16,112},{32,64},{48,80},{64,32},{80,48},{96,0},{112,16},{1... | collective-permute-start | bytes 466952 | tf_op jit(solution)/shard_map/ppermute | solution.py:638
  120.7 6.5 %collective-permute-start.8 = (f16[152,512]{1,0:T(8,128)(2,1)S(1)}, f16[152,512]{1,0:T(8,128)(2,1)S(1)}, u32[]{:S(2)}, u32[]{:S(2)}) collective-permute-start(f16[152,512]{1,0:T(8,128)(2,1)S(1)} %get-tuple-element.91), channel_id=1, source_target_pairs={{0,96},{16,112},{32,64},{48,80},{64,32},{80,48},{96,0},{112,16},{1... | collective-permute-start | bytes 466952 | tf_op jit(solution)/shard_map/ppermute | solution.py:638
  122.6 5.3 %collective-permute-start.10 = (f16[152,512]{1,0:T(8,128)(2,1)S(1)}, f16[152,512]{1,0:T(8,128)(2,1)S(1)}, u32[]{:S(2)}, u32[]{:S(2)}) collective-permute-start(f16[152,512]{1,0:T(8,128)(2,1)S(1)} %get-tuple-element.87), channel_id=1, source_target_pairs={{0,32},{16,48},{32,0},{48,16},{64,96},{80,112},{96,64},{112,80},{1... | collective-permute-start | bytes 466952 | tf_op jit(solution)/shard_map/ppermute | solution.py:638
  129.1 1.7 %collective-permute-start.11 = (bf16[160,1024]{1,0:T(8,128)(2,1)S(1)}, bf16[160,1024]{1,0:T(8,128)(2,1)S(1)}, u32[]{:S(2)}, u32[]{:S(2)}) collective-permute-start(bf16[160,1024]{1,0:T(8,128)(2,1)S(1)} %get-tuple-element.81.own_ref), channel_id=1, source_target_pairs={{0,16},{16,0},{32,48},{48,32},{64,80},{80,64},{96,112},{112,96},{1... | collective-permute-start | bytes 983048 | tf_op jit(solution)/shard_map/ppermute | solution.py:641

commit v8 on v7

--- a/solution.py
+++ b/solution.py
@@ -354,10 +354,12 @@
     )(core, first, lifted, other, tile)
 
 
-def backward_other_kernel(core_ref, values_ref, turned_ref, other_ref, flat_ref, row_ref):
+def backward_other_kernel(
+    core_ref, values_ref, turned_ref, first_ref, second_ref, flat_ref, row_ref
+):
     shares, height, share = values_ref.shape
     classes, examples = flat_ref.shape
-    half = other_ref.shape[1]
+    wide = first_ref.shape[1]
     for k in range(shares):
         flat_ref[:, k * share : (k + 1) * share] = values_ref[k, :classes]
     row = jnp.zeros((8, 2 * LANES), F32)
@@ -367,13 +369,16 @@
             total = total + values_ref[k, classes:].astype(F32)
         row = jnp.broadcast_to(read_rows(total, 0), (8, 2 * LANES))
     row_ref[...] = row
-    other_ref[classes:, : 2 * LANES] = row
-    other_ref[classes:, 2 * LANES :] = jnp.zeros((8, half - 2 * LANES), F32)
-    for b in range(half // BAND):
-        there = pl.ds(pl.multiple_of((1 - core_ref[0]) * half + b * BAND, BAND), BAND)
-        other_ref[:classes, b * BAND : (b + 1) * BAND] = jnp.dot(
-            flat_ref[...], turned_ref[:, there], preferred_element_type=F32
-        )
+    first_ref[classes:, : 2 * LANES] = row
+    first_ref[classes:, 2 * LANES :] = jnp.zeros((8, wide - 2 * LANES), F32)
+    for k, ref in enumerate((first_ref, second_ref)):
+        for b in range(wide // BAND):
+            there = (1 - core_ref[0]) * (2 * wide) + k * wide + b * BAND
+            ref[:classes, b * BAND : (b + 1) * BAND] = jnp.dot(
+                flat_ref[...],
+                turned_ref[:, pl.ds(pl.multiple_of(there, BAND), BAND)],
+                preferred_element_type=F32,
+            )
 
 
 def backward_own_kernel(core_ref, flat_ref, turned_ref, own_ref):
@@ -391,7 +396,8 @@
         backward_other_kernel,
         "backward_other",
         [
-            shape((classes + 8, count // 2), F32),
+            shape((classes + SCALARS, count // 4), F32),
+            shape((classes, count // 4), F32),
             shape((classes, examples), BF16),
             shape((8, 2 * LANES), F32),
         ],
@@ -438,17 +444,22 @@
     return jnp.exp2(power) * (high + low / 2048.0)
 
 
-def join_kernel(own_ref, row_ref, got_ref, one_ref, two_ref):
-    classes, wide = own_ref.shape[0], one_ref.shape[1]
-    for k, ref in enumerate((one_ref, two_ref)):
-        here = slice(k * wide, (k + 1) * wide)
-        vectors = [row_ref[:1] + got_ref[classes : classes + 1, : 2 * LANES]] if k == 0 else []
-        pack_halves(ref, own_ref[:, here] + got_ref[:classes, here], vectors)
-
-
-def join(own, row, got):
+def join_first_kernel(own_ref, row_ref, got_ref, sum_ref):
+    classes, wide = own_ref.shape[0], sum_ref.shape[1]
+    vector = row_ref[:1] + got_ref[classes : classes + 1, : 2 * LANES]
+    pack_halves(sum_ref, own_ref[:, :wide] + got_ref[:classes], [vector])
+
+
+def join_second_kernel(own_ref, got_ref, sum_ref):
+    pack_halves(sum_ref, own_ref[:, sum_ref.shape[1] :] + got_ref[...], [])
+
+
+def join(own, row, first, second):
     half = shape((own.shape[0] + SCALARS, own.shape[1] // 2), F32)
-    return call(join_kernel, "join", [half, half], 1 << 20, arrays=3)(own, row, got)
+    return (
+        call(join_first_kernel, "join_first", half, 1 << 20, arrays=3)(own, row, first),
+        call(join_second_kernel, "join_second", half, 1 << 20, arrays=2)(own, second),
+    )
 
 
 def add_kernel(own_ref, got_ref, sum_ref):
@@ -650,11 +661,13 @@
         array = lax.reduce_precision(array, 5, 10)
         return array, over_y(array.astype(F16), flip).astype(F32)
 
-    def sum_examples(own, row, got):
-        one, two = join(own, row, got)
-        one, two = swap(one, 1), swap(two, 3)
+    def sum_examples(send):
+        first, second, flat, row = backward_other(core, trade(send), turned, classes)
+        got = over_cores(first), over_cores(second)
+        one, two = join(backward_own(core, flat, turned), row, *got)
+        one, two = swap(one, 3), swap(two, 1)
         one, two = add_halves(*one), add_halves(*two)
-        return *swap(one, 3), *swap(two, 1)
+        return (*swap(one, 1), *swap(two, 3)), got[0]
 
     offset = lax.axis_index("ctr") * share
     label = lax.dynamic_slice_in_dim(labels, offset, share, 0).reshape(1, share)
@@ -669,19 +682,14 @@
     base = jnp.sum(trade_halves(rows), axis=0)
     hessian, send = gradient(base, label, weight, n_ctr)
 
-    other, flat, row = backward_other(core, trade(send), turned, classes)
-    got = over_cores(other)
-    own = backward_own(core, flat, turned)
+    sums, got = sum_examples(send)
     got, late_core = lax.optimization_barrier((got, core))
     blocks = factors(late_core, precond)
-    sums = sum_examples(own, row, got)
     residual, lifted = first_residual(total, sums, blocks)
     rows = forward(core, lifted, over_cores(lifted), tile, share)
     image, norm, send = weigh(trade_halves(rows), hessian)
 
-    other, flat, row = backward_other(core, trade(send), turned, classes)
-    got = over_cores(other)
-    sums = sum_examples(backward_own(core, flat, turned), row, got)
+    sums, _ = sum_examples(send)
     lifted, rough = step(total, sums, blocks, residual, norm)
     rows = forward(core, lifted, over_cores(lifted), tile, share)
     last, scales, curve = last_curve(trade_halves(rows), hessian, image, norm, rough)

time: 166 us -> 165 us (level)
  waiting for transfers between devices: 30.4 us -> 27.9 us
    ppermute x4 -> x6, waiting for transfers between devices: 4.04 us -> 2.12 us  [over_cores(): return lax.ppermute(array, 'ex', core_pairs)]
  transfers between devices with their start and end apart: 13 -> 15, of which waited for: 11 -> 11; matrix products, arithmetic and copies ran while one was open for 1% -> 1% of each run, Pallas kernels for 3% -> 4%
where the time goes in v8:
time: 165 us; the launch traced here: 164 us
  blocking collectives  90.4 us (55%)
  waiting for transfers between devices  27.9 us (17%)
  Pallas kernels  21.2 us (13%)
  starting transfers between devices  20.1 us (12%)
  other arithmetic  2.03 us (1%)
  local copies, waits for them, and re-layouts  1.74 us (1%)
    all_to_all x5, blocking collectives, trade(): return lax.all_to_all(parts, 'ctr', 0, 0)  75.6 us
    ppermute x8, waiting for transfers between devices, over_y(): return lax.ppermute(array, 'ex', pairs)  15.8 us
    all_to_all x1, blocking collectives, shards(): curve = lax.all_to_all(curve, ('ex', 'ctr'), 0, 0)  14.7 us
    ppermute x8, starting transfers between devices, over_y(): return lax.ppermute(array, 'ex', pairs)  10.8 us
    all_to_all x1, waiting for transfers between devices, trade(): return lax.all_to_all(parts, 'ctr', 0, 0)  9.98 us
    all_to_all x1, starting transfers between devices, trade(): return lax.all_to_all(parts, 'ctr', 0, 0)  7.96 us
    pallas_call x1, Pallas kernels, make_tile(): call(tile_kernel, 'tile', [shape((count, examples), BF16), shape((example...  5.66 us
  transfers between devices with their start and end apart: 15, of which 11 were waited for; matrix products, arithmetic and copies ran while one was open for 1% of the time, Pallas kernels for 4%

profile of v8, /device:TPU:0, one launch (start us, length us, event | category | flops | bytes accessed | tf_op | source)
XLA Modules:
  0.0 163.7 jit_solution(11757578511751128534)
XLA Ops:
  0.0 0.8 copy-done.3
  0.8 0.9 copies.1
  1.7 8.0 %all-to-all-start = ((bf16[16,128,128]{2,1,0:T(8,128)(2,1)}), bf16[16,128,128]{2,1,0:T(8,128)(2,1)S(1)}, u32[]{:S(2)}, u32[]{:S(2)}) async-start(bf16[16,128,128]{2,1,0:T(8,128)(2,1)} %copies.1), calls=%async_computation | async-start | bytes 1048576 | tf_op jit(solution)/shard_map/all_to_all | solution.py:655
  9.7 0.7 prepare.1
  10.4 0.8 dynamic-slice_bitcast_fusion.weight_ref
  11.2 10.0 %all-to-all-done.pool_ref = bf16[16,128,128]{2,1,0:T(8,128)(2,1)S(1)} async-done(((bf16[16,128,128]{2,1,0:T(8,128)(2,1)}), bf16[16,128,128]{2,1,0:T(8,128)(2,1)S(1)}, u32[]{:S(2)}, u32[]{:S(2)}) %all-to-all-start) | async-done | bytes 524320 | tf_op jit(solution)/shard_map/all_to_all | solution.py:655
  21.2 5.7 %tile.1 = (bf16[2048,2048]{1,0:T(8,128)(2,1)S(1)}, bf16[2048,2048]{1,0:T(8,128)(2,1)S(1)}, f32[16,144,128]{2,1,0:T(8,128)S(1)}) custom-call(bf16[144,2048]{1,0:T(8,128)(2,1)S(1)} %copy-done.5, s32[1,2048]{1,0:T(1,128)S(1)} %get-tuple-element.47.chunk_ref, bf16[16,128,128]{2,1,0:T(8,128)(2,1)S(1)} %all-to-all-done.pool_ref, ...), custom_call_target="tpu_custom_call" | custom-call | flops 4294967296 | bytes 17956864 | tf_op jit(solution)/shard_map/tile/pallas_call | solution.py:237
  26.9 14.4 %all_to_all.35 = f16[16,144,128]{2,1,0:T(8,128)(2,1)S(1)} all-to-all(f16[16,144,128]{2,1,0:T(8,128)(2,1)S(1)} %convert_element_type.66), channel_id=1, replica_groups=mesh['ex'=8,'ctr'=16] {'ctr'}, dimensions={0} | all-to-all | bytes 1179648 | tf_op jit(solution)/shard_map/all_to_all | solution.py:655
  41.5 13.7 %all_to_all.36.values_ref = bf16[16,144,128]{2,1,0:T(8,128)(2,1)S(1)} all-to-all(bf16[16,144,128]{2,1,0:T(8,128)(2,1)S(1)} %get-tuple-element.54), channel_id=1, replica_groups=mesh['ex'=8,'ctr'=16] {'ctr'}, dimensions={0} | all-to-all | bytes 1179648 | tf_op jit(solution)/shard_map/all_to_all | solution.py:655
  55.1 0.8 backward_other.2
  56.0 0.1 collective-permute-start.3
  56.1 0.5 collective-permute-start
  56.6 0.8 backward_own.2.own_ref
  57.4 0.2 collective-permute-done.3.got_ref
  57.7 0.2 join_second.2
  57.8 0.2 reduce-precision_convert_fusion.5
  58.0 1.7 %collective-permute-start.4 = (f16[152,512]{1,0:T(8,128)(2,1)S(1)}, f16[152,512]{1,0:T(8,128)(2,1)S(1)}, u32[]{:S(2)}, u32[]{:S(2)}) collective-permute-start(f16[152,512]{1,0:T(8,128)(2,1)S(1)} %get-tuple-element.91), channel_id=1, source_target_pairs={{0,32},{16,48},{32,0},{48,16},{64,96},{80,112},{96,64},{112,80},{1... | collective-permute-start | bytes 466952 | tf_op jit(solution)/shard_map/ppermute | solution.py:649
  59.7 0.2 join_first.2
  59.8 0.2 reduce-precision_convert_fusion.7
  60.0 2.3 %collective-permute-start.1 = (f16[152,512]{1,0:T(8,128)(2,1)S(1)}, f16[152,512]{1,0:T(8,128)(2,1)S(1)}, u32[]{:S(2)}, u32[]{:S(2)}) collective-permute-start(f16[152,512]{1,0:T(8,128)(2,1)S(1)} %get-tuple-element.95), channel_id=1, source_target_pairs={{0,96},{16,112},{32,64},{48,80},{64,32},{80,48},{96,0},{112,16},{1... | collective-permute-start | bytes 466952 | tf_op jit(solution)/shard_map/ppermute | solution.py:649
  62.3 1.9 %collective-permute-done.4 = f16[152,512]{1,0:T(8,128)(2,1)S(1)} collective-permute-done((f16[152,512]{1,0:T(8,128)(2,1)S(1)}, f16[152,512]{1,0:T(8,128)(2,1)S(1)}, u32[]{:S(2)}, u32[]{:S(2)}) %collective-permute-start.4) | collective-permute-done | bytes 155680 | tf_op jit(solution)/shard_map/ppermute | solution.py:649
  64.2 0.4 add.15
  64.5 0.2 reduce-precision_convert_fusion.4
  64.7 3.1 %collective-permute-start.5 = (f16[152,512]{1,0:T(8,128)(2,1)S(1)}, f16[152,512]{1,0:T(8,128)(2,1)S(1)}, u32[]{:S(2)}, u32[]{:S(2)}) collective-permute-start(f16[152,512]{1,0:T(8,128)(2,1)S(1)} %get-tuple-element.89), channel_id=1, source_target_pairs={{0,96},{16,112},{32,64},{48,80},{64,32},{80,48},{96,0},{112,16},{1... | collective-permute-start | bytes 466952 | tf_op jit(solution)/shard_map/ppermute | solution.py:649
  67.9 0.4 add.14
  68.2 0.2 reduce-precision_convert_fusion.6
  68.4 0.4 collective-permute-start.2
  68.8 0.3 factors.1
  69.1 2.2 %collective-permute-done.5 = f16[152,512]{1,0:T(8,128)(2,1)S(1)} collective-permute-done((f16[152,512]{1,0:T(8,128)(2,1)S(1)}, f16[152,512]{1,0:T(8,128)(2,1)S(1)}, u32[]{:S(2)}, u32[]{:S(2)}) %collective-permute-start.5) | collective-permute-done | bytes 155680 | tf_op jit(solution)/shard_map/ppermute | solution.py:649
  71.4 2.5 %collective-permute-done.2 = f16[152,512]{1,0:T(8,128)(2,1)S(1)} collective-permute-done((f16[152,512]{1,0:T(8,128)(2,1)S(1)}, f16[152,512]{1,0:T(8,128)(2,1)S(1)}, u32[]{:S(2)}, u32[]{:S(2)}) %collective-permute-start.2) | collective-permute-done | bytes 155680 | tf_op jit(solution)/shard_map/ppermute | solution.py:649
  73.9 1.0 residual.1
  75.0 0.8 forward_own.2.first_ref
  75.9 0.8 collective-permute-done.6.other_ref
  76.7 0.9 forward.2
  77.7 16.0 %all_to_all.37 = f16[16,152,128]{2,1,0:T(8,128)(2,1)S(1)} all-to-all(f16[16,152,128]{2,1,0:T(8,128)(2,1)S(1)} %convert_element_type.76), channel_id=1, replica_groups=mesh['ex'=8,'ctr'=16] {'ctr'}, dimensions={0} | all-to-all | bytes 1245184 | tf_op jit(solution)/shard_map/all_to_all | solution.py:655
  93.7 0.7 weigh.1
  94.4 15.7 %all_to_all.38.values_ref = bf16[16,160,128]{2,1,0:T(8,128)(2,1)S(1)} all-to-all(bf16[16,160,128]{2,1,0:T(8,128)(2,1)S(1)} %get-tuple-element.68), channel_id=1, replica_groups=mesh['ex'=8,'ctr'=16] {'ctr'}, dimensions={0} | all-to-all | bytes 1310720 | tf_op jit(solution)/shard_map/all_to_all | solution.py:655
  110.1 0.8 backward_other.3
  111.0 0.5 collective-permute-start.7
  111.5 0.8 backward_own.3.own_ref
  112.3 0.3 collective-permute-done.10.got_ref
  112.6 0.2 join_second.3
  112.8 0.2 reduce-precision_convert_fusion.1
  113.0 0.2 collective-permute-start.11
  113.2 0.2 join_first.3
  113.4 0.2 reduce-precision_convert_fusion.3
  113.5 1.5 collective-permute-start.8
  115.0 4.1 %collective-permute-done.11 = f16[152,512]{1,0:T(8,128)(2,1)S(1)} collective-permute-done((f16[152,512]{1,0:T(8,128)(2,1)S(1)}, f16[152,512]{1,0:T(8,128)(2,1)S(1)}, u32[]{:S(2)}, u32[]{:S(2)}) %collective-permute-start.11) | collective-permute-done | bytes 155680 | tf_op jit(solution)/shard_map/ppermute | solution.py:649
  119.1 0.4 add.17
  119.5 0.2 reduce-precision_convert_fusion
  119.7 1.5 collective-permute-start.12
  121.2 0.4 add.16
  121.6 0.2 reduce-precision_convert_fusion.2
  121.7 0.2 collective-permute-start.9
  121.9 4.3 %collective-permute-done.12 = f16[152,512]{1,0:T(8,128)(2,1)S(1)} collective-permute-done((f16[152,512]{1,0:T(8,128)(2,1)S(1)}, f16[152,512]{1,0:T(8,128)(2,1)S(1)}, u32[]{:S(2)}, u32[]{:S(2)}) %collective-permute-start.12) | collective-permute-done | bytes 155680 | tf_op jit(solution)/shard_map/ppermute | solution.py:649
  126.2 0.8 collective-permute-done.9
  127.1 1.1 step.1
  128.3 0.8 forward_own.3.first_ref
  129.1 0.8 collective-permute-done.13.other_ref
  129.9 0.9 forward.3
  130.9 16.0 %all_to_all.39 = f16[16,152,128]{2,1,0:T(8,128)(2,1)S(1)} all-to-all(f16[16,152,128]{2,1,0:T(8,128)(2,1)S(1)} %convert_element_type.86), channel_id=1, replica_groups=mesh['ex'=8,'ctr'=16] {'ctr'}, dimensions={0} | all-to-all | bytes 1245184 | tf_op jit(solution)/shard_map/all_to_all | solution.py:655
  147.0 0.9 curve.1
  148.0 14.7 %all_to_all.40.curve_ref = f32[128,1,256]{2,1,0:T(1,128)S(1)} all-to-all(f32[128,1,256]{2,1,0:T(1,128)S(1)} %broadcast_in_dim.3), channel_id=1, replica_groups=mesh['ex'=8,'ctr'=16] {'ex','ctr'}, dimensions={0} | all-to-all | bytes 262144 | tf_op jit(solution)/shard_map/all_to_all | solution.py:698
  162.7 0.9 margins.1
  (35 shorter events, 1.2 us)
Async XLA Ops:
  0.0 10.3 %copy-start = (s32[2048]{0:T(1024)S(1)}, s32[2048]{0:T(1024)}, u32[]{:S(2)}) copy-start(s32[2048]{0:T(1024)} %param.9) | copy-start | bytes 24580
  0.0 9.7 %copy-start.2 = (bf16[64,2048]{1,0:T(8,128)(2,1)S(1)}, bf16[64,2048]{1,0:T(8,128)(2,1)}, u32[]{:S(2)}) copy-start(bf16[64,2048]{1,0:T(8,128)(2,1)} %centers_ref.1) | copy-start | bytes 786436
  0.0 0.8 copy-start.3
  0.8 8.9 %copy-start.4 = (s32[2048]{0:T(1024)S(1)}, s32[2048]{0:T(1024)}, u32[]{:S(2)}) copy-start(s32[2048]{0:T(1024)} %param.8) | copy-start | bytes 24580
  0.8 20.4 %copy-start.5 = (bf16[144,2048]{1,0:T(8,128)(2,1)S(1)}, bf16[144,2048]{1,0:T(8,128)(2,1)}, u32[]{:S(2)}) copy-start(bf16[144,2048]{1,0:T(8,128)(2,1)} %alpha_hbm.1) | copy-start | bytes 1769476
  1.7 19.5 %all-to-all-start = ((bf16[16,128,128]{2,1,0:T(8,128)(2,1)}), bf16[16,128,128]{2,1,0:T(8,128)(2,1)S(1)}, u32[]{:S(2)}, u32[]{:S(2)}) async-start(bf16[16,128,128]{2,1,0:T(8,128)(2,1)} %copies.1), calls=%async_computation | async-start | bytes 1048576 | tf_op jit(solution)/shard_map/all_to_all | solution.py:655
  56.0 1.7 %collective-permute-start.3 = (f32[144,512]{1,0:T(8,128)S(1)}, f32[144,512]{1,0:T(8,128)S(1)}, u32[]{:S(2)}, u32[]{:S(2)}) collective-permute-start(f32[144,512]{1,0:T(8,128)S(1)} %get-tuple-element.59), channel_id=1, source_target_pairs={{0,16},{16,0},{32,48},{48,32},{64,80},{80,64},{96,112},{112,96},{1... | collective-permute-start | bytes 884744 | tf_op jit(solution)/shard_map/ppermute | solution.py:652
  56.1 3.6 %collective-permute-start = (f32[152,512]{1,0:T(8,128)S(1)}, f32[152,512]{1,0:T(8,128)S(1)}, u32[]{:S(2)}, u32[]{:S(2)}) collective-permute-start(f32[152,512]{1,0:T(8,128)S(1)} %get-tuple-element.58), channel_id=1, source_target_pairs={{0,16},{16,0},{32,48},{48,32},{64,80},{80,64},{96,112},{112,96},{1... | collective-permute-start | bytes 933896 | tf_op jit(solution)/shard_map/ppermute | solution.py:652
  58.0 6.1 %collective-permute-start.4 = (f16[152,512]{1,0:T(8,128)(2,1)S(1)}, f16[152,512]{1,0:T(8,128)(2,1)S(1)}, u32[]{:S(2)}, u32[]{:S(2)}) collective-permute-start(f16[152,512]{1,0:T(8,128)(2,1)S(1)} %get-tuple-element.91), channel_id=1, source_target_pairs={{0,32},{16,48},{32,0},{48,16},{64,96},{80,112},{96,64},{112,80},{1... | collective-permute-start | bytes 466952 | tf_op jit(solution)/shard_map/ppermute | solution.py:649
  60.0 7.8 %collective-permute-start.1 = (f16[152,512]{1,0:T(8,128)(2,1)S(1)}, f16[152,512]{1,0:T(8,128)(2,1)S(1)}, u32[]{:S(2)}, u32[]{:S(2)}) collective-permute-start(f16[152,512]{1,0:T(8,128)(2,1)S(1)} %get-tuple-element.95), channel_id=1, source_target_pairs={{0,96},{16,112},{32,64},{48,80},{64,32},{80,48},{96,0},{112,16},{1... | collective-permute-start | bytes 466952 | tf_op jit(solution)/shard_map/ppermute | solution.py:649
  64.7 4.1 %copy-start.1 = (f32[2048,256]{1,0:T(8,128)S(1)}, f32[2048,256]{1,0:T(8,128)}, u32[]{:S(2)}) copy-start(f32[2048,256]{1,0:T(8,128)} %precond_ref.1) | copy-start | bytes 6291460
  64.7 6.6 %collective-permute-start.5 = (f16[152,512]{1,0:T(8,128)(2,1)S(1)}, f16[152,512]{1,0:T(8,128)(2,1)S(1)}, u32[]{:S(2)}, u32[]{:S(2)}) collective-permute-start(f16[152,512]{1,0:T(8,128)(2,1)S(1)} %get-tuple-element.89), channel_id=1, source_target_pairs={{0,96},{16,112},{32,64},{48,80},{64,32},{80,48},{96,0},{112,16},{1... | collective-permute-start | bytes 466952 | tf_op jit(solution)/shard_map/ppermute | solution.py:649
  68.4 5.5 %collective-permute-start.2 = (f16[152,512]{1,0:T(8,128)(2,1)S(1)}, f16[152,512]{1,0:T(8,128)(2,1)S(1)}, u32[]{:S(2)}, u32[]{:S(2)}) collective-permute-start(f16[152,512]{1,0:T(8,128)(2,1)S(1)} %get-tuple-element.93), channel_id=1, source_target_pairs={{0,32},{16,48},{32,0},{48,16},{64,96},{80,112},{96,64},{112,80},{1... | collective-permute-start | bytes 466952 | tf_op jit(solution)/shard_map/ppermute | solution.py:649
  74.9 1.7 %collective-permute-start.6 = (bf16[160,1024]{1,0:T(8,128)(2,1)S(1)}, bf16[160,1024]{1,0:T(8,128)(2,1)S(1)}, u32[]{:S(2)}, u32[]{:S(2)}) collective-permute-start(bf16[160,1024]{1,0:T(8,128)(2,1)S(1)} %get-tuple-element.65.own_ref), channel_id=1, source_target_pairs={{0,16},{16,0},{32,48},{48,32},{64,80},{80,64},{96,112},{112,96},{1... | collective-permute-start | bytes 983048 | tf_op jit(solution)/shard_map/ppermute | solution.py:652
  110.9 1.7 %collective-permute-start.10 = (f32[144,512]{1,0:T(8,128)S(1)}, f32[144,512]{1,0:T(8,128)S(1)}, u32[]{:S(2)}, u32[]{:S(2)}) collective-permute-start(f32[144,512]{1,0:T(8,128)S(1)} %get-tuple-element.72), channel_id=1, source_target_pairs={{0,16},{16,0},{32,48},{48,32},{64,80},{80,64},{96,112},{112,96},{1... | collective-permute-start | bytes 884744 | tf_op jit(solution)/shard_map/ppermute | solution.py:652
  111.0 2.2 %collective-permute-start.7 = (f32[152,512]{1,0:T(8,128)S(1)}, f32[152,512]{1,0:T(8,128)S(1)}, u32[]{:S(2)}, u32[]{:S(2)}) collective-permute-start(f32[152,512]{1,0:T(8,128)S(1)} %get-tuple-element.71), channel_id=1, source_target_pairs={{0,16},{16,0},{32,48},{48,32},{64,80},{80,64},{96,112},{112,96},{1... | collective-permute-start | bytes 933896 | tf_op jit(solution)/shard_map/ppermute | solution.py:652
  113.0 6.1 %collective-permute-start.11 = (f16[152,512]{1,0:T(8,128)(2,1)S(1)}, f16[152,512]{1,0:T(8,128)(2,1)S(1)}, u32[]{:S(2)}, u32[]{:S(2)}) collective-permute-start(f16[152,512]{1,0:T(8,128)(2,1)S(1)} %get-tuple-element.83), channel_id=1, source_target_pairs={{0,32},{16,48},{32,0},{48,16},{64,96},{80,112},{96,64},{112,80},{1... | collective-permute-start | bytes 466952 | tf_op jit(solution)/shard_map/ppermute | solution.py:649
  113.5 7.6 %collective-permute-start.8 = (f16[152,512]{1,0:T(8,128)(2,1)S(1)}, f16[152,512]{1,0:T(8,128)(2,1)S(1)}, u32[]{:S(2)}, u32[]{:S(2)}) collective-permute-start(f16[152,512]{1,0:T(8,128)(2,1)S(1)} %get-tuple-element.87), channel_id=1, source_target_pairs={{0,96},{16,112},{32,64},{48,80},{64,32},{80,48},{96,0},{112,16},{1... | collective-permute-start | bytes 466952 | tf_op jit(solution)/shard_map/ppermute | solution.py:649
  119.7 6.5 %collective-permute-start.12 = (f16[152,512]{1,0:T(8,128)(2,1)S(1)}, f16[152,512]{1,0:T(8,128)(2,1)S(1)}, u32[]{:S(2)}, u32[]{:S(2)}) collective-permute-start(f16[152,512]{1,0:T(8,128)(2,1)S(1)} %get-tuple-element.81), channel_id=1, source_target_pairs={{0,96},{16,112},{32,64},{48,80},{64,32},{80,48},{96,0},{112,16},{1... | collective-permute-start | bytes 466952 | tf_op jit(solution)/shard_map/ppermute | solution.py:649
  121.7 5.3 %collective-permute-start.9 = (f16[152,512]{1,0:T(8,128)(2,1)S(1)}, f16[152,512]{1,0:T(8,128)(2,1)S(1)}, u32[]{:S(2)}, u32[]{:S(2)}) collective-permute-start(f16[152,512]{1,0:T(8,128)(2,1)S(1)} %get-tuple-element.85), channel_id=1, source_target_pairs={{0,32},{16,48},{32,0},{48,16},{64,96},{80,112},{96,64},{112,80},{1... | collective-permute-start | bytes 466952 | tf_op jit(solution)/shard_map/ppermute | solution.py:649
  128.2 1.7 %collective-permute-start.13 = (bf16[160,1024]{1,0:T(8,128)(2,1)S(1)}, bf16[160,1024]{1,0:T(8,128)(2,1)S(1)}, u32[]{:S(2)}, u32[]{:S(2)}) collective-permute-start(bf16[160,1024]{1,0:T(8,128)(2,1)S(1)} %get-tuple-element.75.own_ref), channel_id=1, source_target_pairs={{0,16},{16,0},{32,48},{48,32},{64,80},{80,64},{96,112},{112,96},{1... | collective-permute-start | bytes 983048 | tf_op jit(solution)/shard_map/ppermute | solution.py:652

commit v9 on v8

--- a/solution.py
+++ b/solution.py
@@ -112,6 +112,11 @@
     return total
 
 
+def columns(vectors, classes):
+    turned = stack_rows(vectors).T
+    return [turned[:classes, k : k + 1] for k in range(len(vectors))]
+
+
 def column(vector, classes):
     return jnp.broadcast_to(vector, (8, vector.shape[1])).T[:classes, :1]
 
@@ -128,13 +133,6 @@
     for k, vector in enumerate(vectors):
         out = jnp.where(row == k, vector, out)
     return out
-
-
-def sum_parts(ref):
-    total = ref[0].astype(F32)
-    for k in range(1, ref.shape[0]):
-        total = total + ref[k].astype(F32)
-    return total
 
 
 def shape(dims, dtype):
@@ -418,13 +416,9 @@
     )(core, flat, turned)
 
 
-def pack_halves(ref, values, vectors):
+def put_halves(ref, values, powers, vectors):
     classes, wide = values.shape
-    size = jnp.max(jnp.abs(values), axis=1, keepdims=True)
-    powers = exponents(size) - 14.0
-    ref[:classes] = values * jnp.exp2(-powers)
-    empty = jnp.zeros((2 * LANES - classes, LANES), F32)
-    powers = jnp.concatenate([jnp.broadcast_to(powers, (classes, LANES)), empty], axis=0).T[:1]
+    ref[:classes] = values
     row = lax.broadcasted_iota(jnp.int32, (SCALARS, 2 * LANES), 0)
     out = jnp.zeros((SCALARS, 2 * LANES), F32)
     for p, piece in enumerate(half_pieces(powers, vectors)):
@@ -433,9 +427,26 @@
     ref[classes:, 2 * LANES :] = jnp.zeros((SCALARS, wide - 2 * LANES), F32)
 
 
-def unpack_halves(ref):
+def pack_halves(ref, values, vectors):
+    classes = values.shape[0]
+    size = jnp.max(jnp.abs(values), axis=1, keepdims=True)
+    powers = exponents(size) - 14.0
+    empty = jnp.zeros((2 * LANES - classes, LANES), F32)
+    row = jnp.concatenate([jnp.broadcast_to(powers, (classes, LANES)), empty], axis=0).T[:1]
+    put_halves(ref, values * jnp.exp2(-powers), row, vectors)
+
+
+def powers_of(ref):
     classes = ref.shape[0] - SCALARS
-    return ref[:classes] * column(jnp.exp2(ref[classes : classes + 1, : 2 * LANES]), classes)
+    return ref[classes : classes + 1, : 2 * LANES]
+
+
+def unpack_pairs(pairs):
+    refs = [ref for pair in pairs for ref in pair]
+    classes = refs[0].shape[0] - SCALARS
+    scales = columns([jnp.exp2(powers_of(ref)) for ref in refs], classes)
+    values = [ref[:classes] * scale for ref, scale in zip(refs, scales)]
+    return [values[2 * k] + values[2 * k + 1] for k in range(len(pairs))]
 
 
 def unpack_vector(ref):
@@ -463,8 +474,13 @@
 
 
 def add_kernel(own_ref, got_ref, sum_ref):
+    classes = own_ref.shape[0] - SCALARS
+    powers = jnp.maximum(powers_of(own_ref), powers_of(got_ref)) + 1.0
+    own, got = columns(
+        [jnp.exp2(powers_of(own_ref) - powers), jnp.exp2(powers_of(got_ref) - powers)], classes
+    )
     vector = unpack_vector(own_ref) + unpack_vector(got_ref)
-    pack_halves(sum_ref, unpack_halves(own_ref) + unpack_halves(got_ref), [vector])
+    put_halves(sum_ref, own_ref[:classes] * own + got_ref[:classes] * got, powers, [vector])
 
 
 def add_halves(own, got):
@@ -497,8 +513,7 @@
     total, one_ref, one_in_ref, two_ref, two_in_ref, high_ref, low_ref, high_turned_ref,
     low_turned_ref, residual_ref, lifted_ref,
 ):
-    one = unpack_halves(one_ref) + unpack_halves(one_in_ref)
-    two = unpack_halves(two_ref) + unpack_halves(two_in_ref)
+    one, two = unpack_pairs(((one_ref, one_in_ref), (two_ref, two_in_ref)))
     sums = jnp.concatenate([one, two], axis=1)
     residual = block_products(sums, high_ref, low_ref) * (-1.0 / total)
     residual_ref[...] = residual
@@ -553,8 +568,7 @@
     low_turned_ref, residual_ref, norm_ref, lifted_ref, rough_ref,
 ):
     classes = residual_ref.shape[0]
-    one = unpack_halves(one_ref) + unpack_halves(one_in_ref)
-    two = unpack_halves(two_ref) + unpack_halves(two_in_ref)
+    one, two = unpack_pairs(((one_ref, one_in_ref), (two_ref, two_in_ref)))
     curve = (unpack_vector(one_ref) + unpack_vector(one_in_ref)) / total
     norm = norm_ref[:1]
     lane = lax.broadcasted_iota(jnp.int32, (1, 2 * LANES), 1)
@@ -598,7 +612,8 @@
     scales_ref[...] = stack_rows(
         [rough_ref[:1] * grown, grown, ratio - excess, norm_next, ridge]
     )
-    rows = column(grown, classes) * last + column(ratio - excess, classes) * image_ref[...]
+    scale, other = columns([grown, ratio - excess], classes)
+    rows = scale * last + other * image_ref[...]
     weighted = (hessian_ref[...] * rows).astype(BF16).astype(F32)
     curve_ref[...] = lane_sums(weighted * rows)
 
@@ -622,11 +637,8 @@
     second = jnp.where(
         lane < classes, scales_ref[3:4] / (curve / total + scales_ref[4:5]), 0.0
     )
-    margins_ref[...] = (
-        base_ref[...]
-        + column(first + second * other, classes) * image_ref[...]
-        + column(second * grown, classes) * last_ref[...]
-    )
+    image_scale, last_scale = columns([first + second * other, second * grown], classes)
+    margins_ref[...] = base_ref[...] + image_scale * image_ref[...] + last_scale * last_ref[...]
 
 
 def margins(total, curve, scales, base, image, last):

time: 165 us -> 165 us (level)
  no operation moved by 1% of the time
where the time goes in v9:
time: 165 us; the launch traced here: 163 us
  blocking collectives  90.3 us (55%)
  waiting for transfers between devices  27.8 us (17%)
  Pallas kernels  20.6 us (12%)
  starting transfers between devices  20.3 us (12%)
  other arithmetic  2.02 us (1%)
  local copies, waits for them, and re-layouts  1.74 us (1%)
    all_to_all x5, blocking collectives, trade(): return lax.all_to_all(parts, 'ctr', 0, 0)  75.6 us
    ppermute x8, waiting for transfers between devices, over_y(): return lax.ppermute(array, 'ex', pairs)  15.7 us
    all_to_all x1, blocking collectives, shards(): curve = lax.all_to_all(curve, ('ex', 'ctr'), 0, 0)  14.6 us
    ppermute x8, starting transfers between devices, over_y(): return lax.ppermute(array, 'ex', pairs)  11 us
    all_to_all x1, waiting for transfers between devices, trade(): return lax.all_to_all(parts, 'ctr', 0, 0)  9.98 us
    all_to_all x1, starting transfers between devices, trade(): return lax.all_to_all(parts, 'ctr', 0, 0)  7.96 us
    pallas_call x1, Pallas kernels, make_tile(): call(tile_kernel, 'tile', [shape((count, examples), BF16), shape((example...  5.66 us
  transfers between devices with their start and end apart: 15, of which 11 were waited for; matrix products, arithmetic and copies ran while one was open for 1% of the time, Pallas kernels for 4%

profile of v9, /device:TPU:0, one launch (start us, length us, event | category | flops | bytes accessed | tf_op | source)
XLA Modules:
  0.0 163.1 jit_solution(17649508283921493936)
XLA Ops:
  0.0 0.8 copy-done.3
  0.8 0.9 copies.1
  1.7 8.0 %all-to-all-start = ((bf16[16,128,128]{2,1,0:T(8,128)(2,1)}), bf16[16,128,128]{2,1,0:T(8,128)(2,1)S(1)}, u32[]{:S(2)}, u32[]{:S(2)}) async-start(bf16[16,128,128]{2,1,0:T(8,128)(2,1)} %copies.1), calls=%async_computation | async-start | bytes 1048576 | tf_op jit(solution)/shard_map/all_to_all | solution.py:667
  9.7 0.7 prepare.1
  10.4 0.8 dynamic-slice_bitcast_fusion.weight_ref
  11.2 10.0 %all-to-all-done.pool_ref = bf16[16,128,128]{2,1,0:T(8,128)(2,1)S(1)} async-done(((bf16[16,128,128]{2,1,0:T(8,128)(2,1)}), bf16[16,128,128]{2,1,0:T(8,128)(2,1)S(1)}, u32[]{:S(2)}, u32[]{:S(2)}) %all-to-all-start) | async-done | bytes 524320 | tf_op jit(solution)/shard_map/all_to_all | solution.py:667
  21.2 5.7 %tile.1 = (bf16[2048,2048]{1,0:T(8,128)(2,1)S(1)}, bf16[2048,2048]{1,0:T(8,128)(2,1)S(1)}, f32[16,144,128]{2,1,0:T(8,128)S(1)}) custom-call(bf16[144,2048]{1,0:T(8,128)(2,1)S(1)} %copy-done.5, s32[1,2048]{1,0:T(1,128)S(1)} %get-tuple-element.47.chunk_ref, bf16[16,128,128]{2,1,0:T(8,128)(2,1)S(1)} %all-to-all-done.pool_ref, ...), custom_call_target="tpu_custom_call" | custom-call | flops 4294967296 | bytes 17956864 | tf_op jit(solution)/shard_map/tile/pallas_call | solution.py:235
  26.9 14.4 %all_to_all.35 = f16[16,144,128]{2,1,0:T(8,128)(2,1)S(1)} all-to-all(f16[16,144,128]{2,1,0:T(8,128)(2,1)S(1)} %convert_element_type.66), channel_id=1, replica_groups=mesh['ex'=8,'ctr'=16] {'ctr'}, dimensions={0} | all-to-all | bytes 1179648 | tf_op jit(solution)/shard_map/all_to_all | solution.py:667
  41.5 13.7 %all_to_all.36.values_ref = bf16[16,144,128]{2,1,0:T(8,128)(2,1)S(1)} all-to-all(bf16[16,144,128]{2,1,0:T(8,128)(2,1)S(1)} %get-tuple-element.54), channel_id=1, replica_groups=mesh['ex'=8,'ctr'=16] {'ctr'}, dimensions={0} | all-to-all | bytes 1179648 | tf_op jit(solution)/shard_map/all_to_all | solution.py:667
  55.1 0.8 backward_other.2
  56.0 0.1 collective-permute-start.3
  56.1 0.5 collective-permute-start
  56.6 0.8 backward_own.2.own_ref
  57.4 0.2 collective-permute-done.3.got_ref
  57.7 0.2 join_second.2
  57.8 0.2 reduce-precision_convert_fusion.5
  58.0 1.7 %collective-permute-start.4 = (f16[152,512]{1,0:T(8,128)(2,1)S(1)}, f16[152,512]{1,0:T(8,128)(2,1)S(1)}, u32[]{:S(2)}, u32[]{:S(2)}) collective-permute-start(f16[152,512]{1,0:T(8,128)(2,1)S(1)} %get-tuple-element.91), channel_id=1, source_target_pairs={{0,32},{16,48},{32,0},{48,16},{64,96},{80,112},{96,64},{112,80},{1... | collective-permute-start | bytes 466952 | tf_op jit(solution)/shard_map/ppermute | solution.py:661
  59.7 0.2 join_first.2
  59.8 0.2 reduce-precision_convert_fusion.7
  60.0 2.3 %collective-permute-start.1 = (f16[152,512]{1,0:T(8,128)(2,1)S(1)}, f16[152,512]{1,0:T(8,128)(2,1)S(1)}, u32[]{:S(2)}, u32[]{:S(2)}) collective-permute-start(f16[152,512]{1,0:T(8,128)(2,1)S(1)} %get-tuple-element.95), channel_id=1, source_target_pairs={{0,96},{16,112},{32,64},{48,80},{64,32},{80,48},{96,0},{112,16},{1... | collective-permute-start | bytes 466952 | tf_op jit(solution)/shard_map/ppermute | solution.py:661
  62.3 1.9 %collective-permute-done.4 = f16[152,512]{1,0:T(8,128)(2,1)S(1)} collective-permute-done((f16[152,512]{1,0:T(8,128)(2,1)S(1)}, f16[152,512]{1,0:T(8,128)(2,1)S(1)}, u32[]{:S(2)}, u32[]{:S(2)}) %collective-permute-start.4) | collective-permute-done | bytes 155680 | tf_op jit(solution)/shard_map/ppermute | solution.py:661
  64.2 0.3 add.15
  64.5 0.2 reduce-precision_convert_fusion.4
  64.6 3.1 %collective-permute-start.5 = (f16[152,512]{1,0:T(8,128)(2,1)S(1)}, f16[152,512]{1,0:T(8,128)(2,1)S(1)}, u32[]{:S(2)}, u32[]{:S(2)}) collective-permute-start(f16[152,512]{1,0:T(8,128)(2,1)S(1)} %get-tuple-element.89), channel_id=1, source_target_pairs={{0,96},{16,112},{32,64},{48,80},{64,32},{80,48},{96,0},{112,16},{1... | collective-permute-start | bytes 466952 | tf_op jit(solution)/shard_map/ppermute | solution.py:661
  67.8 0.3 add.14
  68.0 0.2 reduce-precision_convert_fusion.6
  68.2 0.4 collective-permute-start.2
  68.6 0.3 factors.1
  69.0 2.3 %collective-permute-done.5 = f16[152,512]{1,0:T(8,128)(2,1)S(1)} collective-permute-done((f16[152,512]{1,0:T(8,128)(2,1)S(1)}, f16[152,512]{1,0:T(8,128)(2,1)S(1)}, u32[]{:S(2)}, u32[]{:S(2)}) %collective-permute-start.5) | collective-permute-done | bytes 155680 | tf_op jit(solution)/shard_map/ppermute | solution.py:661
  71.3 2.4 %collective-permute-done.2 = f16[152,512]{1,0:T(8,128)(2,1)S(1)} collective-permute-done((f16[152,512]{1,0:T(8,128)(2,1)S(1)}, f16[152,512]{1,0:T(8,128)(2,1)S(1)}, u32[]{:S(2)}, u32[]{:S(2)}) %collective-permute-start.2) | collective-permute-done | bytes 155680 | tf_op jit(solution)/shard_map/ppermute | solution.py:661
  73.7 1.0 residual.1
  74.8 0.8 forward_own.2.first_ref
  75.6 0.8 collective-permute-done.6.other_ref
  76.4 0.9 forward.2
  77.4 16.0 %all_to_all.37 = f16[16,152,128]{2,1,0:T(8,128)(2,1)S(1)} all-to-all(f16[16,152,128]{2,1,0:T(8,128)(2,1)S(1)} %convert_element_type.76), channel_id=1, replica_groups=mesh['ex'=8,'ctr'=16] {'ctr'}, dimensions={0} | all-to-all | bytes 1245184 | tf_op jit(solution)/shard_map/all_to_all | solution.py:667
  93.5 0.7 weigh.1
  94.2 15.7 %all_to_all.38.values_ref = bf16[16,160,128]{2,1,0:T(8,128)(2,1)S(1)} all-to-all(bf16[16,160,128]{2,1,0:T(8,128)(2,1)S(1)} %get-tuple-element.68), channel_id=1, replica_groups=mesh['ex'=8,'ctr'=16] {'ctr'}, dimensions={0} | all-to-all | bytes 1310720 | tf_op jit(solution)/shard_map/all_to_all | solution.py:667
  109.9 0.8 backward_other.3
  110.8 0.5 collective-permute-start.7
  111.3 0.8 backward_own.3.own_ref
  112.1 0.3 collective-permute-done.10.got_ref
  112.4 0.2 join_second.3
  112.6 0.2 reduce-precision_convert_fusion.1
  112.7 0.2 collective-permute-start.11
  112.9 0.2 join_first.3
  113.1 0.2 reduce-precision_convert_fusion.3
  113.3 1.5 collective-permute-start.8
  114.8 4.0 %collective-permute-done.11 = f16[152,512]{1,0:T(8,128)(2,1)S(1)} collective-permute-done((f16[152,512]{1,0:T(8,128)(2,1)S(1)}, f16[152,512]{1,0:T(8,128)(2,1)S(1)}, u32[]{:S(2)}, u32[]{:S(2)}) %collective-permute-start.11) | collective-permute-done | bytes 155680 | tf_op jit(solution)/shard_map/ppermute | solution.py:661
  118.9 0.3 add.17
  119.2 0.2 reduce-precision_convert_fusion
  119.3 1.6 collective-permute-start.12
  121.0 0.3 add.16
  121.3 0.2 reduce-precision_convert_fusion.2
  121.4 0.2 collective-permute-start.9
  121.6 4.3 %collective-permute-done.12 = f16[152,512]{1,0:T(8,128)(2,1)S(1)} collective-permute-done((f16[152,512]{1,0:T(8,128)(2,1)S(1)}, f16[152,512]{1,0:T(8,128)(2,1)S(1)}, u32[]{:S(2)}, u32[]{:S(2)}) %collective-permute-start.12) | collective-permute-done | bytes 155680 | tf_op jit(solution)/shard_map/ppermute | solution.py:661
  125.9 0.8 collective-permute-done.9
  126.8 1.0 step.1
  127.9 0.8 forward_own.3.first_ref
  128.7 0.8 collective-permute-done.13.other_ref
  129.5 0.9 forward.3
  130.5 16.0 %all_to_all.39 = f16[16,152,128]{2,1,0:T(8,128)(2,1)S(1)} all-to-all(f16[16,152,128]{2,1,0:T(8,128)(2,1)S(1)} %convert_element_type.86), channel_id=1, replica_groups=mesh['ex'=8,'ctr'=16] {'ctr'}, dimensions={0} | all-to-all | bytes 1245184 | tf_op jit(solution)/shard_map/all_to_all | solution.py:667
  146.6 0.9 curve.1
  147.5 14.6 %all_to_all.40.curve_ref = f32[128,1,256]{2,1,0:T(1,128)S(1)} all-to-all(f32[128,1,256]{2,1,0:T(1,128)S(1)} %broadcast_in_dim.3), channel_id=1, replica_groups=mesh['ex'=8,'ctr'=16] {'ex','ctr'}, dimensions={0} | all-to-all | bytes 262144 | tf_op jit(solution)/shard_map/all_to_all | solution.py:710
  162.2 1.0 margins.1
  (35 shorter events, 1.2 us)
Async XLA Ops:
  0.0 10.3 %copy-start = (s32[2048]{0:T(1024)S(1)}, s32[2048]{0:T(1024)}, u32[]{:S(2)}) copy-start(s32[2048]{0:T(1024)} %param.9) | copy-start | bytes 24580
  0.0 9.7 %copy-start.2 = (bf16[64,2048]{1,0:T(8,128)(2,1)S(1)}, bf16[64,2048]{1,0:T(8,128)(2,1)}, u32[]{:S(2)}) copy-start(bf16[64,2048]{1,0:T(8,128)(2,1)} %centers_ref.1) | copy-start | bytes 786436
  0.0 0.8 copy-start.3
  0.8 8.9 %copy-start.4 = (s32[2048]{0:T(1024)S(1)}, s32[2048]{0:T(1024)}, u32[]{:S(2)}) copy-start(s32[2048]{0:T(1024)} %param.8) | copy-start | bytes 24580
  0.8 20.4 %copy-start.5 = (bf16[144,2048]{1,0:T(8,128)(2,1)S(1)}, bf16[144,2048]{1,0:T(8,128)(2,1)}, u32[]{:S(2)}) copy-start(bf16[144,2048]{1,0:T(8,128)(2,1)} %alpha_hbm.1) | copy-start | bytes 1769476
  1.7 19.5 %all-to-all-start = ((bf16[16,128,128]{2,1,0:T(8,128)(2,1)}), bf16[16,128,128]{2,1,0:T(8,128)(2,1)S(1)}, u32[]{:S(2)}, u32[]{:S(2)}) async-start(bf16[16,128,128]{2,1,0:T(8,128)(2,1)} %copies.1), calls=%async_computation | async-start | bytes 1048576 | tf_op jit(solution)/shard_map/all_to_all | solution.py:667
  56.0 1.7 %collective-permute-start.3 = (f32[144,512]{1,0:T(8,128)S(1)}, f32[144,512]{1,0:T(8,128)S(1)}, u32[]{:S(2)}, u32[]{:S(2)}) collective-permute-start(f32[144,512]{1,0:T(8,128)S(1)} %get-tuple-element.59), channel_id=1, source_target_pairs={{0,16},{16,0},{32,48},{48,32},{64,80},{80,64},{96,112},{112,96},{1... | collective-permute-start | bytes 884744 | tf_op jit(solution)/shard_map/ppermute | solution.py:664
  56.1 3.6 %collective-permute-start = (f32[152,512]{1,0:T(8,128)S(1)}, f32[152,512]{1,0:T(8,128)S(1)}, u32[]{:S(2)}, u32[]{:S(2)}) collective-permute-start(f32[152,512]{1,0:T(8,128)S(1)} %get-tuple-element.58), channel_id=1, source_target_pairs={{0,16},{16,0},{32,48},{48,32},{64,80},{80,64},{96,112},{112,96},{1... | collective-permute-start | bytes 933896 | tf_op jit(solution)/shard_map/ppermute | solution.py:664
  58.0 6.1 %collective-permute-start.4 = (f16[152,512]{1,0:T(8,128)(2,1)S(1)}, f16[152,512]{1,0:T(8,128)(2,1)S(1)}, u32[]{:S(2)}, u32[]{:S(2)}) collective-permute-start(f16[152,512]{1,0:T(8,128)(2,1)S(1)} %get-tuple-element.91), channel_id=1, source_target_pairs={{0,32},{16,48},{32,0},{48,16},{64,96},{80,112},{96,64},{112,80},{1... | collective-permute-start | bytes 466952 | tf_op jit(solution)/shard_map/ppermute | solution.py:661
  60.0 7.7 %collective-permute-start.1 = (f16[152,512]{1,0:T(8,128)(2,1)S(1)}, f16[152,512]{1,0:T(8,128)(2,1)S(1)}, u32[]{:S(2)}, u32[]{:S(2)}) collective-permute-start(f16[152,512]{1,0:T(8,128)(2,1)S(1)} %get-tuple-element.95), channel_id=1, source_target_pairs={{0,96},{16,112},{32,64},{48,80},{64,32},{80,48},{96,0},{112,16},{1... | collective-permute-start | bytes 466952 | tf_op jit(solution)/shard_map/ppermute | solution.py:661
  64.6 4.0 %copy-start.1 = (f32[2048,256]{1,0:T(8,128)S(1)}, f32[2048,256]{1,0:T(8,128)}, u32[]{:S(2)}) copy-start(f32[2048,256]{1,0:T(8,128)} %precond_ref.1) | copy-start | bytes 6291460
  64.6 6.6 %collective-permute-start.5 = (f16[152,512]{1,0:T(8,128)(2,1)S(1)}, f16[152,512]{1,0:T(8,128)(2,1)S(1)}, u32[]{:S(2)}, u32[]{:S(2)}) collective-permute-start(f16[152,512]{1,0:T(8,128)(2,1)S(1)} %get-tuple-element.89), channel_id=1, source_target_pairs={{0,96},{16,112},{32,64},{48,80},{64,32},{80,48},{96,0},{112,16},{1... | collective-permute-start | bytes 466952 | tf_op jit(solution)/shard_map/ppermute | solution.py:661
  68.2 5.5 %collective-permute-start.2 = (f16[152,512]{1,0:T(8,128)(2,1)S(1)}, f16[152,512]{1,0:T(8,128)(2,1)S(1)}, u32[]{:S(2)}, u32[]{:S(2)}) collective-permute-start(f16[152,512]{1,0:T(8,128)(2,1)S(1)} %get-tuple-element.93), channel_id=1, source_target_pairs={{0,32},{16,48},{32,0},{48,16},{64,96},{80,112},{96,64},{112,80},{1... | collective-permute-start | bytes 466952 | tf_op jit(solution)/shard_map/ppermute | solution.py:661
  74.7 1.7 %collective-permute-start.6 = (bf16[160,1024]{1,0:T(8,128)(2,1)S(1)}, bf16[160,1024]{1,0:T(8,128)(2,1)S(1)}, u32[]{:S(2)}, u32[]{:S(2)}) collective-permute-start(bf16[160,1024]{1,0:T(8,128)(2,1)S(1)} %get-tuple-element.65.own_ref), channel_id=1, source_target_pairs={{0,16},{16,0},{32,48},{48,32},{64,80},{80,64},{96,112},{112,96},{1... | collective-permute-start | bytes 983048 | tf_op jit(solution)/shard_map/ppermute | solution.py:664
  110.7 1.7 %collective-permute-start.10 = (f32[144,512]{1,0:T(8,128)S(1)}, f32[144,512]{1,0:T(8,128)S(1)}, u32[]{:S(2)}, u32[]{:S(2)}) collective-permute-start(f32[144,512]{1,0:T(8,128)S(1)} %get-tuple-element.72), channel_id=1, source_target_pairs={{0,16},{16,0},{32,48},{48,32},{64,80},{80,64},{96,112},{112,96},{1... | collective-permute-start | bytes 884744 | tf_op jit(solution)/shard_map/ppermute | solution.py:664
  110.8 2.1 %collective-permute-start.7 = (f32[152,512]{1,0:T(8,128)S(1)}, f32[152,512]{1,0:T(8,128)S(1)}, u32[]{:S(2)}, u32[]{:S(2)}) collective-permute-start(f32[152,512]{1,0:T(8,128)S(1)} %get-tuple-element.71), channel_id=1, source_target_pairs={{0,16},{16,0},{32,48},{48,32},{64,80},{80,64},{96,112},{112,96},{1... | collective-permute-start | bytes 933896 | tf_op jit(solution)/shard_map/ppermute | solution.py:664
  112.7 6.1 %collective-permute-start.11 = (f16[152,512]{1,0:T(8,128)(2,1)S(1)}, f16[152,512]{1,0:T(8,128)(2,1)S(1)}, u32[]{:S(2)}, u32[]{:S(2)}) collective-permute-start(f16[152,512]{1,0:T(8,128)(2,1)S(1)} %get-tuple-element.83), channel_id=1, source_target_pairs={{0,32},{16,48},{32,0},{48,16},{64,96},{80,112},{96,64},{112,80},{1... | collective-permute-start | bytes 466952 | tf_op jit(solution)/shard_map/ppermute | solution.py:661
  113.3 7.7 %collective-permute-start.8 = (f16[152,512]{1,0:T(8,128)(2,1)S(1)}, f16[152,512]{1,0:T(8,128)(2,1)S(1)}, u32[]{:S(2)}, u32[]{:S(2)}) collective-permute-start(f16[152,512]{1,0:T(8,128)(2,1)S(1)} %get-tuple-element.87), channel_id=1, source_target_pairs={{0,96},{16,112},{32,64},{48,80},{64,32},{80,48},{96,0},{112,16},{1... | collective-permute-start | bytes 466952 | tf_op jit(solution)/shard_map/ppermute | solution.py:661
  119.3 6.5 %collective-permute-start.12 = (f16[152,512]{1,0:T(8,128)(2,1)S(1)}, f16[152,512]{1,0:T(8,128)(2,1)S(1)}, u32[]{:S(2)}, u32[]{:S(2)}) collective-permute-start(f16[152,512]{1,0:T(8,128)(2,1)S(1)} %get-tuple-element.81), channel_id=1, source_target_pairs={{0,96},{16,112},{32,64},{48,80},{64,32},{80,48},{96,0},{112,16},{1... | collective-permute-start | bytes 466952 | tf_op jit(solution)/shard_map/ppermute | solution.py:661
  121.4 5.3 %collective-permute-start.9 = (f16[152,512]{1,0:T(8,128)(2,1)S(1)}, f16[152,512]{1,0:T(8,128)(2,1)S(1)}, u32[]{:S(2)}, u32[]{:S(2)}) collective-permute-start(f16[152,512]{1,0:T(8,128)(2,1)S(1)} %get-tuple-element.85), channel_id=1, source_target_pairs={{0,32},{16,48},{32,0},{48,16},{64,96},{80,112},{96,64},{112,80},{1... | collective-permute-start | bytes 466952 | tf_op jit(solution)/shard_map/ppermute | solution.py:661
  127.8 1.7 %collective-permute-start.13 = (bf16[160,1024]{1,0:T(8,128)(2,1)S(1)}, bf16[160,1024]{1,0:T(8,128)(2,1)S(1)}, u32[]{:S(2)}, u32[]{:S(2)}) collective-permute-start(bf16[160,1024]{1,0:T(8,128)(2,1)S(1)} %get-tuple-element.75.own_ref), channel_id=1, source_target_pairs={{0,16},{16,0},{32,48},{48,32},{64,80},{80,64},{96,112},{112,96},{1... | collective-permute-start | bytes 983048 | tf_op jit(solution)/shard_map/ppermute | solution.py:664

commit v10 on v9

--- a/solution.py
+++ b/solution.py
@@ -288,9 +288,10 @@
     return jnp.concatenate(out, axis=1)
 
 
-def put_lifted(ref, lifted, vectors):
-    classes, half = lifted.shape
-    ref[:classes] = lifted
+def put_lifted(ref, second_ref, lifted, vectors):
+    classes, half = lifted.shape[0], ref.shape[1]
+    ref[:classes] = lifted[:, :half]
+    second_ref[...] = lifted[:, half:]
     row = lax.broadcasted_iota(jnp.int32, (EXTRA, 2 * LANES), 0)
     out = jnp.zeros((EXTRA, 2 * LANES), F32)
     for k, vector in enumerate(vectors):
@@ -300,21 +301,31 @@
     ref[classes:, 2 * LANES :] = jnp.zeros((EXTRA, half - 2 * LANES), BF16)
 
 
-def forward_own_kernel(core_ref, own_ref, tile_ref, first_ref):
-    classes, half = first_ref.shape[0], own_ref.shape[1]
-    mine = pl.ds(pl.multiple_of(core_ref[0] * half, half), half)
-    for b in range(first_ref.shape[1] // BAND):
+def forward_own_kernel(core_ref, own_ref, second_ref, tile_ref, sums_ref):
+    classes, wide = second_ref.shape
+    first = core_ref[0] * (2 * wide)
+    mine = [pl.ds(pl.multiple_of(first + k * wide, wide), wide) for k in range(2)]
+    for b in range(sums_ref.shape[1] // BAND):
         here = slice(b * BAND, (b + 1) * BAND)
-        first_ref[:, here] = jnp.dot(
-            own_ref[:classes], tile_ref[mine, here], preferred_element_type=F32
-        )
-
-
-def forward_kernel(core_ref, first_ref, own_ref, other_ref, tile_ref, rows_ref):
+        rows = jnp.dot(own_ref[:classes], tile_ref[mine[0], here], preferred_element_type=F32)
+        rows += jnp.dot(second_ref[...], tile_ref[mine[1], here], preferred_element_type=F32)
+        sums_ref[:, here] = rows
+
+
+def forward_more_kernel(core_ref, sums_ref, other_ref, tile_ref, more_ref):
+    classes, wide = sums_ref.shape[0], other_ref.shape[1]
+    theirs = pl.ds(pl.multiple_of((1 - core_ref[0]) * (2 * wide), wide), wide)
+    for b in range(sums_ref.shape[1] // BAND):
+        here = slice(b * BAND, (b + 1) * BAND)
+        rows = jnp.dot(other_ref[:classes], tile_ref[theirs, here], preferred_element_type=F32)
+        more_ref[:, here] = sums_ref[:, here] + rows
+
+
+def forward_kernel(core_ref, first_ref, own_ref, other_ref, second_ref, tile_ref, rows_ref):
     classes, half = first_ref.shape[0], other_ref.shape[1]
     share = rows_ref.shape[2]
     examples = tile_ref.shape[1]
-    theirs = pl.ds(pl.multiple_of((1 - core_ref[0]) * half, half), half)
+    theirs = pl.ds(pl.multiple_of((1 - core_ref[0]) * (2 * half) + half, half), half)
     part = [ref[classes:, : 2 * LANES].astype(F32) for ref in (own_ref, other_ref)]
     part = part[0] + part[1]
     part = [part[3 * k : 3 * k + 1] + part[3 * k + 1 : 3 * k + 2] + part[3 * k + 2 : 3 * k + 3] for k in range(3)]
@@ -323,7 +334,7 @@
     scales = column(jnp.exp2(-powers), classes)
     for b in range(examples // BAND):
         here = slice(b * BAND, (b + 1) * BAND)
-        rows = jnp.dot(other_ref[:classes], tile_ref[theirs, here], preferred_element_type=F32)
+        rows = jnp.dot(second_ref[...], tile_ref[theirs, here], preferred_element_type=F32)
         rows = (rows + first_ref[:, here]) * scales
         for k in range(BAND // share):
             at = b * (BAND // share) + k
@@ -331,25 +342,24 @@
             rows_ref[at, classes:] = extra
 
 
-def forward(core, lifted, other, tile, share):
-    classes = lifted.shape[0] - EXTRA
+def forward(core, own, other, tile, share):
+    classes = own[1].shape[0]
     examples = tile.shape[1]
+    sums = shape((classes, examples), F32)
     first = call(
-        forward_own_kernel,
-        "forward_own",
-        shape((classes, examples), F32),
-        604 << 20,
-        scalars=1,
-        arrays=2,
-    )(core, lifted, tile)
+        forward_own_kernel, "forward_own", sums, 604 << 20, scalars=1, arrays=3
+    )(core, *own, tile)
+    first = call(
+        forward_more_kernel, "forward_more", sums, 302 << 20, scalars=1, arrays=3
+    )(core, first, other[0], tile)
     return call(
         forward_kernel,
         "forward",
         shape((examples // share, classes + SCALARS, share), F32),
-        604 << 20,
+        302 << 20,
         scalars=1,
-        arrays=4,
-    )(core, first, lifted, other, tile)
+        arrays=5,
+    )(core, first, own[0], *other, tile)
 
 
 def backward_other_kernel(
@@ -511,7 +521,7 @@
 
 def residual_kernel(
     total, one_ref, one_in_ref, two_ref, two_in_ref, high_ref, low_ref, high_turned_ref,
-    low_turned_ref, residual_ref, lifted_ref,
+    low_turned_ref, residual_ref, lifted_ref, second_ref,
 ):
     one, two = unpack_pairs(((one_ref, one_in_ref), (two_ref, two_in_ref)))
     sums = jnp.concatenate([one, two], axis=1)
@@ -520,7 +530,7 @@
     lifted = block_products(residual, high_turned_ref, low_turned_ref).astype(BF16)
     zero = jnp.zeros((1, 2 * LANES), F32)
     sizes = lane_sums(jnp.abs(lifted.astype(F32)))
-    put_lifted(lifted_ref, lifted, [lane_sums(residual * residual), zero, sizes])
+    put_lifted(lifted_ref, second_ref, lifted, [lane_sums(residual * residual), zero, sizes])
 
 
 def first_residual(total, sums, blocks):
@@ -530,7 +540,8 @@
         "residual",
         [
             shape((classes, 2 * wide), F32),
-            shape((classes + EXTRA, 2 * wide), BF16),
+            shape((classes + EXTRA, wide), BF16),
+            shape((classes, wide), BF16),
         ],
         450 << 20,
         arrays=8,
@@ -565,7 +576,7 @@
 
 def step_kernel(
     total, one_ref, one_in_ref, two_ref, two_in_ref, high_ref, low_ref, high_turned_ref,
-    low_turned_ref, residual_ref, norm_ref, lifted_ref, rough_ref,
+    low_turned_ref, residual_ref, norm_ref, lifted_ref, second_ref, rough_ref,
 ):
     classes = residual_ref.shape[0]
     one, two = unpack_pairs(((one_ref, one_in_ref), (two_ref, two_in_ref)))
@@ -580,7 +591,7 @@
     new = old - column(rough, classes) * image
     lifted = block_products(new, high_turned_ref, low_turned_ref).astype(BF16)
     sizes = lane_sums(jnp.abs(lifted.astype(F32)))
-    put_lifted(lifted_ref, lifted, [lane_sums(old * new), lane_sums(new * new), sizes])
+    put_lifted(lifted_ref, second_ref, lifted, [lane_sums(old * new), lane_sums(new * new), sizes])
 
 
 def step(total, sums, blocks, residual, norm):
@@ -588,7 +599,11 @@
     return call(
         functools.partial(step_kernel, total),
         "step",
-        [shape((classes + EXTRA, half), BF16), shape((8, 2 * LANES), F32)],
+        [
+            shape((classes + EXTRA, half // 2), BF16),
+            shape((classes, half // 2), BF16),
+            shape((8, 2 * LANES), F32),
+        ],
         450 << 20,
         arrays=10,
     )(*sums, *blocks, residual, norm)
@@ -697,13 +712,13 @@
     sums, got = sum_examples(send)
     got, late_core = lax.optimization_barrier((got, core))
     blocks = factors(late_core, precond)
-    residual, lifted = first_residual(total, sums, blocks)
-    rows = forward(core, lifted, over_cores(lifted), tile, share)
+    residual, *lifted = first_residual(total, sums, blocks)
+    rows = forward(core, lifted, [over_cores(part) for part in lifted], tile, share)
     image, norm, send = weigh(trade_halves(rows), hessian)
 
     sums, _ = sum_examples(send)
-    lifted, rough = step(total, sums, blocks, residual, norm)
-    rows = forward(core, lifted, over_cores(lifted), tile, share)
+    *lifted, rough = step(total, sums, blocks, residual, norm)
+    rows = forward(core, lifted, [over_cores(part) for part in lifted], tile, share)
     last, scales, curve = last_curve(trade_halves(rows), hessian, image, norm, rough)
 
     curve = jnp.broadcast_to(curve, (n_ex * n_ctr,) + curve.shape)

time: 165 us -> 164 us (level)
  transfers between devices with their start and end apart: 15 -> 17, of which waited for: 11 -> 11; matrix products, arithmetic and copies ran while one was open for 1% -> 1% of each run, Pallas kernels for 4% -> 4%
where the time goes in v10:
time: 164 us; the launch traced here: 163 us
  blocking collectives  90.3 us (55%)
  waiting for transfers between devices  26.4 us (16%)
  starting transfers between devices  21.3 us (13%)
  Pallas kernels  21 us (13%)
  other arithmetic  2.02 us (1%)
  local copies, waits for them, and re-layouts  1.74 us (1%)
    all_to_all x5, blocking collectives, trade(): return lax.all_to_all(parts, 'ctr', 0, 0)  75.7 us
    ppermute x8, waiting for transfers between devices, over_y(): return lax.ppermute(array, 'ex', pairs)  15.7 us
    all_to_all x1, blocking collectives, shards(): curve = lax.all_to_all(curve, ('ex', 'ctr'), 0, 0)  14.6 us
    ppermute x8, starting transfers between devices, over_y(): return lax.ppermute(array, 'ex', pairs)  11 us
    all_to_all x1, waiting for transfers between devices, trade(): return lax.all_to_all(parts, 'ctr', 0, 0)  9.98 us
    all_to_all x1, starting transfers between devices, trade(): return lax.all_to_all(parts, 'ctr', 0, 0)  7.96 us
    pallas_call x1, Pallas kernels, make_tile(): call(tile_kernel, 'tile', [shape((count, examples), BF16), shape((example...  5.66 us
  transfers between devices with their start and end apart: 17, of which 11 were waited for; matrix products, arithmetic and copies ran while one was open for 1% of the time, Pallas kernels for 4%

profile of v10, /device:TPU:0, one launch (start us, length us, event | category | flops | bytes accessed | tf_op | source)
XLA Modules:
  0.0 163.1 jit_solution(9560773525975992685)
XLA Ops:
  0.0 0.8 copy-done.3
  0.8 0.9 copies.1
  1.7 8.0 %all-to-all-start = ((bf16[16,128,128]{2,1,0:T(8,128)(2,1)}), bf16[16,128,128]{2,1,0:T(8,128)(2,1)S(1)}, u32[]{:S(2)}, u32[]{:S(2)}) async-start(bf16[16,128,128]{2,1,0:T(8,128)(2,1)} %copies.1), calls=%async_computation | async-start | bytes 1048576 | tf_op jit(solution)/shard_map/all_to_all | solution.py:682
  9.7 0.7 prepare.1
  10.4 0.8 dynamic-slice_bitcast_fusion.weight_ref
  11.2 10.0 %all-to-all-done.pool_ref = bf16[16,128,128]{2,1,0:T(8,128)(2,1)S(1)} async-done(((bf16[16,128,128]{2,1,0:T(8,128)(2,1)}), bf16[16,128,128]{2,1,0:T(8,128)(2,1)S(1)}, u32[]{:S(2)}, u32[]{:S(2)}) %all-to-all-start) | async-done | bytes 524320 | tf_op jit(solution)/shard_map/all_to_all | solution.py:682
  21.2 5.7 %tile.1 = (bf16[2048,2048]{1,0:T(8,128)(2,1)S(1)}, bf16[2048,2048]{1,0:T(8,128)(2,1)S(1)}, f32[16,144,128]{2,1,0:T(8,128)S(1)}) custom-call(bf16[144,2048]{1,0:T(8,128)(2,1)S(1)} %copy-done.5, s32[1,2048]{1,0:T(1,128)S(1)} %get-tuple-element.49.chunk_ref, bf16[16,128,128]{2,1,0:T(8,128)(2,1)S(1)} %all-to-all-done.pool_ref, ...), custom_call_target="tpu_custom_call" | custom-call | flops 4294967296 | bytes 17956864 | tf_op jit(solution)/shard_map/tile/pallas_call | solution.py:235
  26.9 14.4 %all_to_all.35 = f16[16,144,128]{2,1,0:T(8,128)(2,1)S(1)} all-to-all(f16[16,144,128]{2,1,0:T(8,128)(2,1)S(1)} %convert_element_type.66), channel_id=1, replica_groups=mesh['ex'=8,'ctr'=16] {'ctr'}, dimensions={0} | all-to-all | bytes 1179648 | tf_op jit(solution)/shard_map/all_to_all | solution.py:682
  41.5 13.7 %all_to_all.36.values_ref = bf16[16,144,128]{2,1,0:T(8,128)(2,1)S(1)} all-to-all(bf16[16,144,128]{2,1,0:T(8,128)(2,1)S(1)} %get-tuple-element.56), channel_id=1, replica_groups=mesh['ex'=8,'ctr'=16] {'ctr'}, dimensions={0} | all-to-all | bytes 1179648 | tf_op jit(solution)/shard_map/all_to_all | solution.py:682
  55.1 0.8 backward_other.2
  56.1 0.5 collective-permute-start
  56.6 0.8 backward_own.2.own_ref
  57.4 0.2 collective-permute-done.3.got_ref
  57.7 0.2 join_second.2
  57.8 0.2 reduce-precision_convert_fusion.5
  58.0 1.7 %collective-permute-start.4 = (f16[152,512]{1,0:T(8,128)(2,1)S(1)}, f16[152,512]{1,0:T(8,128)(2,1)S(1)}, u32[]{:S(2)}, u32[]{:S(2)}) collective-permute-start(f16[152,512]{1,0:T(8,128)(2,1)S(1)} %get-tuple-element.95), channel_id=1, source_target_pairs={{0,32},{16,48},{32,0},{48,16},{64,96},{80,112},{96,64},{112,80},{1... | collective-permute-start | bytes 466952 | tf_op jit(solution)/shard_map/ppermute | solution.py:676
  59.7 0.2 join_first.2
  59.8 0.2 reduce-precision_convert_fusion.7
  60.0 2.3 %collective-permute-start.1 = (f16[152,512]{1,0:T(8,128)(2,1)S(1)}, f16[152,512]{1,0:T(8,128)(2,1)S(1)}, u32[]{:S(2)}, u32[]{:S(2)}) collective-permute-start(f16[152,512]{1,0:T(8,128)(2,1)S(1)} %get-tuple-element.99), channel_id=1, source_target_pairs={{0,96},{16,112},{32,64},{48,80},{64,32},{80,48},{96,0},{112,16},{1... | collective-permute-start | bytes 466952 | tf_op jit(solution)/shard_map/ppermute | solution.py:676
  62.3 1.9 %collective-permute-done.4 = f16[152,512]{1,0:T(8,128)(2,1)S(1)} collective-permute-done((f16[152,512]{1,0:T(8,128)(2,1)S(1)}, f16[152,512]{1,0:T(8,128)(2,1)S(1)}, u32[]{:S(2)}, u32[]{:S(2)}) %collective-permute-start.4) | collective-permute-done | bytes 155680 | tf_op jit(solution)/shard_map/ppermute | solution.py:676
  64.2 0.3 add.15
  64.5 0.2 reduce-precision_convert_fusion.4
  64.6 3.1 %collective-permute-start.5 = (f16[152,512]{1,0:T(8,128)(2,1)S(1)}, f16[152,512]{1,0:T(8,128)(2,1)S(1)}, u32[]{:S(2)}, u32[]{:S(2)}) collective-permute-start(f16[152,512]{1,0:T(8,128)(2,1)S(1)} %get-tuple-element.93), channel_id=1, source_target_pairs={{0,96},{16,112},{32,64},{48,80},{64,32},{80,48},{96,0},{112,16},{1... | collective-permute-start | bytes 466952 | tf_op jit(solution)/shard_map/ppermute | solution.py:676
  67.8 0.3 add.14
  68.0 0.2 reduce-precision_convert_fusion.6
  68.2 0.4 collective-permute-start.2
  68.6 0.3 factors.1
  69.0 2.3 %collective-permute-done.5 = f16[152,512]{1,0:T(8,128)(2,1)S(1)} collective-permute-done((f16[152,512]{1,0:T(8,128)(2,1)S(1)}, f16[152,512]{1,0:T(8,128)(2,1)S(1)}, u32[]{:S(2)}, u32[]{:S(2)}) %collective-permute-start.5) | collective-permute-done | bytes 155680 | tf_op jit(solution)/shard_map/ppermute | solution.py:676
  71.3 2.4 %collective-permute-done.2 = f16[152,512]{1,0:T(8,128)(2,1)S(1)} collective-permute-done((f16[152,512]{1,0:T(8,128)(2,1)S(1)}, f16[152,512]{1,0:T(8,128)(2,1)S(1)}, u32[]{:S(2)}, u32[]{:S(2)}) %collective-permute-start.2) | collective-permute-done | bytes 155680 | tf_op jit(solution)/shard_map/ppermute | solution.py:676
  73.7 1.0 residual.1
  74.8 0.5 collective-permute-start.7
  75.3 0.8 forward_own.2.sums_ref
  76.2 0.5 forward_more.2.first_ref
  76.7 0.6 forward.2
  77.4 16.0 %all_to_all.37 = f16[16,152,128]{2,1,0:T(8,128)(2,1)S(1)} all-to-all(f16[16,152,128]{2,1,0:T(8,128)(2,1)S(1)} %convert_element_type.76), channel_id=1, replica_groups=mesh['ex'=8,'ctr'=16] {'ctr'}, dimensions={0} | all-to-all | bytes 1245184 | tf_op jit(solution)/shard_map/all_to_all | solution.py:682
  93.4 0.7 weigh.1
  94.1 15.7 %all_to_all.38.values_ref = bf16[16,160,128]{2,1,0:T(8,128)(2,1)S(1)} all-to-all(bf16[16,160,128]{2,1,0:T(8,128)(2,1)S(1)} %get-tuple-element.71), channel_id=1, replica_groups=mesh['ex'=8,'ctr'=16] {'ctr'}, dimensions={0} | all-to-all | bytes 1310720 | tf_op jit(solution)/shard_map/all_to_all | solution.py:682
  109.8 0.8 backward_other.3
  110.7 0.5 collective-permute-start.8
  111.2 0.8 backward_own.3.own_ref
  112.0 0.3 collective-permute-done.11.got_ref
  112.3 0.2 join_second.3
  112.7 0.2 collective-permute-start.12
  112.9 0.2 join_first.3
  113.1 0.2 reduce-precision_convert_fusion.3
  113.2 1.5 collective-permute-start.9
  114.8 4.0 %collective-permute-done.12 = f16[152,512]{1,0:T(8,128)(2,1)S(1)} collective-permute-done((f16[152,512]{1,0:T(8,128)(2,1)S(1)}, f16[152,512]{1,0:T(8,128)(2,1)S(1)}, u32[]{:S(2)}, u32[]{:S(2)}) %collective-permute-start.12) | collective-permute-done | bytes 155680 | tf_op jit(solution)/shard_map/ppermute | solution.py:676
  118.8 0.3 add.17
  119.1 0.2 reduce-precision_convert_fusion
  119.3 1.6 collective-permute-start.13
  120.9 0.3 add.16
  121.2 0.2 reduce-precision_convert_fusion.2
  121.4 0.2 collective-permute-start.10
  121.5 4.3 %collective-permute-done.13 = f16[152,512]{1,0:T(8,128)(2,1)S(1)} collective-permute-done((f16[152,512]{1,0:T(8,128)(2,1)S(1)}, f16[152,512]{1,0:T(8,128)(2,1)S(1)}, u32[]{:S(2)}, u32[]{:S(2)}) %collective-permute-start.13) | collective-permute-done | bytes 155680 | tf_op jit(solution)/shard_map/ppermute | solution.py:676
  125.8 0.8 collective-permute-done.10
  126.7 1.0 step.1
  127.8 0.5 collective-permute-start.15
  128.3 0.8 forward_own.3.sums_ref
  129.2 0.5 forward_more.3.first_ref
  129.8 0.6 forward.3
  130.4 16.0 %all_to_all.39 = f16[16,152,128]{2,1,0:T(8,128)(2,1)S(1)} all-to-all(f16[16,152,128]{2,1,0:T(8,128)(2,1)S(1)} %convert_element_type.86), channel_id=1, replica_groups=mesh['ex'=8,'ctr'=16] {'ctr'}, dimensions={0} | all-to-all | bytes 1245184 | tf_op jit(solution)/shard_map/all_to_all | solution.py:682
  146.5 0.9 curve.1
  147.4 14.6 %all_to_all.40.curve_ref = f32[128,1,256]{2,1,0:T(1,128)S(1)} all-to-all(f32[128,1,256]{2,1,0:T(1,128)S(1)} %broadcast_in_dim.3), channel_id=1, replica_groups=mesh['ex'=8,'ctr'=16] {'ex','ctr'}, dimensions={0} | all-to-all | bytes 262144 | tf_op jit(solution)/shard_map/all_to_all | solution.py:725
  162.1 1.0 margins.1
  (41 shorter events, 1.6 us)
Async XLA Ops:
  0.0 10.3 %copy-start = (s32[2048]{0:T(1024)S(1)}, s32[2048]{0:T(1024)}, u32[]{:S(2)}) copy-start(s32[2048]{0:T(1024)} %param.9) | copy-start | bytes 24580
  0.0 9.7 %copy-start.2 = (bf16[64,2048]{1,0:T(8,128)(2,1)S(1)}, bf16[64,2048]{1,0:T(8,128)(2,1)}, u32[]{:S(2)}) copy-start(bf16[64,2048]{1,0:T(8,128)(2,1)} %centers_ref.1) | copy-start | bytes 786436
  0.0 0.8 copy-start.3
  0.8 8.9 %copy-start.4 = (s32[2048]{0:T(1024)S(1)}, s32[2048]{0:T(1024)}, u32[]{:S(2)}) copy-start(s32[2048]{0:T(1024)} %param.8) | copy-start | bytes 24580
  0.8 20.4 %copy-start.5 = (bf16[144,2048]{1,0:T(8,128)(2,1)S(1)}, bf16[144,2048]{1,0:T(8,128)(2,1)}, u32[]{:S(2)}) copy-start(bf16[144,2048]{1,0:T(8,128)(2,1)} %alpha_hbm.1) | copy-start | bytes 1769476
  1.7 19.5 %all-to-all-start = ((bf16[16,128,128]{2,1,0:T(8,128)(2,1)}), bf16[16,128,128]{2,1,0:T(8,128)(2,1)S(1)}, u32[]{:S(2)}, u32[]{:S(2)}) async-start(bf16[16,128,128]{2,1,0:T(8,128)(2,1)} %copies.1), calls=%async_computation | async-start | bytes 1048576 | tf_op jit(solution)/shard_map/all_to_all | solution.py:682
  56.0 1.7 %collective-permute-start.3 = (f32[144,512]{1,0:T(8,128)S(1)}, f32[144,512]{1,0:T(8,128)S(1)}, u32[]{:S(2)}, u32[]{:S(2)}) collective-permute-start(f32[144,512]{1,0:T(8,128)S(1)} %get-tuple-element.61), channel_id=1, source_target_pairs={{0,16},{16,0},{32,48},{48,32},{64,80},{80,64},{96,112},{112,96},{1... | collective-permute-start | bytes 884744 | tf_op jit(solution)/shard_map/ppermute | solution.py:679
  56.1 3.6 %collective-permute-start = (f32[152,512]{1,0:T(8,128)S(1)}, f32[152,512]{1,0:T(8,128)S(1)}, u32[]{:S(2)}, u32[]{:S(2)}) collective-permute-start(f32[152,512]{1,0:T(8,128)S(1)} %get-tuple-element.60), channel_id=1, source_target_pairs={{0,16},{16,0},{32,48},{48,32},{64,80},{80,64},{96,112},{112,96},{1... | collective-permute-start | bytes 933896 | tf_op jit(solution)/shard_map/ppermute | solution.py:679
  58.0 6.1 %collective-permute-start.4 = (f16[152,512]{1,0:T(8,128)(2,1)S(1)}, f16[152,512]{1,0:T(8,128)(2,1)S(1)}, u32[]{:S(2)}, u32[]{:S(2)}) collective-permute-start(f16[152,512]{1,0:T(8,128)(2,1)S(1)} %get-tuple-element.95), channel_id=1, source_target_pairs={{0,32},{16,48},{32,0},{48,16},{64,96},{80,112},{96,64},{112,80},{1... | collective-permute-start | bytes 466952 | tf_op jit(solution)/shard_map/ppermute | solution.py:676
  60.0 7.7 %collective-permute-start.1 = (f16[152,512]{1,0:T(8,128)(2,1)S(1)}, f16[152,512]{1,0:T(8,128)(2,1)S(1)}, u32[]{:S(2)}, u32[]{:S(2)}) collective-permute-start(f16[152,512]{1,0:T(8,128)(2,1)S(1)} %get-tuple-element.99), channel_id=1, source_target_pairs={{0,96},{16,112},{32,64},{48,80},{64,32},{80,48},{96,0},{112,16},{1... | collective-permute-start | bytes 466952 | tf_op jit(solution)/shard_map/ppermute | solution.py:676
  64.6 4.0 %copy-start.1 = (f32[2048,256]{1,0:T(8,128)S(1)}, f32[2048,256]{1,0:T(8,128)}, u32[]{:S(2)}) copy-start(f32[2048,256]{1,0:T(8,128)} %precond_ref.1) | copy-start | bytes 6291460
  64.6 6.6 %collective-permute-start.5 = (f16[152,512]{1,0:T(8,128)(2,1)S(1)}, f16[152,512]{1,0:T(8,128)(2,1)S(1)}, u32[]{:S(2)}, u32[]{:S(2)}) collective-permute-start(f16[152,512]{1,0:T(8,128)(2,1)S(1)} %get-tuple-element.93), channel_id=1, source_target_pairs={{0,96},{16,112},{32,64},{48,80},{64,32},{80,48},{96,0},{112,16},{1... | collective-permute-start | bytes 466952 | tf_op jit(solution)/shard_map/ppermute | solution.py:676
  68.2 5.5 %collective-permute-start.2 = (f16[152,512]{1,0:T(8,128)(2,1)S(1)}, f16[152,512]{1,0:T(8,128)(2,1)S(1)}, u32[]{:S(2)}, u32[]{:S(2)}) collective-permute-start(f16[152,512]{1,0:T(8,128)(2,1)S(1)} %get-tuple-element.97), channel_id=1, source_target_pairs={{0,32},{16,48},{32,0},{48,16},{64,96},{80,112},{96,64},{112,80},{1... | collective-permute-start | bytes 466952 | tf_op jit(solution)/shard_map/ppermute | solution.py:676
  74.7 1.5 collective-permute-start.6
  74.8 1.9 %collective-permute-start.7 = (bf16[144,512]{1,0:T(8,128)(2,1)S(1)}, bf16[144,512]{1,0:T(8,128)(2,1)S(1)}, u32[]{:S(2)}, u32[]{:S(2)}) collective-permute-start(bf16[144,512]{1,0:T(8,128)(2,1)S(1)} %get-tuple-element.68.second_ref), channel_id=1, source_target_pairs={{0,16},{16,0},{32,48},{48,32},{64,80},{80,64},{96,112},{112,96},{1... | collective-permute-start | bytes 442376 | tf_op jit(solution)/shard_map/ppermute | solution.py:679
  110.6 1.7 %collective-permute-start.11 = (f32[144,512]{1,0:T(8,128)S(1)}, f32[144,512]{1,0:T(8,128)S(1)}, u32[]{:S(2)}, u32[]{:S(2)}) collective-permute-start(f32[144,512]{1,0:T(8,128)S(1)} %get-tuple-element.75), channel_id=1, source_target_pairs={{0,16},{16,0},{32,48},{48,32},{64,80},{80,64},{96,112},{112,96},{1... | collective-permute-start | bytes 884744 | tf_op jit(solution)/shard_map/ppermute | solution.py:679
  110.7 2.1 %collective-permute-start.8 = (f32[152,512]{1,0:T(8,128)S(1)}, f32[152,512]{1,0:T(8,128)S(1)}, u32[]{:S(2)}, u32[]{:S(2)}) collective-permute-start(f32[152,512]{1,0:T(8,128)S(1)} %get-tuple-element.74), channel_id=1, source_target_pairs={{0,16},{16,0},{32,48},{48,32},{64,80},{80,64},{96,112},{112,96},{1... | collective-permute-start | bytes 933896 | tf_op jit(solution)/shard_map/ppermute | solution.py:679
  112.7 6.1 %collective-permute-start.12 = (f16[152,512]{1,0:T(8,128)(2,1)S(1)}, f16[152,512]{1,0:T(8,128)(2,1)S(1)}, u32[]{:S(2)}, u32[]{:S(2)}) collective-permute-start(f16[152,512]{1,0:T(8,128)(2,1)S(1)} %get-tuple-element.87), channel_id=1, source_target_pairs={{0,32},{16,48},{32,0},{48,16},{64,96},{80,112},{96,64},{112,80},{1... | collective-permute-start | bytes 466952 | tf_op jit(solution)/shard_map/ppermute | solution.py:676
  113.2 7.7 %collective-permute-start.9 = (f16[152,512]{1,0:T(8,128)(2,1)S(1)}, f16[152,512]{1,0:T(8,128)(2,1)S(1)}, u32[]{:S(2)}, u32[]{:S(2)}) collective-permute-start(f16[152,512]{1,0:T(8,128)(2,1)S(1)} %get-tuple-element.91), channel_id=1, source_target_pairs={{0,96},{16,112},{32,64},{48,80},{64,32},{80,48},{96,0},{112,16},{1... | collective-permute-start | bytes 466952 | tf_op jit(solution)/shard_map/ppermute | solution.py:676
  119.3 6.5 %collective-permute-start.13 = (f16[152,512]{1,0:T(8,128)(2,1)S(1)}, f16[152,512]{1,0:T(8,128)(2,1)S(1)}, u32[]{:S(2)}, u32[]{:S(2)}) collective-permute-start(f16[152,512]{1,0:T(8,128)(2,1)S(1)} %get-tuple-element.85), channel_id=1, source_target_pairs={{0,96},{16,112},{32,64},{48,80},{64,32},{80,48},{96,0},{112,16},{1... | collective-permute-start | bytes 466952 | tf_op jit(solution)/shard_map/ppermute | solution.py:676
  121.4 5.3 %collective-permute-start.10 = (f16[152,512]{1,0:T(8,128)(2,1)S(1)}, f16[152,512]{1,0:T(8,128)(2,1)S(1)}, u32[]{:S(2)}, u32[]{:S(2)}) collective-permute-start(f16[152,512]{1,0:T(8,128)(2,1)S(1)} %get-tuple-element.89), channel_id=1, source_target_pairs={{0,32},{16,48},{32,0},{48,16},{64,96},{80,112},{96,64},{112,80},{1... | collective-permute-start | bytes 466952 | tf_op jit(solution)/shard_map/ppermute | solution.py:676
  127.7 1.5 collective-permute-start.14
  127.8 1.9 %collective-permute-start.15 = (bf16[144,512]{1,0:T(8,128)(2,1)S(1)}, bf16[144,512]{1,0:T(8,128)(2,1)S(1)}, u32[]{:S(2)}, u32[]{:S(2)}) collective-permute-start(bf16[144,512]{1,0:T(8,128)(2,1)S(1)} %get-tuple-element.79.second_ref), channel_id=1, source_target_pairs={{0,16},{16,0},{32,48},{48,32},{64,80},{80,64},{96,112},{112,96},{1... | collective-permute-start | bytes 442376 | tf_op jit(solution)/shard_map/ppermute | solution.py:679

commit v11 on v10

--- a/solution.py
+++ b/solution.py
@@ -121,10 +121,16 @@
     return jnp.broadcast_to(vector, (8, vector.shape[1])).T[:classes, :1]
 
 
-def lane_sums(values):
-    folded = sum(values[:, k : k + LANES] for k in range(0, values.shape[1], LANES))
-    empty = jnp.zeros((2 * LANES - values.shape[0], LANES), F32)
-    return jnp.sum(jnp.concatenate([folded, empty], axis=0).T, axis=0, keepdims=True)
+def lane_sums_of(arrays):
+    classes = arrays[0].shape[0]
+    lane = lax.broadcasted_iota(jnp.int32, (classes, LANES), 1)
+    out = jnp.zeros((classes, LANES), F32)
+    for k, values in enumerate(arrays):
+        folded = sum(values[:, j : j + LANES] for j in range(0, values.shape[1], LANES))
+        out = jnp.where(lane == k, jnp.sum(folded, axis=1, keepdims=True), out)
+    empty = jnp.zeros((2 * LANES - classes, LANES), F32)
+    turned = jnp.concatenate([out, empty], axis=0).T
+    return [turned[k : k + 1] for k in range(len(arrays))]
 
 
 def stack_rows(vectors):
@@ -529,8 +535,8 @@
     residual_ref[...] = residual
     lifted = block_products(residual, high_turned_ref, low_turned_ref).astype(BF16)
     zero = jnp.zeros((1, 2 * LANES), F32)
-    sizes = lane_sums(jnp.abs(lifted.astype(F32)))
-    put_lifted(lifted_ref, second_ref, lifted, [lane_sums(residual * residual), zero, sizes])
+    norm, sizes = lane_sums_of([residual * residual, jnp.abs(lifted.astype(F32))])
+    put_lifted(lifted_ref, second_ref, lifted, [norm, zero, sizes])
 
 
 def first_residual(total, sums, blocks):
@@ -554,7 +560,7 @@
     image_ref[...] = image
     norm_ref[...] = stack_rows([half_vector(parts_ref, classes, 0)])
     weighted = (hessian_ref[...] * image).astype(BF16)
-    extra = rows_of([lane_sums(weighted.astype(F32) * image)])
+    extra = rows_of([lane_sums_of([weighted.astype(F32) * image])[0]])
     for k in range(send_ref.shape[0]):
         send_ref[k, :classes] = weighted
         send_ref[k, classes:] = extra
@@ -590,8 +596,8 @@
     image = block_products(sums, high_ref, low_ref) / total + RIDGE * old
     new = old - column(rough, classes) * image
     lifted = block_products(new, high_turned_ref, low_turned_ref).astype(BF16)
-    sizes = lane_sums(jnp.abs(lifted.astype(F32)))
-    put_lifted(lifted_ref, second_ref, lifted, [lane_sums(old * new), lane_sums(new * new), sizes])
+    sums = lane_sums_of([old * new, new * new, jnp.abs(lifted.astype(F32))])
+    put_lifted(lifted_ref, second_ref, lifted, sums)
 
 
 def step(total, sums, blocks, residual, norm):
@@ -630,7 +636,7 @@
     scale, other = columns([grown, ratio - excess], classes)
     rows = scale * last + other * image_ref[...]
     weighted = (hessian_ref[...] * rows).astype(BF16).astype(F32)
-    curve_ref[...] = lane_sums(weighted * rows)
+    curve_ref[...] = lane_sums_of([weighted * rows])[0]
 
 
 def last_curve(parts, hessian, image, norm, rough):

time: 164 us -> 165 us (level)
  no operation moved by 1% of the time
where the time goes in v11:
time: 165 us; the launch traced here: 163 us
  blocking collectives  90.3 us (55%)
  waiting for transfers between devices  26.3 us (16%)
  starting transfers between devices  21.3 us (13%)
  Pallas kernels  21.1 us (13%)
  other arithmetic  2.02 us (1%)
  local copies, waits for them, and re-layouts  1.78 us (1%)
    all_to_all x5, blocking collectives, trade(): return lax.all_to_all(parts, 'ctr', 0, 0)  75.7 us
    ppermute x8, waiting for transfers between devices, over_y(): return lax.ppermute(array, 'ex', pairs)  15.7 us
    all_to_all x1, blocking collectives, shards(): curve = lax.all_to_all(curve, ('ex', 'ctr'), 0, 0)  14.6 us
    ppermute x8, starting transfers between devices, over_y(): return lax.ppermute(array, 'ex', pairs)  11 us
    all_to_all x1, waiting for transfers between devices, trade(): return lax.all_to_all(parts, 'ctr', 0, 0)  9.98 us
    all_to_all x1, starting transfers between devices, trade(): return lax.all_to_all(parts, 'ctr', 0, 0)  7.96 us
    pallas_call x1, Pallas kernels, make_tile(): call(tile_kernel, 'tile', [shape((count, examples), BF16), shape((example...  5.66 us
  transfers between devices with their start and end apart: 17, of which 11 were waited for; matrix products, arithmetic and copies ran while one was open for 1% of the time, Pallas kernels for 4%

profile of v11, /device:TPU:0, one launch (start us, length us, event | category | flops | bytes accessed | tf_op | source)
XLA Modules:
  0.0 163.3 jit_solution(56649931169706622)
XLA Ops:
  0.0 0.8 copy-done.3
  0.8 0.9 copies.1
  1.7 8.0 %all-to-all-start = ((bf16[16,128,128]{2,1,0:T(8,128)(2,1)}), bf16[16,128,128]{2,1,0:T(8,128)(2,1)S(1)}, u32[]{:S(2)}, u32[]{:S(2)}) async-start(bf16[16,128,128]{2,1,0:T(8,128)(2,1)} %copies.1), calls=%async_computation | async-start | bytes 1048576 | tf_op jit(solution)/shard_map/all_to_all | solution.py:688
  9.7 0.7 prepare.1
  10.4 0.8 dynamic-slice_bitcast_fusion.weight_ref
  11.2 10.0 %all-to-all-done.pool_ref = bf16[16,128,128]{2,1,0:T(8,128)(2,1)S(1)} async-done(((bf16[16,128,128]{2,1,0:T(8,128)(2,1)}), bf16[16,128,128]{2,1,0:T(8,128)(2,1)S(1)}, u32[]{:S(2)}, u32[]{:S(2)}) %all-to-all-start) | async-done | bytes 524320 | tf_op jit(solution)/shard_map/all_to_all | solution.py:688
  21.2 5.7 %tile.1 = (bf16[2048,2048]{1,0:T(8,128)(2,1)S(1)}, bf16[2048,2048]{1,0:T(8,128)(2,1)S(1)}, f32[16,144,128]{2,1,0:T(8,128)S(1)}) custom-call(bf16[144,2048]{1,0:T(8,128)(2,1)S(1)} %copy-done.5, s32[1,2048]{1,0:T(1,128)S(1)} %get-tuple-element.49.chunk_ref, bf16[16,128,128]{2,1,0:T(8,128)(2,1)S(1)} %all-to-all-done.pool_ref, ...), custom_call_target="tpu_custom_call" | custom-call | flops 4294967296 | bytes 17956864 | tf_op jit(solution)/shard_map/tile/pallas_call | solution.py:241
  26.9 14.4 %all_to_all.35 = f16[16,144,128]{2,1,0:T(8,128)(2,1)S(1)} all-to-all(f16[16,144,128]{2,1,0:T(8,128)(2,1)S(1)} %convert_element_type.66), channel_id=1, replica_groups=mesh['ex'=8,'ctr'=16] {'ctr'}, dimensions={0} | all-to-all | bytes 1179648 | tf_op jit(solution)/shard_map/all_to_all | solution.py:688
  41.5 13.7 %all_to_all.36.values_ref = bf16[16,144,128]{2,1,0:T(8,128)(2,1)S(1)} all-to-all(bf16[16,144,128]{2,1,0:T(8,128)(2,1)S(1)} %get-tuple-element.56), channel_id=1, replica_groups=mesh['ex'=8,'ctr'=16] {'ctr'}, dimensions={0} | all-to-all | bytes 1179648 | tf_op jit(solution)/shard_map/all_to_all | solution.py:688
  55.1 0.8 backward_other.2
  56.1 0.5 collective-permute-start
  56.6 0.8 backward_own.2.own_ref
  57.4 0.2 collective-permute-done.3.got_ref
  57.7 0.2 join_second.2
  58.0 1.7 %collective-permute-start.4 = (f16[152,512]{1,0:T(8,128)(2,1)S(1)}, f16[152,512]{1,0:T(8,128)(2,1)S(1)}, u32[]{:S(2)}, u32[]{:S(2)}) collective-permute-start(f16[152,512]{1,0:T(8,128)(2,1)S(1)} %get-tuple-element.95), channel_id=1, source_target_pairs={{0,32},{16,48},{32,0},{48,16},{64,96},{80,112},{96,64},{112,80},{1... | collective-permute-start | bytes 466952 | tf_op jit(solution)/shard_map/ppermute | solution.py:682
  59.7 0.2 join_first.2
  59.8 0.2 reduce-precision_convert_fusion.7
  60.0 2.3 %collective-permute-start.1 = (f16[152,512]{1,0:T(8,128)(2,1)S(1)}, f16[152,512]{1,0:T(8,128)(2,1)S(1)}, u32[]{:S(2)}, u32[]{:S(2)}) collective-permute-start(f16[152,512]{1,0:T(8,128)(2,1)S(1)} %get-tuple-element.99), channel_id=1, source_target_pairs={{0,96},{16,112},{32,64},{48,80},{64,32},{80,48},{96,0},{112,16},{1... | collective-permute-start | bytes 466952 | tf_op jit(solution)/shard_map/ppermute | solution.py:682
  62.3 1.9 %collective-permute-done.4 = f16[152,512]{1,0:T(8,128)(2,1)S(1)} collective-permute-done((f16[152,512]{1,0:T(8,128)(2,1)S(1)}, f16[152,512]{1,0:T(8,128)(2,1)S(1)}, u32[]{:S(2)}, u32[]{:S(2)}) %collective-permute-start.4) | collective-permute-done | bytes 155680 | tf_op jit(solution)/shard_map/ppermute | solution.py:682
  64.2 0.3 add.15
  64.5 0.2 reduce-precision_convert_fusion.4
  64.6 3.1 %collective-permute-start.5 = (f16[152,512]{1,0:T(8,128)(2,1)S(1)}, f16[152,512]{1,0:T(8,128)(2,1)S(1)}, u32[]{:S(2)}, u32[]{:S(2)}) collective-permute-start(f16[152,512]{1,0:T(8,128)(2,1)S(1)} %get-tuple-element.93), channel_id=1, source_target_pairs={{0,96},{16,112},{32,64},{48,80},{64,32},{80,48},{96,0},{112,16},{1... | collective-permute-start | bytes 466952 | tf_op jit(solution)/shard_map/ppermute | solution.py:682
  67.8 0.3 add.14
  68.0 0.2 reduce-precision_convert_fusion.6
  68.2 0.4 collective-permute-start.2
  68.6 0.3 factors.1
  69.0 2.3 %collective-permute-done.5 = f16[152,512]{1,0:T(8,128)(2,1)S(1)} collective-permute-done((f16[152,512]{1,0:T(8,128)(2,1)S(1)}, f16[152,512]{1,0:T(8,128)(2,1)S(1)}, u32[]{:S(2)}, u32[]{:S(2)}) %collective-permute-start.5) | collective-permute-done | bytes 155680 | tf_op jit(solution)/shard_map/ppermute | solution.py:682
  71.3 2.4 %collective-permute-done.2 = f16[152,512]{1,0:T(8,128)(2,1)S(1)} collective-permute-done((f16[152,512]{1,0:T(8,128)(2,1)S(1)}, f16[152,512]{1,0:T(8,128)(2,1)S(1)}, u32[]{:S(2)}, u32[]{:S(2)}) %collective-permute-start.2) | collective-permute-done | bytes 155680 | tf_op jit(solution)/shard_map/ppermute | solution.py:682
  73.7 1.0 residual.1
  74.8 0.5 collective-permute-start.7
  75.3 0.8 forward_own.2.sums_ref
  76.2 0.5 forward_more.2.first_ref
  76.7 0.6 forward.2
  77.4 16.0 %all_to_all.37 = f16[16,152,128]{2,1,0:T(8,128)(2,1)S(1)} all-to-all(f16[16,152,128]{2,1,0:T(8,128)(2,1)S(1)} %convert_element_type.76), channel_id=1, replica_groups=mesh['ex'=8,'ctr'=16] {'ctr'}, dimensions={0} | all-to-all | bytes 1245184 | tf_op jit(solution)/shard_map/all_to_all | solution.py:688
  93.5 0.7 weigh.1
  94.2 15.7 %all_to_all.38.values_ref = bf16[16,160,128]{2,1,0:T(8,128)(2,1)S(1)} all-to-all(bf16[16,160,128]{2,1,0:T(8,128)(2,1)S(1)} %get-tuple-element.71), channel_id=1, replica_groups=mesh['ex'=8,'ctr'=16] {'ctr'}, dimensions={0} | all-to-all | bytes 1310720 | tf_op jit(solution)/shard_map/all_to_all | solution.py:688
  109.9 0.8 backward_other.3
  110.8 0.5 collective-permute-start.8
  111.3 0.8 backward_own.3.own_ref
  112.1 0.3 collective-permute-done.11.got_ref
  112.4 0.2 join_second.3
  112.6 0.2 reduce-precision_convert_fusion.1
  112.7 0.2 collective-permute-start.12
  112.9 0.2 join_first.3
  113.1 0.2 reduce-precision_convert_fusion.3
  113.3 1.6 collective-permute-start.9
  114.9 4.0 %collective-permute-done.12 = f16[152,512]{1,0:T(8,128)(2,1)S(1)} collective-permute-done((f16[152,512]{1,0:T(8,128)(2,1)S(1)}, f16[152,512]{1,0:T(8,128)(2,1)S(1)}, u32[]{:S(2)}, u32[]{:S(2)}) %collective-permute-start.12) | collective-permute-done | bytes 155680 | tf_op jit(solution)/shard_map/ppermute | solution.py:682
  118.9 0.3 add.17
  119.2 0.2 reduce-precision_convert_fusion
  119.3 1.6 collective-permute-start.13
  121.0 0.3 add.16
  121.3 0.2 reduce-precision_convert_fusion.2
  121.4 0.2 collective-permute-start.10
  121.6 4.3 %collective-permute-done.13 = f16[152,512]{1,0:T(8,128)(2,1)S(1)} collective-permute-done((f16[152,512]{1,0:T(8,128)(2,1)S(1)}, f16[152,512]{1,0:T(8,128)(2,1)S(1)}, u32[]{:S(2)}, u32[]{:S(2)}) %collective-permute-start.13) | collective-permute-done | bytes 155680 | tf_op jit(solution)/shard_map/ppermute | solution.py:682
  125.9 0.8 collective-permute-done.10
  126.8 1.1 step.1
  127.9 0.5 collective-permute-start.15
  128.4 0.8 forward_own.3.sums_ref
  129.3 0.5 forward_more.3.first_ref
  129.9 0.6 forward.3
  130.5 16.0 %all_to_all.39 = f16[16,152,128]{2,1,0:T(8,128)(2,1)S(1)} all-to-all(f16[16,152,128]{2,1,0:T(8,128)(2,1)S(1)} %convert_element_type.86), channel_id=1, replica_groups=mesh['ex'=8,'ctr'=16] {'ctr'}, dimensions={0} | all-to-all | bytes 1245184 | tf_op jit(solution)/shard_map/all_to_all | solution.py:688
  146.6 0.9 curve.1
  147.7 14.6 %all_to_all.40.curve_ref = f32[128,1,256]{2,1,0:T(1,128)S(1)} all-to-all(f32[128,1,256]{2,1,0:T(1,128)S(1)} %broadcast_in_dim.3), channel_id=1, replica_groups=mesh['ex'=8,'ctr'=16] {'ex','ctr'}, dimensions={0} | all-to-all | bytes 262144 | tf_op jit(solution)/shard_map/all_to_all | solution.py:731
  162.3 1.0 margins.1
  (41 shorter events, 1.6 us)
Async XLA Ops:
  0.0 10.3 %copy-start = (s32[2048]{0:T(1024)S(1)}, s32[2048]{0:T(1024)}, u32[]{:S(2)}) copy-start(s32[2048]{0:T(1024)} %param.9) | copy-start | bytes 24580
  0.0 9.7 %copy-start.2 = (bf16[64,2048]{1,0:T(8,128)(2,1)S(1)}, bf16[64,2048]{1,0:T(8,128)(2,1)}, u32[]{:S(2)}) copy-start(bf16[64,2048]{1,0:T(8,128)(2,1)} %centers_ref.1) | copy-start | bytes 786436
  0.0 0.8 copy-start.3
  0.8 8.9 %copy-start.4 = (s32[2048]{0:T(1024)S(1)}, s32[2048]{0:T(1024)}, u32[]{:S(2)}) copy-start(s32[2048]{0:T(1024)} %param.8) | copy-start | bytes 24580
  0.8 20.4 %copy-start.5 = (bf16[144,2048]{1,0:T(8,128)(2,1)S(1)}, bf16[144,2048]{1,0:T(8,128)(2,1)}, u32[]{:S(2)}) copy-start(bf16[144,2048]{1,0:T(8,128)(2,1)} %alpha_hbm.1) | copy-start | bytes 1769476
  1.7 19.5 %all-to-all-start = ((bf16[16,128,128]{2,1,0:T(8,128)(2,1)}), bf16[16,128,128]{2,1,0:T(8,128)(2,1)S(1)}, u32[]{:S(2)}, u32[]{:S(2)}) async-start(bf16[16,128,128]{2,1,0:T(8,128)(2,1)} %copies.1), calls=%async_computation | async-start | bytes 1048576 | tf_op jit(solution)/shard_map/all_to_all | solution.py:688
  56.0 1.7 %collective-permute-start.3 = (f32[144,512]{1,0:T(8,128)S(1)}, f32[144,512]{1,0:T(8,128)S(1)}, u32[]{:S(2)}, u32[]{:S(2)}) collective-permute-start(f32[144,512]{1,0:T(8,128)S(1)} %get-tuple-element.61), channel_id=1, source_target_pairs={{0,16},{16,0},{32,48},{48,32},{64,80},{80,64},{96,112},{112,96},{1... | collective-permute-start | bytes 884744 | tf_op jit(solution)/shard_map/ppermute | solution.py:685
  56.1 3.6 %collective-permute-start = (f32[152,512]{1,0:T(8,128)S(1)}, f32[152,512]{1,0:T(8,128)S(1)}, u32[]{:S(2)}, u32[]{:S(2)}) collective-permute-start(f32[152,512]{1,0:T(8,128)S(1)} %get-tuple-element.60), channel_id=1, source_target_pairs={{0,16},{16,0},{32,48},{48,32},{64,80},{80,64},{96,112},{112,96},{1... | collective-permute-start | bytes 933896 | tf_op jit(solution)/shard_map/ppermute | solution.py:685
  58.0 6.1 %collective-permute-start.4 = (f16[152,512]{1,0:T(8,128)(2,1)S(1)}, f16[152,512]{1,0:T(8,128)(2,1)S(1)}, u32[]{:S(2)}, u32[]{:S(2)}) collective-permute-start(f16[152,512]{1,0:T(8,128)(2,1)S(1)} %get-tuple-element.95), channel_id=1, source_target_pairs={{0,32},{16,48},{32,0},{48,16},{64,96},{80,112},{96,64},{112,80},{1... | collective-permute-start | bytes 466952 | tf_op jit(solution)/shard_map/ppermute | solution.py:682
  60.0 7.7 %collective-permute-start.1 = (f16[152,512]{1,0:T(8,128)(2,1)S(1)}, f16[152,512]{1,0:T(8,128)(2,1)S(1)}, u32[]{:S(2)}, u32[]{:S(2)}) collective-permute-start(f16[152,512]{1,0:T(8,128)(2,1)S(1)} %get-tuple-element.99), channel_id=1, source_target_pairs={{0,96},{16,112},{32,64},{48,80},{64,32},{80,48},{96,0},{112,16},{1... | collective-permute-start | bytes 466952 | tf_op jit(solution)/shard_map/ppermute | solution.py:682
  64.6 4.0 %copy-start.1 = (f32[2048,256]{1,0:T(8,128)S(1)}, f32[2048,256]{1,0:T(8,128)}, u32[]{:S(2)}) copy-start(f32[2048,256]{1,0:T(8,128)} %precond_ref.1) | copy-start | bytes 6291460
  64.6 6.6 %collective-permute-start.5 = (f16[152,512]{1,0:T(8,128)(2,1)S(1)}, f16[152,512]{1,0:T(8,128)(2,1)S(1)}, u32[]{:S(2)}, u32[]{:S(2)}) collective-permute-start(f16[152,512]{1,0:T(8,128)(2,1)S(1)} %get-tuple-element.93), channel_id=1, source_target_pairs={{0,96},{16,112},{32,64},{48,80},{64,32},{80,48},{96,0},{112,16},{1... | collective-permute-start | bytes 466952 | tf_op jit(solution)/shard_map/ppermute | solution.py:682
  68.2 5.5 %collective-permute-start.2 = (f16[152,512]{1,0:T(8,128)(2,1)S(1)}, f16[152,512]{1,0:T(8,128)(2,1)S(1)}, u32[]{:S(2)}, u32[]{:S(2)}) collective-permute-start(f16[152,512]{1,0:T(8,128)(2,1)S(1)} %get-tuple-element.97), channel_id=1, source_target_pairs={{0,32},{16,48},{32,0},{48,16},{64,96},{80,112},{96,64},{112,80},{1... | collective-permute-start | bytes 466952 | tf_op jit(solution)/shard_map/ppermute | solution.py:682
  74.8 1.5 collective-permute-start.6
  74.8 1.9 %collective-permute-start.7 = (bf16[144,512]{1,0:T(8,128)(2,1)S(1)}, bf16[144,512]{1,0:T(8,128)(2,1)S(1)}, u32[]{:S(2)}, u32[]{:S(2)}) collective-permute-start(bf16[144,512]{1,0:T(8,128)(2,1)S(1)} %get-tuple-element.68.second_ref), channel_id=1, source_target_pairs={{0,16},{16,0},{32,48},{48,32},{64,80},{80,64},{96,112},{112,96},{1... | collective-permute-start | bytes 442376 | tf_op jit(solution)/shard_map/ppermute | solution.py:685
  110.7 1.7 %collective-permute-start.11 = (f32[144,512]{1,0:T(8,128)S(1)}, f32[144,512]{1,0:T(8,128)S(1)}, u32[]{:S(2)}, u32[]{:S(2)}) collective-permute-start(f32[144,512]{1,0:T(8,128)S(1)} %get-tuple-element.75), channel_id=1, source_target_pairs={{0,16},{16,0},{32,48},{48,32},{64,80},{80,64},{96,112},{112,96},{1... | collective-permute-start | bytes 884744 | tf_op jit(solution)/shard_map/ppermute | solution.py:685
  110.8 2.1 %collective-permute-start.8 = (f32[152,512]{1,0:T(8,128)S(1)}, f32[152,512]{1,0:T(8,128)S(1)}, u32[]{:S(2)}, u32[]{:S(2)}) collective-permute-start(f32[152,512]{1,0:T(8,128)S(1)} %get-tuple-element.74), channel_id=1, source_target_pairs={{0,16},{16,0},{32,48},{48,32},{64,80},{80,64},{96,112},{112,96},{1... | collective-permute-start | bytes 933896 | tf_op jit(solution)/shard_map/ppermute | solution.py:685
  112.7 6.1 %collective-permute-start.12 = (f16[152,512]{1,0:T(8,128)(2,1)S(1)}, f16[152,512]{1,0:T(8,128)(2,1)S(1)}, u32[]{:S(2)}, u32[]{:S(2)}) collective-permute-start(f16[152,512]{1,0:T(8,128)(2,1)S(1)} %get-tuple-element.87), channel_id=1, source_target_pairs={{0,32},{16,48},{32,0},{48,16},{64,96},{80,112},{96,64},{112,80},{1... | collective-permute-start | bytes 466952 | tf_op jit(solution)/shard_map/ppermute | solution.py:682
  113.3 7.7 %collective-permute-start.9 = (f16[152,512]{1,0:T(8,128)(2,1)S(1)}, f16[152,512]{1,0:T(8,128)(2,1)S(1)}, u32[]{:S(2)}, u32[]{:S(2)}) collective-permute-start(f16[152,512]{1,0:T(8,128)(2,1)S(1)} %get-tuple-element.91), channel_id=1, source_target_pairs={{0,96},{16,112},{32,64},{48,80},{64,32},{80,48},{96,0},{112,16},{1... | collective-permute-start | bytes 466952 | tf_op jit(solution)/shard_map/ppermute | solution.py:682
  119.3 6.5 %collective-permute-start.13 = (f16[152,512]{1,0:T(8,128)(2,1)S(1)}, f16[152,512]{1,0:T(8,128)(2,1)S(1)}, u32[]{:S(2)}, u32[]{:S(2)}) collective-permute-start(f16[152,512]{1,0:T(8,128)(2,1)S(1)} %get-tuple-element.85), channel_id=1, source_target_pairs={{0,96},{16,112},{32,64},{48,80},{64,32},{80,48},{96,0},{112,16},{1... | collective-permute-start | bytes 466952 | tf_op jit(solution)/shard_map/ppermute | solution.py:682
  121.4 5.3 %collective-permute-start.10 = (f16[152,512]{1,0:T(8,128)(2,1)S(1)}, f16[152,512]{1,0:T(8,128)(2,1)S(1)}, u32[]{:S(2)}, u32[]{:S(2)}) collective-permute-start(f16[152,512]{1,0:T(8,128)(2,1)S(1)} %get-tuple-element.89), channel_id=1, source_target_pairs={{0,32},{16,48},{32,0},{48,16},{64,96},{80,112},{96,64},{112,80},{1... | collective-permute-start | bytes 466952 | tf_op jit(solution)/shard_map/ppermute | solution.py:682
  127.8 1.5 collective-permute-start.14
  127.9 1.9 %collective-permute-start.15 = (bf16[144,512]{1,0:T(8,128)(2,1)S(1)}, bf16[144,512]{1,0:T(8,128)(2,1)S(1)}, u32[]{:S(2)}, u32[]{:S(2)}) collective-permute-start(bf16[144,512]{1,0:T(8,128)(2,1)S(1)} %get-tuple-element.79.second_ref), channel_id=1, source_target_pairs={{0,16},{16,0},{32,48},{48,32},{64,80},{80,64},{96,112},{112,96},{1... | collective-permute-start | bytes 442376 | tf_op jit(solution)/shard_map/ppermute | solution.py:685
